TPU v7x, 256 devices: a whole 4x4x8 slice. The times are simulated.
256 devices in a mesh: dp: 8 (over z), seq: 32 (over x, y, core).
Axes of the slice: x: 4, y: 4, z: 8, core: 2. Of those that a mesh axis runs over, the one named last changes fastest.
Arguments:
- slide_tiles: bfloat16 [512, 256, 384], P(('dp', 'seq')), parts along dimension 0, may hold values from -6 to 6
- norm_gain: float32 [2, 384], replicated, may hold values from 0.1 to 1.9
- in_weight: bfloat16 [2, 384, 1536], replicated, may hold values from -0.3125 to 0.3125
- state_weight: bfloat16 [2, 384, 44], replicated, may hold values from -0.3125 to 0.3125
- conv_weight: float32 [2, 4, 800], replicated, may hold values from -2.5 to 2.5
- conv_bias: float32 [2, 800], replicated, may hold values from -0.5 to 0.5
- step_bias: float32 [2, 12], replicated, may hold values from -5 to -3
- decay_log: float32 [2, 12], replicated, may hold values from -8.5 to 1
- skip_gain: float32 [2, 12], replicated, may hold values from 0.5 to 1.5
- out_gain: float32 [2, 768], replicated, may hold values from 0.1 to 1.9
- out_weight: bfloat16 [2, 768, 384], replicated, may hold values from -0.21875 to 0.21875
Outputs:
- tile_out: bfloat16 [512, 256, 384], P(('dp', 'seq')), parts along dimension 0
There are 8 independent parts, one for each index of `dp`. A program takes and returns all parts, laid end to end along the dimension named above; an argument that names none is the same for every part. Nothing has to cross between parts.
All inputs are finite; a program needn't handle non-finite values.
Results may differ from a plain program's by a relative error of at most 0.014.
Values may be sent and summed in bfloat16 or wider, within the bound.
No kernel may reach another device: no remote copies, remote signals or barrier semaphores. Data moves between devices by JAX's collectives and lax.ppermute only.
A program may use at most 64 MiB of HBM per device.

v0:
```python
import jax
import jax.numpy as jnp
from jax import lax
from jax.sharding import PartitionSpec as P

HEADS = 12
HEADDIM = 64
STATE = 16
GROUP = 256


epsilon = 1e-05


def entering_2(x, axis, join, neutral):
    place = lax.axis_index(axis)
    gathered = jax.tree.map(
        lambda a, kind: lax.all_gather(a.astype(kind), axis), x, (jnp.bfloat16, jnp.bfloat16)
    )
    state = jax.tree.map(lambda a, e: jnp.zeros_like(a) + jnp.asarray(e, a.dtype), x, neutral)

    def one(step, state):
        return join(
            state,
            jax.tree.map(
                lambda a, own: lax.dynamic_index_in_dim(a, step, 0, False).astype(own.dtype),
                gathered,
                x,
            ),
        )

    return lax.fori_loop(0, place, one, state)


def passed_along(value, axis, steps):
    count = lax.axis_size(axis)
    first, last = (max(0, -steps), min(count, count - steps))
    return lax.ppermute(value, axis, [(source, source + steps) for source in range(first, last)])


def rms_scaled(values, scale_gain):
    values = values.astype(jnp.float32)
    return (
        values * lax.rsqrt(jnp.mean(values * values, axis=-1, keepdims=True) + epsilon) * scale_gain
    )


def group_terms(group_in):
    group_x, group_b, group_c, group_step, group_rate = group_in
    cumulative = jnp.cumsum(group_rate, axis=0)
    positions = jnp.arange(group_x.shape[0])
    lower_mask = positions[:, None] >= positions[None, :]
    cum_heads = cumulative.T
    differences = cum_heads[:, :, None] - cum_heads[:, None, :]
    decay_mask = jnp.exp(jnp.where(lower_mask[None], differences, -jnp.inf))
    scores = jnp.dot(group_c, group_b.T, preferred_element_type=jnp.float32)
    weights = (scores[None] * decay_mask * group_step.T[:, None, :]).astype(jnp.bfloat16)
    intra_out = jnp.einsum("hts,shp->thp", weights, group_x, preferred_element_type=jnp.float32)
    tail_weight = jnp.exp(cumulative[-1][None, :] - cumulative) * group_step
    weighted_x = (group_x.astype(jnp.float32) * tail_weight[:, :, None]).astype(jnp.bfloat16)
    local_state = jnp.einsum("shp,sn->hpn", weighted_x, group_b, preferred_element_type=jnp.float32)
    return (intra_out, local_state, cumulative)


def link_states(earlier, latter):
    return (earlier[0] + latter[0], jnp.exp(latter[0])[:, None, None] * earlier[1] + latter[1])


def incoming_state(whole_decay, final_state):
    identity = (jnp.zeros_like(whole_decay), jnp.zeros_like(final_state))
    passed = entering_2((whole_decay, final_state), "seq", link_states, identity)
    return passed[1]


def advance(carry_state, group_item):
    group_total, local_state = group_item
    return (jnp.exp(group_total)[:, None, None] * carry_state + local_state, carry_state)


def mixer(
    sequence,
    layer,
    norm_gain,
    in_weight,
    state_weight,
    conv_weight,
    conv_bias,
    step_bias,
    decay_log,
    skip_gain,
    out_gain,
):
    length = sequence.shape[0]
    inner_width = in_weight.shape[2] // 2
    normed = rms_scaled(sequence, norm_gain[layer]).astype(jnp.bfloat16)
    gate_x = jnp.dot(normed, in_weight[layer], preferred_element_type=jnp.float32).astype(
        jnp.bfloat16
    )
    state_proj = jnp.dot(normed, state_weight[layer], preferred_element_type=jnp.float32).astype(
        jnp.bfloat16
    )
    x_part = gate_x[:, inner_width:]
    bc_part = state_proj[:, : 2 * STATE]
    margin = conv_weight.shape[1] - 1
    edge_rows = passed_along((x_part[length - margin :], bc_part[length - margin :]), "seq", 1)
    x_padded = jnp.concatenate([edge_rows[0], x_part], axis=0)
    bc_padded = jnp.concatenate([edge_rows[1], bc_part], axis=0)
    taps = conv_weight[layer]
    conv_x = jnp.zeros((length, inner_width), jnp.float32) + conv_bias[layer][None, :inner_width]
    conv_bc = jnp.zeros((length, 2 * STATE), jnp.float32) + conv_bias[layer][None, inner_width:]
    for offset in range(margin + 1):
        conv_x = conv_x + taps[offset][None, :inner_width] * x_padded[
            offset : offset + length
        ].astype(jnp.float32)
        conv_bc = conv_bc + taps[offset][None, inner_width:] * bc_padded[
            offset : offset + length
        ].astype(jnp.float32)
    x_conv = jax.nn.silu(conv_x).astype(jnp.bfloat16)
    bc_conv = jax.nn.silu(conv_bc).astype(jnp.bfloat16)
    step_size = jax.nn.softplus(
        state_proj[:, 2 * STATE :].astype(jnp.float32) + step_bias[layer][None, :]
    )
    log_rates = -step_size * jnp.exp(decay_log[layer])[None, :]
    group_count = length // GROUP
    group_x = x_conv.reshape(group_count, GROUP, HEADS, HEADDIM)
    group_c = bc_conv[:, STATE:].reshape(group_count, GROUP, STATE)
    inputs = (
        group_x,
        bc_conv[:, :STATE].reshape(group_count, GROUP, STATE),
        group_c,
        step_size.reshape(group_count, GROUP, HEADS),
        log_rates.reshape(group_count, GROUP, HEADS),
    )
    intra_out, local_states, cumulative = lax.map(group_terms, inputs)
    totals = cumulative[:, -1, :]
    final_state, entering = lax.scan(
        advance, jnp.zeros((HEADS, HEADDIM, STATE), jnp.float32), (totals, local_states)
    )
    arriving = incoming_state(jnp.sum(totals, axis=0), final_state)
    before = jnp.cumsum(totals, axis=0) - totals
    start_states = entering + jnp.exp(before)[:, :, None, None] * arriving[None]
    inter_out = jnp.exp(cumulative)[..., None] * jnp.einsum(
        "ctn,chpn->cthp", group_c.astype(jnp.float32), start_states, precision=lax.Precision.HIGHEST
    )
    y_total = (
        intra_out + inter_out + skip_gain[layer][None, None, :, None] * group_x.astype(jnp.float32)
    )
    gated = y_total.reshape(length, inner_width) * jax.nn.silu(
        gate_x[:, :inner_width].astype(jnp.float32)
    )
    return rms_scaled(gated, out_gain[layer]).astype(jnp.bfloat16)


def on_device(
    slide_tiles,
    norm_gain,
    in_weight,
    state_weight,
    conv_weight,
    conv_bias,
    step_bias,
    decay_log,
    skip_gain,
    out_gain,
    out_weight,
):
    row_count, col_count, feature_count = slide_tiles.shape
    params = (
        norm_gain,
        in_weight,
        state_weight,
        conv_weight,
        conv_bias,
        step_bias,
        decay_log,
        skip_gain,
        out_gain,
    )
    flipped = slide_tiles[:, ::-1, :]
    columns = lax.all_to_all(flipped, "seq", split_axis=1, concat_axis=0, tiled=True)
    full_rows, block_cols = (columns.shape[0], columns.shape[1])
    first_order = jnp.transpose(columns[::-1], (1, 0, 2)).reshape(
        full_rows * block_cols, feature_count
    )
    mixed_out = mixer(first_order, 0, *params)
    layer_out = (
        first_order.astype(jnp.float32)
        + jnp.dot(mixed_out, out_weight[0], preferred_element_type=jnp.float32)
    ).astype(jnp.bfloat16)
    row_grid = jnp.transpose(layer_out.reshape(block_cols, full_rows, feature_count), (1, 0, 2))[
        ::-1
    ]
    returned = lax.all_to_all(row_grid, "seq", split_axis=0, concat_axis=1, tiled=True)
    second = returned[:, ::-1, :].reshape(row_count * col_count, feature_count)
    mixed_out = mixer(second, 1, *params)
    result = (
        second.astype(jnp.float32)
        + jnp.dot(mixed_out, out_weight[1], preferred_element_type=jnp.float32)
    ).astype(jnp.bfloat16)
    return result.reshape(row_count, col_count, feature_count)


def solution(mesh):
    placed = (P(("dp", "seq"), None, None), P(), P(), P(), P(), P(), P(), P(), P(), P(), P())
    return jax.shard_map(
        on_device,
        mesh=mesh,
        in_specs=placed,
        out_specs=P(("dp", "seq"), None, None),
        check_vma=False,
    )
```

profile of v0, /device:TPU:127, one launch (start us, length us, event | category | flops | bytes accessed | tf_op | source)
XLA Modules:
  0.0 336.7 jit_solution(9005171873712246071)
XLA Ops:
  0.1 1.5 copy.98
  2.5 7.6 %all-to-all-start = ((bf16[2,256,384]{2,0,1:T(2,128)(2,1)}), bf16[2,256,384]{2,0,1:T(2,128)(2,1)S(1)}, u32[]{:S(2)}, u32[]{:S(2)}) async-start(bf16[2,256,384]{2,0,1:T(2,128)(2,1)} %rev.12), calls=%async_computation | async-start | bytes 786432 | tf_op jit(solution)/shard_map/all_to_all | solution.py:180
  18.7 2.2 convolution_convert_fusion.1
  22.3 1.3 collective-permute-start.1
  23.6 1.3 collective-permute-start
  29.8 7.9 %while.78 = (s32[]{:T(128)}, f32[2,256,12,64]{1,3,2,0:T(8,128)S(1)}, f32[2,12,64,16]{2,3,1,0:T(8,128)S(1)}, f32[2,256,12]{1,2,0:T(8,128)}, bf16[2,256,12,64]{1,3...) while((s32[]{:T(128)}, ...), condition=%wide.region_4.5_spmd, body=%wide.region_1.4_spmd.sunk | while | flops 114038824 | bytes 2966549 | solution.py:134
  39.9 30.6 %all-gather.1 = bf16[384,64,16]{1,2,0:T(8,128)(2,1)} all-gather(bf16[12,64,16]{1,2,0:T(8,128)(2,1)S(1)} %convert_element_type.257), channel_id=3, replica_groups=mesh['dp'=8,'seq'=32] {'seq'}, dimensions={0}, use_global_device_ids=true | all-gather | bytes 811008 | tf_op jit(solution)/shard_map/all_gather | solution.py:18
  70.8 62.2 %all-reduce = bf16[384]{0:T(512)(128)(2,1)S(1)} all-reduce(bf16[384]{0:T(512)(128)(2,1)S(1)} %dynamic-update-slice), channel_id=2, replica_groups=mesh['dp'=8,'seq'=32] {'seq'}, use_global_device_ids=true, to_apply=%add | all-reduce | flops 384 | bytes 1536
  133.1 29.3 %while.79 = (s32[]{:T(128)}, f32[12,64,16]{1,2,0:T(8,128)S(1)}, s32[]{:T(128)}, bf16[32,12]{1,0:T(8,128)(2,1)S(1)}, bf16[32,12,64,16]{2,3,1,0:T(8,128)(2,1)}, /*index=5*/s32[]{:T(128)}, s32[]{:T(128)}, s32[]{:T(128)}) while((s32[]{:T(128)}, f32[12,64,16]{1,2,0:T(8,128)S(1)}, s32[]{:T(128)}, bf16[32,12]{1,0:T(8,128)(2,1)S(1)}, ...), condition=%wide.region_10.11_spmd, body=%wide.region_9.10_spmd.sunk | while | flops 36881 | bytes 123127 | solution.py:32
  162.4 1.3 multiply_add_fusion.1
  165.6 1.9 multiply_reduce_fusion.1
  167.5 1.9 fusion.68
  170.4 6.7 %all-to-all-start.1 = ((bf16[64,8,384]{2,1,0:T(8,128)(2,1)}), bf16[64,8,384]{2,1,0:T(8,128)(2,1)S(1)}, u32[]{:S(2)}, u32[]{:S(2)}) async-start(bf16[64,8,384]{2,1,0:T(8,128)(2,1)} %rev.14), calls=%async_computation.1 | async-start | bytes 786432 | tf_op jit(solution)/shard_map/all_to_all | solution.py:193
  177.1 7.1 %all-to-all-done.1 = bf16[64,8,384]{2,1,0:T(8,128)(2,1)S(1)} async-done(((bf16[64,8,384]{2,1,0:T(8,128)(2,1)}), bf16[64,8,384]{2,1,0:T(8,128)(2,1)S(1)}, u32[]{:S(2)}, u32[]{:S(2)}) %all-to-all-start.1) | async-done | bytes 393248 | tf_op jit(solution)/shard_map/all_to_all | solution.py:193
  185.5 2.3 convolution_convert_fusion
  188.9 1.3 collective-permute-start.3
  190.2 1.3 collective-permute-start.2
  196.4 7.9 %while.80 = (s32[]{:T(128)}, f32[2,256,12,64]{1,3,2,0:T(8,128)S(1)}, f32[2,12,64,16]{2,3,1,0:T(8,128)S(1)}, f32[2,256,12]{1,2,0:T(8,128)}, bf16[2,256,12,64]{1,3...) while((s32[]{:T(128)}, ...), condition=%wide.region_16.17_spmd, body=%wide.region_13.16_spmd.sunk | while | flops 114038824 | bytes 2966549 | solution.py:134
  206.5 30.6 %all-gather.3 = bf16[384,64,16]{1,2,0:T(8,128)(2,1)} all-gather(bf16[12,64,16]{1,2,0:T(8,128)(2,1)S(1)} %convert_element_type.282), channel_id=5, replica_groups=mesh['dp'=8,'seq'=32] {'seq'}, dimensions={0}, use_global_device_ids=true | all-gather | bytes 811008 | tf_op jit(solution)/shard_map/all_gather | solution.py:18
  237.4 62.4 %all-reduce.1 = bf16[384]{0:T(512)(128)(2,1)S(1)} all-reduce(bf16[384]{0:T(512)(128)(2,1)S(1)} %dynamic-update-slice.1), channel_id=4, replica_groups=mesh['dp'=8,'seq'=32] {'seq'}, use_global_device_ids=true, to_apply=%add.1 | all-reduce | flops 384 | bytes 1536
  299.9 29.1 %while.81 = (s32[]{:T(128)}, f32[12,64,16]{1,2,0:T(8,128)S(1)}, s32[]{:T(128)}, bf16[32,12]{1,0:T(8,128)(2,1)S(1)}, bf16[32,12,64,16]{2,3,1,0:T(8,128)(2,1)}, /*index=5*/s32[]{:T(128)}, s32[]{:T(128)}, s32[]{:T(128)}) while((s32[]{:T(128)}, f32[12,64,16]{1,2,0:T(8,128)S(1)}, s32[]{:T(128)}, bf16[32,12]{1,0:T(8,128)(2,1)S(1)}, ...), condition=%wide.region_22.23_spmd, body=%wide.region_21.22_spmd.sunk | while | flops 36881 | bytes 123127 | solution.py:32
  329.0 1.3 multiply_add_fusion
  332.2 1.8 multiply_reduce_fusion
  334.1 2.6 fusion.69
  (405 shorter events, 103.5 us)
Async XLA Ops:
  0.0 14.3 %copy-start.39 = (u32[256]{0:T(256)S(1)}, u32[256]{0:T(256)}, u32[]{:S(2)}) copy-start(u32[256]{0:T(256)} %constant.128) | copy-start | bytes 3076
  0.0 10.2 %copy-start.22 = (f32[2,800]{1,0:T(2,128)S(1)}, f32[2,800]{1,0:T(2,128)}, u32[]{:S(2)}) copy-start(f32[2,800]{1,0:T(2,128)} %param.28) | copy-start | bytes 19204
  0.0 11.3 %copy-start.15 = (f32[2,4,800]{2,1,0:T(4,128)S(1)}, f32[2,4,800]{2,1,0:T(4,128)}, u32[]{:S(2)}) copy-start(f32[2,4,800]{2,1,0:T(4,128)} %param.27) | copy-start | bytes 76804
  0.0 11.9 %copy-start.36 = (f32[2,12]{1,0:T(2,128)S(1)}, f32[2,12]{1,0:T(2,128)}, u32[]{:S(2)}) copy-start(f32[2,12]{1,0:T(2,128)} %param.31) | copy-start | bytes 292
  0.0 12.5 %copy-start.23 = (f32[2,768]{1,0:T(2,128)S(1)}, f32[2,768]{1,0:T(2,128)}, u32[]{:S(2)}) copy-start(f32[2,768]{1,0:T(2,128)} %param.32) | copy-start | bytes 18436
  0.0 13.1 %copy-start.38 = (f32[2,12]{1,0:T(2,128)S(1)}, f32[2,12]{1,0:T(2,128)}, u32[]{:S(2)}) copy-start(f32[2,12]{1,0:T(2,128)} %param.29) | copy-start | bytes 292
  0.0 13.1 %copy-start.37 = (f32[2,12]{1,0:T(2,128)S(1)}, f32[2,12]{1,0:T(2,128)}, u32[]{:S(2)}) copy-start(f32[2,12]{1,0:T(2,128)} %param.30) | copy-start | bytes 292
  0.0 13.6 %copy-start.26 = (f32[2,384]{1,0:T(2,128)S(1)}, f32[2,384]{1,0:T(2,128)}, u32[]{:S(2)}) copy-start(f32[2,384]{1,0:T(2,128)} %param.24) | copy-start | bytes 9220
  0.1 16.1 %copy-start.11 = (bf16[2,384,44]{1,0,2:T(2,128)(2,1)S(1)}, bf16[2,384,44]{1,0,2:T(2,128)(2,1)}, u32[]{:S(2)}) copy-start(bf16[2,384,44]{1,0,2:T(2,128)(2,1)} %param.26) | copy-start | bytes 202756
  2.5 14.8 %all-to-all-start = ((bf16[2,256,384]{2,0,1:T(2,128)(2,1)}), bf16[2,256,384]{2,0,1:T(2,128)(2,1)S(1)}, u32[]{:S(2)}, u32[]{:S(2)}) async-start(bf16[2,256,384]{2,0,1:T(2,128)(2,1)} %rev.12), calls=%async_computation | async-start | bytes 786432 | tf_op jit(solution)/shard_map/all_to_all | solution.py:180
  22.3 3.1 collective-permute-start.1
  23.6 3.7 %collective-permute-start = (bf16[3,768]{1,0:T(4,128)(2,1)S(1)}, bf16[3,768]{1,0:T(4,128)(2,1)S(1)}, u32[]{:S(2)}, u32[]{:S(2)}) collective-permute-start(bf16[3,768]{1,0:T(4,128)(2,1)S(1)} %slice.368), channel_id=1, source_target_pairs={{0,1},{1,2},{2,3},{3,4},{4,5},{5,6},{6,7},{7,8},{8,9},{9,10},{10,1... | collective-permute-start | bytes 13832 | tf_op jit(solution)/shard_map/ppermute | solution.py:38
  39.9 122.5 %copy-start.14 = (bf16[2,256,16]{1,0,2:T(2,128)(2,1)S(1)}, bf16[2,256,16]{1,0,2:T(2,128)(2,1)}, u32[]{:S(2)}) copy-start(bf16[2,256,16]{1,0,2:T(2,128)(2,1)} %reshape.377) | copy-start | bytes 49156
  39.9 122.5 %copy-start.33 = (f32[12]{0:T(128)S(1)}, f32[12]{0:T(128)}, u32[]{:S(2)}) copy-start(f32[12]{0:T(128)} %get-tuple-element.486) | copy-start | bytes 148
  170.4 14.6 %copy-start.21 = (f32[384]{0:T(512)S(1)}, f32[384]{0:T(512)}, u32[]{:S(2)}) copy-start(f32[384]{0:T(512)} %get-tuple-element.383) | copy-start | bytes 4612
  170.4 13.9 %all-to-all-start.1 = ((bf16[64,8,384]{2,1,0:T(8,128)(2,1)}), bf16[64,8,384]{2,1,0:T(8,128)(2,1)S(1)}, u32[]{:S(2)}, u32[]{:S(2)}) async-start(bf16[64,8,384]{2,1,0:T(8,128)(2,1)} %rev.14), calls=%async_computation.1 | async-start | bytes 786432 | tf_op jit(solution)/shard_map/all_to_all | solution.py:193
  177.1 8.0 %copy-start.12 = (bf16[1,384,44]{1,0,2:T(2,128)(2,1)S(1)}, bf16[1,384,44]{1,0,2:T(2,128)(2,1)}, u32[]{:S(2)}) copy-start(bf16[1,384,44]{1,0,2:T(2,128)(2,1)} %get-tuple-element.465) | copy-start | bytes 101380
  187.9 6.1 %copy-start.16 = (f32[768]{0:T(1024)S(1)}, f32[768]{0:T(1024)}, u32[]{:S(2)}) copy-start(f32[768]{0:T(1024)} %get-tuple-element.371) | copy-start | bytes 9220
  187.9 6.1 %copy-start.17 = (f32[768]{0:T(1024)S(1)}, f32[768]{0:T(1024)}, u32[]{:S(2)}) copy-start(f32[768]{0:T(1024)} %get-tuple-element.372) | copy-start | bytes 9220
  187.9 6.0 %copy-start.18 = (f32[768]{0:T(1024)S(1)}, f32[768]{0:T(1024)}, u32[]{:S(2)}) copy-start(f32[768]{0:T(1024)} %get-tuple-element.373) | copy-start | bytes 9220
  188.9 3.1 collective-permute-start.3
  190.2 3.7 %collective-permute-start.2 = (bf16[3,768]{1,0:T(4,128)(2,1)S(1)}, bf16[3,768]{1,0:T(4,128)(2,1)S(1)}, u32[]{:S(2)}, u32[]{:S(2)}) collective-permute-start(bf16[3,768]{1,0:T(4,128)(2,1)S(1)} %slice.384), channel_id=1, source_target_pairs={{0,1},{1,2},{2,3},{3,4},{4,5},{5,6},{6,7},{7,8},{8,9},{9,10},{10,1... | collective-permute-start | bytes 13832 | tf_op jit(solution)/shard_map/ppermute | solution.py:38
  206.5 122.6 %copy-start.13 = (bf16[2,256,16]{1,0,2:T(2,128)(2,1)S(1)}, bf16[2,256,16]{1,0,2:T(2,128)(2,1)}, u32[]{:S(2)}) copy-start(bf16[2,256,16]{1,0,2:T(2,128)(2,1)} %reshape.384) | copy-start | bytes 49156
  206.5 122.6 %copy-start.31 = (f32[12]{0:T(128)S(1)}, f32[12]{0:T(128)}, u32[]{:S(2)}) copy-start(f32[12]{0:T(128)} %get-tuple-element.485) | copy-start | bytes 148
  (26 other events, 68.3 us)
where the time goes:
time: 341 us; the launch traced here: 337 us
  blocking collectives  186 us (55%)
  other arithmetic  69.6 us (20%)
  local copies, waits for them, and re-layouts  28.8 us (8%)
  starting transfers between devices  19.5 us (6%)
  matrix products  17.9 us (5%)
  waiting for transfers between devices  10.4 us (3%)
    unnamed x2, blocking collectives  125 us
    all_gather x2, blocking collectives, entering_2(): lax.all_gather(a.astype(kind), axis)  61.3 us
    add x62, other arithmetic, link_states(): jnp.exp(latter[0])[:, None, None] * earlier[1] + latter[1]  55 us
    all_to_all x1, starting transfers between devices, on_device(): lax.all_to_all(flipped, 'seq', split_axis=1, concat_axis=0, tiled=True)  7.63 us
    all_to_all x1, waiting for transfers between devices, on_device(): lax.all_to_all(row_grid, 'seq', split_axis=0, concat_axis=1, tiled=True)  7.11 us
  transfers between devices with their start and end apart: 6, of which 6 were waited for; matrix products, arithmetic and copies ran while one was open for 2% of the time, Pallas kernels for 0%

commit v1 on v0

v1 whole, which is shorter than its diff:
```python
import functools

import jax
import jax.numpy as jnp
from jax import lax
from jax.experimental import pallas as pl
from jax.experimental.pallas import tpu as pltpu
from jax.sharding import PartitionSpec as P

D = 384
INNER = 768
HEADS = 12
HEADDIM = 64
STATE = 16
GROUP = 256
TOKENS = 512
PEERS = 32
CHUNK = 24
STATE_ROWS = 104
EPS = 1e-05
BF = jnp.bfloat16
F32 = jnp.float32
EXACT = lax.Precision.HIGHEST


def iota(shape, dim):
    return lax.broadcasted_iota(jnp.int32, shape, dim)


def dot(a, b, precision=None):
    return lax.dot_general(
        a, b, (((1,), (0,)), ((), ())), precision=precision, preferred_element_type=F32
    )


def dot_rows(a, b):
    return lax.dot_general(a, b, (((1,), (1,)), ((), ())), preferred_element_type=F32)


def one_hot(shape, column):
    return jnp.where(iota(shape, 1) == column, 1.0, 0.0).astype(BF)


def silu(v):
    half = 0.5 * v
    return half + half * jnp.tanh(half)


def rms(values, gain):
    return values * lax.rsqrt(jnp.mean(values * values, axis=-1, keepdims=True) + EPS) * gain


def in_two(values):
    high = values.astype(BF)
    return high, (values - high.astype(F32)).astype(BF)


def spread(values, width):
    lanes = HEADS * width
    shift = width.bit_length() - 1
    mask = lax.shift_right_logical(iota((16, lanes), 1), shift) == iota((16, lanes), 0)
    return dot(values, jnp.where(mask, 1.0, 0.0), EXACT)


def pack_body(tiles_ref, send_ref):
    rows = [tiles_ref[r].astype(F32).reshape(PEERS, 8, D) for r in range(2)]
    after = [jnp.concatenate([r[1:], jnp.zeros((1, 8, D), F32)], axis=0) for r in rows]
    place = iota((PEERS, 8, D), 1)
    second = jnp.concatenate([after[1][:, :1], after[1][:, :1]], axis=1)
    halo = jnp.where(
        place == 0,
        after[0],
        jnp.where(place == 1, jnp.broadcast_to(second[:, :1], (PEERS, 8, D)), 0.0),
    )
    send_ref[...] = jnp.concatenate([rows[0], rows[1], halo], axis=1).astype(BF)


def front_body(
    layer,
    recv_ref,
    gain_ref,
    wx_ref,
    ws_ref,
    cw_ref,
    cb_ref,
    col_ref,
    xs_ref,
    nm_ref,
    xc_ref,
    bt_ref,
    cc_ref,
    cum_ref,
    rt_ref,
    loc_ref,
    dec_ref,
    send_ref,
    conv_ref,
):
    main = recv_ref[:, 0:16, :].reshape(TOKENS, D)
    t = iota((TOKENS, 1), 0)
    if layer == 0:
        column = 511 - 8 * jnp.bitwise_and(t, 63) - lax.shift_right_logical(t, 6)
        halo_in = jnp.concatenate(
            [recv_ref[0, 16:24, :].astype(F32), recv_ref[1, 16:24, :].astype(F32)], axis=0
        )
        place = iota((16, 1), 0)
        picked = jnp.where(
            place == 13, 8, jnp.where(place == 14, 1, jnp.where(place == 15, 0, -1))
        )
    else:
        low = jnp.bitwise_and(t, 7)
        column = (
            2 * (jnp.bitwise_and(t, 255) - low) + 8 * lax.shift_right_logical(t, 8) + low
        )
        halo_in = jnp.concatenate(
            [recv_ref[PEERS - 1, 16:24, :].astype(F32), jnp.zeros((8, D), F32)], axis=0
        )
        place = iota((16, 1), 0)
        picked = jnp.where(place >= 13, place - 13, -1)
    xs = dot(one_hot((TOKENS, TOKENS), column), main)
    halo = dot(one_hot((16, 16), picked), halo_in.astype(BF))
    xs_ref[...] = xs.astype(BF)
    gain = gain_ref[layer : layer + 1, :]
    normed = rms(xs, gain).astype(BF)
    halo_normed = rms(halo, gain).astype(BF)
    nm_ref[...] = normed
    wx = wx_ref[0]
    conv_ref[8 : 8 + TOKENS, :] = dot(normed, wx).astype(BF).astype(F32)
    conv_ref[0:8, :] = dot(halo_normed, wx).astype(BF).astype(F32)[8:16]
    for block in range(INNER // 128):
        lanes = slice(128 * block, 128 * block + 128)
        total = cb_ref[layer : layer + 1, lanes] + cw_ref[layer, 0:1, lanes] * conv_ref[
            5 : 5 + TOKENS, lanes
        ]
        for tap in range(1, 4):
            total = total + cw_ref[layer, tap : tap + 1, lanes] * conv_ref[
                5 + tap : 5 + tap + TOKENS, lanes
            ]
        xc_ref[:, lanes] = silu(total).astype(BF)

    tall = jnp.concatenate([normed, jnp.zeros((112, D), BF), halo_normed], axis=0)
    proj = dot_rows(ws_ref[layer], tall).astype(BF).astype(F32)
    col = col_ref[layer]
    bc_in = proj[0:32, :]
    bc = col[0:32, 4:5] + col[0:32, 3:4] * bc_in
    for back in range(1, 4):
        bc = bc + col[0:32, 3 - back : 4 - back] * pltpu.roll(bc_in, back, 1)
    bc = silu(bc[:, 0:TOKENS])
    bt = bc[0:16]
    bt_ref[...] = bt.astype(BF)
    cc_ref[...] = bc.T[:, 16:32].astype(BF)

    raw = proj[32:48, 0:TOKENS] + col[32:48, 5:6]
    step = jnp.maximum(raw, 0.0) + jnp.log1p(jnp.exp(-jnp.abs(raw)))
    rate = -step * jnp.exp(col[32:48, 6:7])
    upper = jnp.where(iota((GROUP, GROUP), 0) <= iota((GROUP, GROUP), 1), 1.0, 0.0)
    cums = [dot(rate[:, g * GROUP : (g + 1) * GROUP], upper, EXACT) for g in range(2)]
    cum_rows = jnp.concatenate(cums, axis=1)
    rt = cum_rows - jnp.log(step)
    rt_ref[...] = rt
    cum = cum_rows.T
    cum_ref[...] = cum
    totals = jnp.concatenate([cum[255:256], cum[511:512], jnp.zeros((6, 16), F32)], axis=0)
    decays = spread(jnp.exp(totals), HEADDIM)
    dec_ref[...] = decays
    bt_held = bt.astype(BF).astype(F32)
    head = lax.shift_right_logical(iota((16, INNER), 1), 6)
    locals_ = []
    for g in range(2):
        span = slice(g * GROUP, (g + 1) * GROUP)
        tail = jnp.exp(cums[g][:, GROUP - 1 : GROUP] - rt[:, span])
        tilted = jnp.concatenate(
            [bt_held[:, span] * tail[h : h + 1, :] for h in range(HEADS)], axis=0
        ).astype(BF)
        every = dot(tilted, xc_ref[span, :])
        local = every[0:16]
        for h in range(1, HEADS):
            local = jnp.where(head == h, every[16 * h : 16 * h + 16], local)
        locals_.append(local)
    loc_ref[...] = locals_[0]
    final = (decays[1:2] * locals_[0] + locals_[1]).astype(BF)
    total = totals[0:1] + totals[1:2]
    high, low = in_two(total)
    pad = jnp.zeros((1, 112), F32)
    decay_rows = jnp.concatenate(
        [
            jnp.concatenate([high.astype(F32), pad], axis=1),
            jnp.concatenate([low.astype(F32), pad], axis=1),
            jnp.zeros((6, 128), F32),
        ],
        axis=0,
    )
    packed = jnp.concatenate(
        [final[:, 128 * b : 128 * b + 128].astype(F32) for b in range(6)] + [decay_rows], axis=0
    ).astype(BF)
    for peer in range(PEERS):
        send_ref[peer] = packed


def middle_body(
    layer, nm_ref, wz_ref, xc_ref, bt_ref, cc_ref, cum_ref, rt_ref, skip_ref, z_ref, y_ref, ct_ref
):
    z_ref[...] = dot(nm_ref[...], wz_ref[0]).astype(BF)
    held = cc_ref[...]
    mask = jnp.bitwise_and(iota((16, 192), 1), 15) == iota((16, 192), 0)
    repeated = dot(held, jnp.where(mask, 1.0, 0.0).astype(BF))
    ct_ref[...] = (repeated * spread(jnp.exp(cum_ref[...]), STATE)).astype(BF)
    skip = spread(jnp.broadcast_to(skip_ref[layer : layer + 1, :], (8, 16)), HEADDIM)
    half = GROUP // 2
    lower = iota((half, half), 0) >= iota((half, half), 1)
    left = iota((1, 128), 1) < HEADDIM
    for g in range(2):
        base = g * GROUP
        scores = dot(held[base : base + GROUP], bt_ref[:, base : base + GROUP])
        s00 = jnp.where(lower, scores[:half, :half], 0.0)
        s10 = scores[half:, :half]
        s11 = jnp.where(lower, scores[half:, half:], 0.0)
        for pair in range(HEADS // 2):
            lanes = slice(128 * pair, 128 * pair + 128)
            x = xc_ref[base : base + GROUP, lanes].astype(F32)
            top, low, inputs0, inputs1 = [], [], [], []
            for which in range(2):
                h = 2 * pair + which
                c0 = cum_ref[base : base + half, h : h + 1]
                c1 = cum_ref[base + half : base + GROUP, h : h + 1]
                r0 = rt_ref[h : h + 1, base : base + half]
                r1 = rt_ref[h : h + 1, base + half : base + GROUP]
                top.append((s00 * jnp.exp(jnp.minimum(c0 - r0, 80.0))).astype(BF))
                low.append((s10 * jnp.exp(c1 - r0)).astype(BF))
                low.append((s11 * jnp.exp(jnp.minimum(c1 - r1, 80.0))).astype(BF))
                own = jnp.where(left if which == 0 else ~left, x, 0.0).astype(BF)
                inputs0.append(own[:half])
                inputs1.append(own)
            y0 = dot(jnp.concatenate(top, axis=1), jnp.concatenate(inputs0, axis=0))
            y1 = dot(jnp.concatenate(low, axis=1), jnp.concatenate(inputs1, axis=0))
            weight = skip[0:1, lanes]
            y_ref[base : base + half, lanes] = y0 + weight * x[:half]
            y_ref[base + half : base + GROUP, lanes] = y1 + weight * x[half:]


def finish_body(
    layer,
    place_ref,
    recv_ref,
    loc_ref,
    dec_ref,
    z_ref,
    y_ref,
    ct_ref,
    xs_ref,
    gain_ref,
    wo_ref,
    out_ref,
):
    place = place_ref[0]
    decays = jnp.sum(recv_ref[:, 96:104, :].astype(F32), axis=1)
    source, between = iota((PEERS, PEERS), 0), iota((PEERS, PEERS), 1)
    if layer == 0:
        link = (between > place) & (between < source)
        valid = iota((PEERS, 128), 0) > place
    else:
        link = (between < place) & (between > source)
        valid = iota((PEERS, 128), 0) < place
    passed = dot(jnp.where(link, 1.0, 0.0), decays, EXACT)
    factor = jnp.where(valid, jnp.exp(passed), 0.0)
    mask = lax.shift_right_logical(iota((128, INNER), 1), 6) == iota((128, INNER), 0)
    factors = dot(factor, jnp.where(mask, 1.0, 0.0), EXACT)
    blocks = []
    for b in range(6):
        lanes = slice(128 * b, 128 * b + 128)
        total = jnp.zeros((16, 128), F32)
        for peer in range(PEERS):
            total = total + factors[peer : peer + 1, lanes] * recv_ref[
                peer, 16 * b : 16 * b + 16, :
            ].astype(F32)
        blocks.append(total)
    start = jnp.concatenate(blocks, axis=1)
    starts = [start, dec_ref[0:1, :] * start + loc_ref[...]]
    own = lax.shift_right_logical(iota((192, INNER), 1), 6) == lax.shift_right_logical(
        iota((192, INNER), 0), 4
    )
    mixed = []
    for g in range(2):
        span = slice(g * GROUP, (g + 1) * GROUP)
        wide = jnp.where(own, jnp.concatenate([starts[g]] * HEADS, axis=0), 0.0).astype(BF)
        y = y_ref[span, :] + dot(ct_ref[span, :], wide)
        gated = y * silu(z_ref[span, :].astype(F32))
        mixed.append(rms(gated, gain_ref[layer : layer + 1, :]).astype(BF))
    result = (
        xs_ref[...].astype(F32) + dot(jnp.concatenate(mixed, axis=0), wo_ref[0])
    ).astype(BF)
    if layer == 1:
        out_ref[...] = result
        return
    row = iota((PEERS * CHUNK, 1), 0)
    peer = lax.shift_right_logical(row * 2731, 16)
    slot = row - CHUNK * peer
    token = (7 - jnp.bitwise_and(slot, 7)) * 64 + 63 - 2 * peer - lax.shift_right_logical(slot, 3)
    edge = (18 - slot) * 64 + 64 - 2 * peer
    token = jnp.where(slot < 16, token, jnp.where((slot < 19) & (peer > 0), edge, -1))
    out_ref[...] = (
        dot(one_hot((PEERS * CHUNK, TOKENS), token), result)
        .reshape(PEERS, CHUNK, D)
        .astype(BF)
    )


def layer_half(which, axis_size):
    return pl.BlockSpec((1, D, INNER), lambda *_: (which[0], 0, which[1]))


def shaped(shape, dtype):
    return jax.ShapeDtypeStruct(shape, dtype)


def whole(a):
    return pl.BlockSpec(a.shape, lambda *_: (0,) * len(a.shape))


def call(body, args, specs, outs, flops, scratch=(), many=True):
    moved = sum(a.size * a.dtype.itemsize for a in args) + sum(
        o.size * o.dtype.itemsize for o in outs
    )
    return pl.pallas_call(
        body,
        grid=(1,),
        out_shape=tuple(outs) if many else outs[0],
        in_specs=[whole(a) if s is None else s for a, s in zip(args, specs)],
        out_specs=tuple(whole(o) for o in outs) if many else whole(outs[0]),
        scratch_shapes=list(scratch),
        compiler_params=pltpu.CompilerParams(vmem_limit_bytes=40 * 1024 * 1024),
        cost_estimate=pl.CostEstimate(flops=flops, bytes_accessed=moved, transcendentals=0),
    )(*args)


def exchange(chunks):
    return lax.all_to_all(chunks, "seq", 0, 0, tiled=True)


def run_layer(layer, received, place, params):
    gain, in_weight, ws, conv_weight, conv_bias, cols, skip, out_gain, out_weight = params
    fronts = call(
        functools.partial(front_body, layer),
        (received, gain, in_weight, ws, conv_weight, conv_bias, cols),
        (None, None, layer_half((layer, 1), 0), None, None, None, None),
        (
            shaped((TOKENS, D), BF),
            shaped((TOKENS, D), BF),
            shaped((TOKENS, INNER), BF),
            shaped((16, TOKENS), BF),
            shaped((TOKENS, 16), BF),
            shaped((TOKENS, 16), F32),
            shaped((16, TOKENS), F32),
            shaped((16, INNER), F32),
            shaped((8, INNER), F32),
            shaped((PEERS, STATE_ROWS, 128), BF),
        ),
        1_000_000_000,
        [pltpu.VMEM((TOKENS + 8, INNER), F32)],
    )
    xs, normed, xc, bt, cc, cum, rt, local, decays, send = fronts
    arrived = exchange(send)
    z, y, ct = call(
        functools.partial(middle_body, layer),
        (normed, in_weight, xc, bt, cc, cum, rt, skip),
        (None, layer_half((layer, 0), 0)) + (None,) * 6,
        (
            shaped((TOKENS, INNER), BF),
            shaped((TOKENS, INNER), F32),
            shaped((TOKENS, 192), BF),
        ),
        1_000_000_000,
    )
    out = shaped((TOKENS, D), BF) if layer else shaped((PEERS, CHUNK, D), BF)
    args = (place, arrived, local, decays, z, y, ct, xs, out_gain, out_weight)
    specs = [pl.BlockSpec(memory_space=pltpu.SMEM)] + [None] * 8
    specs.append(pl.BlockSpec((1, INNER, D), lambda *_: (layer, 0, 0)))
    return call(
        functools.partial(finish_body, layer), args, specs, (out,), 1_000_000_000, many=False
    )


def on_device(
    slide_tiles,
    norm_gain,
    in_weight,
    state_weight,
    conv_weight,
    conv_bias,
    step_bias,
    decay_log,
    skip_gain,
    out_gain,
    out_weight,
):
    place = lax.axis_index("seq").astype(jnp.int32).reshape(1)
    ws = jnp.pad(jnp.swapaxes(state_weight, 1, 2), ((0, 0), (0, 4), (0, 0)))
    conv_cols = jnp.concatenate(
        [
            jnp.swapaxes(conv_weight[:, :, INNER:], 1, 2),
            conv_bias[:, INNER:, None],
            jnp.zeros((2, 32, 3), F32),
        ],
        axis=2,
    )
    head_cols = jnp.stack([step_bias, decay_log], axis=2)
    head_cols = jnp.pad(head_cols, ((0, 0), (0, 4), (5, 1)))
    cols = jnp.concatenate([conv_cols, head_cols], axis=1)
    skip = jnp.pad(skip_gain, ((0, 0), (0, 4)))
    params = (
        norm_gain,
        in_weight,
        ws,
        conv_weight,
        conv_bias,
        cols,
        skip,
        out_gain,
        out_weight,
    )
    send = call(
        pack_body,
        (slide_tiles,),
        (None,),
        (shaped((PEERS, CHUNK, D), BF),),
        1_000_000,
        many=False,
    )
    middle = run_layer(0, exchange(send), place, params)
    result = run_layer(1, exchange(middle), place, params)
    return result.reshape(slide_tiles.shape)


def solution(mesh):
    placed = (P(("dp", "seq"), None, None), P(), P(), P(), P(), P(), P(), P(), P(), P(), P())
    return jax.shard_map(
        on_device,
        mesh=mesh,
        in_specs=placed,
        out_specs=P(("dp", "seq"), None, None),
        check_vma=False,
    )
```

time: 341 us -> 118 us (0.35)
  the two profiles are of different devices: /device:TPU:127 before, /device:TPU:1 now
where the time goes in v1:
time: 118 us; the launch traced here: 117 us
  local copies, waits for them, and re-layouts  45.4 us (38%)
  Pallas kernels  19 us (16%)
  starting transfers between devices  17.7 us (15%)
  waiting for transfers between devices  17.5 us (15%)
  blocking collectives  15.9 us (13%)
    unnamed x127, local copies, waits for them, and re-layouts  43.9 us
    pallas_call x7, Pallas kernels, call(): pl.pallas_call(body, grid=(1,), out_shape=tuple(outs) if many else outs[0...  19 us
    all_to_all x3, starting transfers between devices, exchange(): return lax.all_to_all(chunks, 'seq', 0, 0, tiled=True)  17.7 us
    all_to_all x3, waiting for transfers between devices, exchange(): return lax.all_to_all(chunks, 'seq', 0, 0, tiled=True)  17.5 us
    all_to_all x1, blocking collectives, exchange(): return lax.all_to_all(chunks, 'seq', 0, 0, tiled=True)  15.9 us
  transfers between devices with their start and end apart: 3, of which 3 were waited for; matrix products, arithmetic and copies ran while one was open for 3% of the time, Pallas kernels for 4%

profile of v1, /device:TPU:1, one launch (start us, length us, event | category | flops | bytes accessed | tf_op | source)
XLA Modules:
  0.0 116.5 jit_solution(4681771967417690016)
XLA Ops:
  0.0 1.1 copy-done.23
  2.1 8.6 %all-to-all-start = ((bf16[32,24,384]{2,1,0:T(8,128)(2,1)}), bf16[32,24,384]{2,1,0:T(8,128)(2,1)S(1)}, u32[]{:S(2)}, u32[]{:S(2)}) async-start(bf16[32,24,384]{2,1,0:T(8,128)(2,1)} %shard_map.109), calls=%async_computation | async-start | bytes 1179648 | tf_op jit(solution)/shard_map/all_to_all | solution.py:337
  13.9 9.1 %all-to-all-done.recv_ref = bf16[32,24,384]{2,1,0:T(8,128)(2,1)S(1)} async-done(((bf16[32,24,384]{2,1,0:T(8,128)(2,1)}), bf16[32,24,384]{2,1,0:T(8,128)(2,1)S(1)}, u32[]{:S(2)}, u32[]{:S(2)}) %all-to-all-start) | async-done | bytes 589856 | tf_op jit(solution)/shard_map/all_to_all | solution.py:337
  23.0 3.9 %shard_map.110 = (bf16[512,384]{1,0:T(8,128)(2,1)S(1)}, bf16[512,384]{1,0:T(8,128)(2,1)S(1)}, bf16[512,768]{1,0:T(8,128)(2,1)S(1)}, bf16[16,512]{1,0:T(8,128)(2,...) custom-call(bf16[32,24,384]{2,1,0:T(8,128)(2,1)S(1)} %all-to-all-don, ...), custom_call_target="tpu_custom_call" | custom-call | flops 1000000000 | bytes 5657856 | tf_op jit(solution)/shard_map/pallas_call | solution.py:324
  33.1 4.6 %all-to-all-start.1 = ((bf16[32,104,128]{2,1,0:T(8,128)(2,1)}), bf16[32,104,128]{2,1,0:T(8,128)(2,1)}, u32[]{:S(2)}, u32[]{:S(2)}) async-start(bf16[32,104,128]{2,1,0:T(8,128)(2,1)} %get-tuple-element.31), calls=%async_computation.1 | async-start | bytes 1703936 | tf_op jit(solution)/shard_map/all_to_all | solution.py:337
  37.7 1.1 copy-done.12
  38.8 1.0 copy-done.20
  43.2 2.1 %shard_map.111 = (bf16[512,768]{1,0:T(8,128)(2,1)S(1)}, f32[512,768]{1,0:T(8,128)S(1)}, bf16[512,192]{1,0:T(8,128)(2,1)S(1)}) custom-call(bf16[512,384]{1,0:T(8,128)(2,1)S(1)} %copy-done.20, bf16[2,384,1536]{2,1,0:T(8,128)(2,1)S(1)} %copy-done, bf16[512,768]{1,0:T(8,128)(2,1)S(1)} %copy-done.12, bf16[16,512]{1,0:T(8,128)(2,1)S(1)} %copy-done.54, ...), custom_call_target="tpu_custom_call" | custom-call | flops 1000000000 | bytes 6193280 | tf_op jit(solution)/shard_map/pallas_call | solution.py:324
  45.3 1.2 %copy-done.4 = f32[512,768]{1,0:T(8,128)} copy-done((f32[512,768]{1,0:T(8,128)}, f32[512,768]{1,0:T(8,128)S(1)}, u32[]{:S(2)}) %copy-start.4) | copy-done | bytes 1572888
  48.1 4.2 %all-to-all-done.1.recv_ref = bf16[32,104,128]{2,1,0:T(8,128)(2,1)} async-done(((bf16[32,104,128]{2,1,0:T(8,128)(2,1)}), bf16[32,104,128]{2,1,0:T(8,128)(2,1)}, u32[]{:S(2)}, u32[]{:S(2)}) %all-to-all-start.1) | async-done | bytes 852000 | tf_op jit(solution)/shard_map/all_to_all | solution.py:337
  52.3 1.4 %copy-done.5 = f32[512,768]{1,0:T(8,128)S(1)} copy-done((f32[512,768]{1,0:T(8,128)S(1)}, f32[512,768]{1,0:T(8,128)}, u32[]{:S(2)}) %copy-start.5) | copy-done | bytes 1572888
  53.7 1.1 copy-done.10
  54.8 1.0 copy-done.16
  58.3 3.4 %shard_map.112 = bf16[32,24,384]{2,1,0:T(8,128)(2,1)S(1)} custom-call(s32[1]{0:T(128)} %bitcast.place_ref, bf16[32,104,128]{2,1,0:T(8,128)(2,1)} %all-to-all-done.1.recv_ref, f32[16,768]{1,0:T(8,128)S(1)} %copy-done.39, f32[8,768]{1,0:T(8,128)S(1)} %copy-done.49, bf16[512,768]{1,0:T(8,128)(2,1)S(1)} %copy-done.10, f32[512,768]{1,0:T(8,128)S(1)} %copy-done.5, ...), custom_call_target="tpu_custom_call" | custom-call | flops 1000000000 | bytes 5650436 | tf_op jit(solution)/shard_map/pallas_call | solution.py:324
  61.7 15.9 %all_to_all.20.recv_ref = bf16[32,24,384]{2,1,0:T(8,128)(2,1)S(1)} all-to-all(bf16[32,24,384]{2,1,0:T(8,128)(2,1)S(1)} %shard_map.112), channel_id=1, replica_groups=mesh['dp'=8,'seq'=32] {'seq'}, dimensions={0} | all-to-all | bytes 1179648 | tf_op jit(solution)/shard_map/all_to_all | solution.py:337
  77.7 3.0 %shard_map.113 = (bf16[512,384]{1,0:T(8,128)(2,1)S(1)}, bf16[512,384]{1,0:T(8,128)(2,1)S(1)}, bf16[512,768]{1,0:T(8,128)(2,1)S(1)}, bf16[16,512]{1,0:T(8,128)(2,...) custom-call(bf16[32,24,384]{2,1,0:T(8,128)(2,1)S(1)} %all_to_all.20., ...), custom_call_target="tpu_custom_call" | custom-call | flops 1000000000 | bytes 5657856 | tf_op jit(solution)/shard_map/pallas_call | solution.py:324
  87.8 4.6 %all-to-all-start.3 = ((bf16[32,104,128]{2,1,0:T(8,128)(2,1)}), bf16[32,104,128]{2,1,0:T(8,128)(2,1)}, u32[]{:S(2)}, u32[]{:S(2)}) async-start(bf16[32,104,128]{2,1,0:T(8,128)(2,1)} %copy-done.6), calls=%async_computation.3 | async-start | bytes 1703936 | tf_op jit(solution)/shard_map/all_to_all | solution.py:337
  92.4 1.1 copy-done.14
  97.9 2.1 %shard_map.114 = (bf16[512,768]{1,0:T(8,128)(2,1)S(1)}, f32[512,768]{1,0:T(8,128)S(1)}, bf16[512,192]{1,0:T(8,128)(2,1)S(1)}) custom-call(bf16[512,384]{1,0:T(8,128)(2,1)S(1)} %copy-done.22, bf16[2,384,1536]{2,1,0:T(8,128)(2,1)S(1)} %copy-done, bf16[512,768]{1,0:T(8,128)(2,1)S(1)} %copy-done.14, bf16[16,512]{1,0:T(8,128)(2,1)S(1)} %copy-done.56, ...), custom_call_target="tpu_custom_call" | custom-call | flops 1000000000 | bytes 6193280 | tf_op jit(solution)/shard_map/pallas_call | solution.py:324
  100.0 1.2 %copy-done.2 = f32[512,768]{1,0:T(8,128)} copy-done((f32[512,768]{1,0:T(8,128)}, f32[512,768]{1,0:T(8,128)S(1)}, u32[]{:S(2)}) %copy-start.2) | copy-done | bytes 1572888
  102.8 4.2 %all-to-all-done.3.recv_ref = bf16[32,104,128]{2,1,0:T(8,128)(2,1)} async-done(((bf16[32,104,128]{2,1,0:T(8,128)(2,1)}), bf16[32,104,128]{2,1,0:T(8,128)(2,1)}, u32[]{:S(2)}, u32[]{:S(2)}) %all-to-all-start.3) | async-done | bytes 852000 | tf_op jit(solution)/shard_map/all_to_all | solution.py:337
  107.0 1.4 %copy-done.3 = f32[512,768]{1,0:T(8,128)S(1)} copy-done((f32[512,768]{1,0:T(8,128)S(1)}, f32[512,768]{1,0:T(8,128)}, u32[]{:S(2)}) %copy-start.3) | copy-done | bytes 1572888
  108.4 1.1 copy-done.8
  113.0 3.5 %shard_map.115 = bf16[512,384]{1,0:T(8,128)(2,1)} custom-call(s32[1]{0:T(128)} %bitcast.place_ref, bf16[32,104,128]{2,1,0:T(8,128)(2,1)} %all-to-all-done.3.recv_ref, f32[16,768]{1,0:T(8,128)S(1)} %copy-done.41, f32[8,768]{1,0:T(8,128)S(1)} %copy-done.51, bf16[512,768]{1,0:T(8,128)(2,1)S(1)} %copy-done.8, f32[512,768]{1,0:T(8,128)S(1)} %copy-done.3, ...), custom_call_target="tpu_custom_call" | custom-call | flops 1000000000 | bytes 5453828 | tf_op jit(solution)/shard_map/pallas_call | solution.py:324
  (126 shorter events, 34.3 us)
Async XLA Ops:
  0.0 23.0 %copy-start = (bf16[2,384,1536]{2,1,0:T(8,128)(2,1)S(1)}, bf16[2,384,1536]{2,1,0:T(8,128)(2,1)}, u32[]{:S(2)}) copy-start(bf16[2,384,1536]{2,1,0:T(8,128)(2,1)} %wz_ref.3) | copy-start | bytes 7077892
  0.0 1.1 copy-start.23
  1.1 21.8 %copy-start.57 = (f32[2,4,800]{2,1,0:T(4,128)S(1)}, f32[2,4,800]{2,1,0:T(4,128)}, u32[]{:S(2)}) copy-start(f32[2,4,800]{2,1,0:T(4,128)} %cw_ref.3) | copy-start | bytes 76804
  1.2 21.8 %copy-start.59 = (f32[2,800]{1,0:T(2,128)S(1)}, f32[2,800]{1,0:T(2,128)}, u32[]{:S(2)}) copy-start(f32[2,800]{1,0:T(2,128)} %cb_ref.3) | copy-start | bytes 19204
  1.2 21.8 %copy-start.61 = (f32[2,384]{1,0:T(2,128)S(1)}, f32[2,384]{1,0:T(2,128)}, u32[]{:S(2)}) copy-start(f32[2,384]{1,0:T(2,128)} %gain_ref.6) | copy-start | bytes 9220
  2.1 20.9 %all-to-all-start = ((bf16[32,24,384]{2,1,0:T(8,128)(2,1)}), bf16[32,24,384]{2,1,0:T(8,128)(2,1)S(1)}, u32[]{:S(2)}, u32[]{:S(2)}) async-start(bf16[32,24,384]{2,1,0:T(8,128)(2,1)} %shard_map.109), calls=%async_computation | async-start | bytes 1179648 | tf_op jit(solution)/shard_map/all_to_all | solution.py:337
  13.9 13.0 %copy-start.42 = (f32[2,48,8]{2,1,0:T(8,128)}, f32[2,48,8]{2,1,0:T(8,128)S(1)}, u32[]{:S(2)}) copy-start(f32[2,48,8]{2,1,0:T(8,128)S(1)} %copy.21.col_ref) | copy-start | bytes 9220
  13.9 13.0 %copy-start.36 = (bf16[2,48,384]{2,1,0:T(8,128)(2,1)}, bf16[2,48,384]{2,1,0:T(8,128)(2,1)S(1)}, u32[]{:S(2)}) copy-start(bf16[2,48,384]{2,1,0:T(8,128)(2,1)S(1)} %pad.12.ws_ref) | copy-start | bytes 221188
  33.1 4.6 %copy-start.62 = (f32[2,12]{1,0:T(2,128)S(1)}, f32[2,12]{1,0:T(2,128)}, u32[]{:S(2)}) copy-start(f32[2,12]{1,0:T(2,128)} %param.19) | copy-start | bytes 292
  33.1 19.2 %all-to-all-start.1 = ((bf16[32,104,128]{2,1,0:T(8,128)(2,1)}), bf16[32,104,128]{2,1,0:T(8,128)(2,1)}, u32[]{:S(2)}, u32[]{:S(2)}) async-start(bf16[32,104,128]{2,1,0:T(8,128)(2,1)} %get-tuple-element.31), calls=%async_computation.1 | async-start | bytes 1703936 | tf_op jit(solution)/shard_map/all_to_all | solution.py:337
  37.7 1.1 copy-start.12
  43.2 9.1 %copy-start.1 = (bf16[2,768,384]{2,1,0:T(8,128)(2,1)S(1)}, bf16[2,768,384]{2,1,0:T(8,128)(2,1)}, u32[]{:S(2)}) copy-start(bf16[2,768,384]{2,1,0:T(8,128)(2,1)} %wo_ref.3) | copy-start | bytes 3538948
  43.2 9.1 %copy-start.52 = (f32[2,768]{1,0:T(2,128)S(1)}, f32[2,768]{1,0:T(2,128)}, u32[]{:S(2)}) copy-start(f32[2,768]{1,0:T(2,128)} %gain_ref.7) | copy-start | bytes 18436
  45.3 1.2 %copy-start.4 = (f32[512,768]{1,0:T(8,128)}, f32[512,768]{1,0:T(8,128)S(1)}, u32[]{:S(2)}) copy-start(f32[512,768]{1,0:T(8,128)S(1)} %get-tuple-element.41.y_ref) | copy-start | bytes 4718596
  52.3 1.4 %copy-start.5 = (f32[512,768]{1,0:T(8,128)S(1)}, f32[512,768]{1,0:T(8,128)}, u32[]{:S(2)}) copy-start(f32[512,768]{1,0:T(8,128)} %copy-done.4) | copy-start | bytes 4718596
  53.7 1.1 copy-start.10
  58.3 19.4 %copy-start.37 = (bf16[2,48,384]{2,1,0:T(8,128)(2,1)S(1)}, bf16[2,48,384]{2,1,0:T(8,128)(2,1)}, u32[]{:S(2)}) copy-start(bf16[2,48,384]{2,1,0:T(8,128)(2,1)} %copy-done.36) | copy-start | bytes 221188
  58.3 19.4 %copy-start.43 = (f32[2,48,8]{2,1,0:T(8,128)S(1)}, f32[2,48,8]{2,1,0:T(8,128)}, u32[]{:S(2)}) copy-start(f32[2,48,8]{2,1,0:T(8,128)} %copy-done.42) | copy-start | bytes 9220
  58.3 19.4 %copy-start.58 = (f32[2,4,800]{2,1,0:T(4,128)S(1)}, f32[2,4,800]{2,1,0:T(4,128)}, u32[]{:S(2)}) copy-start(f32[2,4,800]{2,1,0:T(4,128)} %cw_ref.3) | copy-start | bytes 76804
  58.3 19.4 %copy-start.60 = (f32[2,800]{1,0:T(2,128)S(1)}, f32[2,800]{1,0:T(2,128)}, u32[]{:S(2)}) copy-start(f32[2,800]{1,0:T(2,128)} %cb_ref.3) | copy-start | bytes 19204
  87.8 19.2 %all-to-all-start.3 = ((bf16[32,104,128]{2,1,0:T(8,128)(2,1)}), bf16[32,104,128]{2,1,0:T(8,128)(2,1)}, u32[]{:S(2)}, u32[]{:S(2)}) async-start(bf16[32,104,128]{2,1,0:T(8,128)(2,1)} %copy-done.6), calls=%async_computation.3 | async-start | bytes 1703936 | tf_op jit(solution)/shard_map/all_to_all | solution.py:337
  92.4 1.1 copy-start.14
  100.0 1.2 %copy-start.2 = (f32[512,768]{1,0:T(8,128)}, f32[512,768]{1,0:T(8,128)S(1)}, u32[]{:S(2)}) copy-start(f32[512,768]{1,0:T(8,128)S(1)} %get-tuple-element.54.y_ref) | copy-start | bytes 4718596
  107.0 1.4 %copy-start.3 = (f32[512,768]{1,0:T(8,128)S(1)}, f32[512,768]{1,0:T(8,128)}, u32[]{:S(2)}) copy-start(f32[512,768]{1,0:T(8,128)} %copy-done.2) | copy-start | bytes 4718596
  (42 other events, 33.3 us)

commit v2 on v1

--- a/solution.py
+++ b/solution.py
@@ -1,4 +1,5 @@
 import functools
+import math
 
 import jax
 import jax.numpy as jnp
@@ -63,16 +64,16 @@
 
 
 def pack_body(tiles_ref, send_ref):
-    rows = [tiles_ref[r].astype(F32).reshape(PEERS, 8, D) for r in range(2)]
-    after = [jnp.concatenate([r[1:], jnp.zeros((1, 8, D), F32)], axis=0) for r in rows]
-    place = iota((PEERS, 8, D), 1)
-    second = jnp.concatenate([after[1][:, :1], after[1][:, :1]], axis=1)
-    halo = jnp.where(
-        place == 0,
-        after[0],
-        jnp.where(place == 1, jnp.broadcast_to(second[:, :1], (PEERS, 8, D)), 0.0),
-    )
-    send_ref[...] = jnp.concatenate([rows[0], rows[1], halo], axis=1).astype(BF)
+    halo = jnp.zeros((PEERS, 8, 128), F32)
+    slot = iota((PEERS, 8, 128), 1)
+    for b in range(3):
+        lanes = slice(128 * b, 128 * b + 128)
+        rows = [tiles_ref[r, :, lanes].astype(F32).reshape(PEERS, 8, 128) for r in range(2)]
+        send_ref[:, 16 * b : 16 * b + 16, :] = jnp.concatenate(rows, axis=1).astype(BF)
+        for r in range(2):
+            after = jnp.concatenate([rows[r][1:, 0:1], jnp.zeros((1, 1, 128), F32)], axis=0)
+            halo = jnp.where(slot == 2 * b + r, after, halo)
+    send_ref[:, 48:56, :] = halo.astype(BF)
 
 
 def front_body(
@@ -96,29 +97,33 @@
     send_ref,
     conv_ref,
 ):
-    main = recv_ref[:, 0:16, :].reshape(TOKENS, D)
     t = iota((TOKENS, 1), 0)
+    place = iota((16, 1), 0)
     if layer == 0:
+        main = jnp.concatenate(
+            [recv_ref[:, 16 * b : 16 * b + 16, :].reshape(TOKENS, 128) for b in range(3)], axis=1
+        )
         column = 511 - 8 * jnp.bitwise_and(t, 63) - lax.shift_right_logical(t, 6)
         halo_in = jnp.concatenate(
-            [recv_ref[0, 16:24, :].astype(F32), recv_ref[1, 16:24, :].astype(F32)], axis=0
+            [recv_ref[0, 48:56, :].astype(F32), recv_ref[1, 48:56, :].astype(F32)], axis=0
+        ).astype(BF)
+        picked = jnp.where(
+            place == 13, 8, jnp.where(place == 14, 1, jnp.where(place == 15, 0, -16))
         )
-        place = iota((16, 1), 0)
-        picked = jnp.where(
-            place == 13, 8, jnp.where(place == 14, 1, jnp.where(place == 15, 0, -1))
+        halo = jnp.concatenate(
+            [dot(one_hot((16, 16), picked + 2 * b), halo_in) for b in range(3)], axis=1
         )
     else:
+        main = recv_ref[:, 0:16, :].reshape(TOKENS, D)
         low = jnp.bitwise_and(t, 7)
         column = (
             2 * (jnp.bitwise_and(t, 255) - low) + 8 * lax.shift_right_logical(t, 8) + low
         )
         halo_in = jnp.concatenate(
             [recv_ref[PEERS - 1, 16:24, :].astype(F32), jnp.zeros((8, D), F32)], axis=0
-        )
-        place = iota((16, 1), 0)
-        picked = jnp.where(place >= 13, place - 13, -1)
+        ).astype(BF)
+        halo = dot(one_hot((16, 16), jnp.where(place >= 13, place - 13, -1)), halo_in)
     xs = dot(one_hot((TOKENS, TOKENS), column), main)
-    halo = dot(one_hot((16, 16), picked), halo_in.astype(BF))
     xs_ref[...] = xs.astype(BF)
     gain = gain_ref[layer : layer + 1, :]
     normed = rms(xs, gain).astype(BF)
@@ -313,13 +318,21 @@
     return jax.ShapeDtypeStruct(shape, dtype)
 
 
+def kept(shape, dtype):
+    return pltpu.HBM(shape, dtype)
+
+
+def pinned(*arrays):
+    return tuple(pltpu.with_memory_space_constraint(a, pltpu.HBM) for a in arrays)
+
+
 def whole(a):
     return pl.BlockSpec(a.shape, lambda *_: (0,) * len(a.shape))
 
 
 def call(body, args, specs, outs, flops, scratch=(), many=True):
     moved = sum(a.size * a.dtype.itemsize for a in args) + sum(
-        o.size * o.dtype.itemsize for o in outs
+        math.prod(o.shape) * jnp.dtype(o.dtype).itemsize for o in outs
     )
     return pl.pallas_call(
         body,
@@ -344,33 +357,33 @@
         (received, gain, in_weight, ws, conv_weight, conv_bias, cols),
         (None, None, layer_half((layer, 1), 0), None, None, None, None),
         (
-            shaped((TOKENS, D), BF),
-            shaped((TOKENS, D), BF),
-            shaped((TOKENS, INNER), BF),
-            shaped((16, TOKENS), BF),
-            shaped((TOKENS, 16), BF),
-            shaped((TOKENS, 16), F32),
-            shaped((16, TOKENS), F32),
-            shaped((16, INNER), F32),
-            shaped((8, INNER), F32),
-            shaped((PEERS, STATE_ROWS, 128), BF),
+            kept((TOKENS, D), BF),
+            kept((TOKENS, D), BF),
+            kept((TOKENS, INNER), BF),
+            kept((16, TOKENS), BF),
+            kept((TOKENS, 16), BF),
+            kept((TOKENS, 16), F32),
+            kept((16, TOKENS), F32),
+            kept((16, INNER), F32),
+            kept((8, INNER), F32),
+            kept((PEERS, STATE_ROWS, 128), BF),
         ),
         1_000_000_000,
         [pltpu.VMEM((TOKENS + 8, INNER), F32)],
     )
-    xs, normed, xc, bt, cc, cum, rt, local, decays, send = fronts
+    xs, normed, xc, bt, cc, cum, rt, local, decays, send = pinned(*fronts)
     arrived = exchange(send)
-    z, y, ct = call(
+    z, y, ct = pinned(*call(
         functools.partial(middle_body, layer),
         (normed, in_weight, xc, bt, cc, cum, rt, skip),
         (None, layer_half((layer, 0), 0)) + (None,) * 6,
         (
-            shaped((TOKENS, INNER), BF),
-            shaped((TOKENS, INNER), F32),
-            shaped((TOKENS, 192), BF),
+            kept((TOKENS, INNER), BF),
+            kept((TOKENS, INNER), F32),
+            kept((TOKENS, 192), BF),
         ),
         1_000_000_000,
-    )
+    ))
     out = shaped((TOKENS, D), BF) if layer else shaped((PEERS, CHUNK, D), BF)
     args = (place, arrived, local, decays, z, y, ct, xs, out_gain, out_weight)
     specs = [pl.BlockSpec(memory_space=pltpu.SMEM)] + [None] * 8
@@ -422,7 +435,7 @@
         pack_body,
         (slide_tiles,),
         (None,),
-        (shaped((PEERS, CHUNK, D), BF),),
+        (kept((PEERS, 56, 128), BF),),
         1_000_000,
         many=False,
     )

time: 118 us -> 95.1 us (0.81)
  local copies, waits for them, and re-layouts: 45.4 us -> 2.88 us
  waiting for transfers between devices: 17.5 us -> 30 us
  Pallas kernels: 19 us -> 27.8 us
    unnamed x127 -> x39, local copies, waits for them, and re-layouts: 43.9 us -> 2.75 us
    all_to_all x3, waiting for transfers between devices: 17.5 us -> 30 us  [exchange(): return lax.all_to_all(chunks, 'seq', 0, 0, tiled=True)]
    pallas_call x7, Pallas kernels: 19 us -> 27.8 us  [call(): pl.pallas_call(body, grid=(1,), out_shape=tuple(outs) if many else outs[0...]
  transfers between devices with their start and end apart: 3 -> 3, of which waited for: 3 -> 3; matrix products, arithmetic and copies ran while one was open for 3% -> 0% of each run, Pallas kernels for 4% -> 10%
where the time goes in v2:
time: 95.1 us; the launch traced here: 94.5 us
  waiting for transfers between devices  30 us (32%)
  Pallas kernels  27.8 us (29%)
  starting transfers between devices  17.6 us (19%)
  blocking collectives  15.9 us (17%)
  local copies, waits for them, and re-layouts  2.88 us (3%)
    all_to_all x3, waiting for transfers between devices, exchange(): return lax.all_to_all(chunks, 'seq', 0, 0, tiled=True)  30 us
    pallas_call x7, Pallas kernels, call(): pl.pallas_call(body, grid=(1,), out_shape=tuple(outs) if many else outs[0...  27.8 us
    all_to_all x3, starting transfers between devices, exchange(): return lax.all_to_all(chunks, 'seq', 0, 0, tiled=True)  17.6 us
    all_to_all x1, blocking collectives, exchange(): return lax.all_to_all(chunks, 'seq', 0, 0, tiled=True)  15.9 us
    unnamed x39, local copies, waits for them, and re-layouts  2.75 us
  transfers between devices with their start and end apart: 3, of which 3 were waited for; matrix products, arithmetic and copies ran while one was open for 0% of the time, Pallas kernels for 10%

profile of v2, /device:TPU:1, one launch (start us, length us, event | category | flops | bytes accessed | tf_op | source)
XLA Modules:
  0.0 94.5 jit_solution(2782276776446566400)
XLA Ops:
  0.0 1.0 %copy-done.3 = bf16[2,256,384]{2,1,0:T(8,128)(2,1)S(1)} copy-done((bf16[2,256,384]{2,1,0:T(8,128)(2,1)S(1)}, bf16[2,256,384]{2,1,0:T(8,128)(2,1)}, u32[]{:S(2)}) %copy-start.3) | copy-done | bytes 393240
  1.0 0.0 slice-start
  1.0 0.0 copy-start.13
  1.0 0.9 shard_map.109
  2.0 8.6 %all-to-all-start = ((bf16[32,56,128]{2,1,0:T(8,128)(2,1)}), bf16[32,56,128]{2,1,0:T(8,128)(2,1)S(1)}, u32[]{:S(2)}, u32[]{:S(2)}) async-start(bf16[32,56,128]{2,1,0:T(8,128)(2,1)} %shard_map.109), calls=%async_computation | async-start | bytes 917504 | tf_op jit(solution)/shard_map/all_to_all | solution.py:350
  10.7 0.1 pad_maximum_fusion
  10.8 0.1 copy.21.col_ref
  10.9 10.6 %all-to-all-done.recv_ref = bf16[32,56,128]{2,1,0:T(8,128)(2,1)S(1)} async-done(((bf16[32,56,128]{2,1,0:T(8,128)(2,1)}), bf16[32,56,128]{2,1,0:T(8,128)(2,1)S(1)}, u32[]{:S(2)}, u32[]{:S(2)}) %all-to-all-start) | async-done | bytes 458784 | tf_op jit(solution)/shard_map/all_to_all | solution.py:350
  21.5 1.7 %copy-done = bf16[2,384,1536]{2,1,0:T(8,128)(2,1)S(1)} copy-done((bf16[2,384,1536]{2,1,0:T(8,128)(2,1)S(1)}, bf16[2,384,1536]{2,1,0:T(8,128)(2,1)}, u32[]{:S(2)}) %copy-start) | copy-done | bytes 2359320
  23.2 4.3 %shard_map.110 = (bf16[512,384]{1,0:T(8,128)(2,1)}, bf16[512,384]{1,0:T(8,128)(2,1)}, bf16[512,768]{1,0:T(8,128)(2,1)}, bf16[16,512]{1,0:T(8,128)(2,1)}, bf16[51...) custom-call(bf16[32,56,128]{2,1,0:T(8,128)(2,1)S(1)} %all-to-all-don, ...), custom_call_target="tpu_custom_call" | custom-call | flops 1000000000 | bytes 5526784 | tf_op jit(solution)/shard_map/pallas_call | solution.py:337
  27.5 4.4 %all-to-all-start.1 = ((bf16[32,104,128]{2,1,0:T(8,128)(2,1)}), bf16[32,104,128]{2,1,0:T(8,128)(2,1)}, u32[]{:S(2)}, u32[]{:S(2)}) async-start(bf16[32,104,128]{2,1,0:T(8,128)(2,1)} %get-tuple-element.31), calls=%async_computation.1 | async-start | bytes 1703936 | tf_op jit(solution)/shard_map/all_to_all | solution.py:350
  31.9 0.0 copy-start.2
  32.0 0.0 copy-start.8
  32.0 4.9 %shard_map.111 = (bf16[512,768]{1,0:T(8,128)(2,1)}, f32[512,768]{1,0:T(8,128)}, bf16[512,192]{1,0:T(8,128)(2,1)}) custom-call(bf16[512,384]{1,0:T(8,128)(2,1)} %get-tuple-element.34.nm_ref, bf16[2,384,1536]{2,1,0:T(8,128)(2,1)S(1)} %copy-done.1, bf16[512,768]{1,0:T(8,128)(2,1)} %get-tuple-element.35.xc_ref, bf16[16,512]{1,0:T(8,128)(2,1)} %get-tuple-element.36.bt_ref, ...), custom_call_target="tpu_custom_call" | custom-call | flops 1000000000 | bytes 6193280 | tf_op jit(solution)/shard_map/pallas_call | solution.py:337
  36.8 9.7 %all-to-all-done.1.recv_ref = bf16[32,104,128]{2,1,0:T(8,128)(2,1)} async-done(((bf16[32,104,128]{2,1,0:T(8,128)(2,1)}), bf16[32,104,128]{2,1,0:T(8,128)(2,1)}, u32[]{:S(2)}, u32[]{:S(2)}) %all-to-all-start.1) | async-done | bytes 852000 | tf_op jit(solution)/shard_map/all_to_all | solution.py:350
  46.6 0.0 copy-start.10
  46.6 0.0 copy-start.14
  46.6 4.3 %shard_map.112 = bf16[32,24,384]{2,1,0:T(8,128)(2,1)S(1)} custom-call(s32[1]{0:T(128)} %bitcast.place_ref, bf16[32,104,128]{2,1,0:T(8,128)(2,1)} %all-to-all-done.1.recv_ref, f32[16,768]{1,0:T(8,128)} %get-tuple-element.32.loc_ref, f32[8,768]{1,0:T(8,128)} %get-tuple-element.33.dec_ref, bf16[512,768]{1,0:T(8,128)(2,1)} %get-tuple-element.40.z_ref, ...), custom_call_target="tpu_custom_call" | custom-call | flops 1000000000 | bytes 5650436 | tf_op jit(solution)/shard_map/pallas_call | solution.py:337
  50.9 15.9 %all_to_all.20.recv_ref = bf16[32,24,384]{2,1,0:T(8,128)(2,1)S(1)} all-to-all(bf16[32,24,384]{2,1,0:T(8,128)(2,1)S(1)} %shard_map.112), channel_id=1, replica_groups=mesh['dp'=8,'seq'=32] {'seq'}, dimensions={0} | all-to-all | bytes 1179648 | tf_op jit(solution)/shard_map/all_to_all | solution.py:350
  66.9 4.2 %shard_map.113 = (bf16[512,384]{1,0:T(8,128)(2,1)}, bf16[512,384]{1,0:T(8,128)(2,1)}, bf16[512,768]{1,0:T(8,128)(2,1)}, bf16[16,512]{1,0:T(8,128)(2,1)}, bf16[51...) custom-call(bf16[32,24,384]{2,1,0:T(8,128)(2,1)S(1)} %all_to_all.20., ...), custom_call_target="tpu_custom_call" | custom-call | flops 1000000000 | bytes 5657856 | tf_op jit(solution)/shard_map/pallas_call | solution.py:337
  71.1 4.6 %all-to-all-start.3 = ((bf16[32,104,128]{2,1,0:T(8,128)(2,1)}), bf16[32,104,128]{2,1,0:T(8,128)(2,1)}, u32[]{:S(2)}, u32[]{:S(2)}) async-start(bf16[32,104,128]{2,1,0:T(8,128)(2,1)} %get-tuple-element.44), calls=%async_computation.3 | async-start | bytes 1703936 | tf_op jit(solution)/shard_map/all_to_all | solution.py:350
  75.7 4.8 %shard_map.114 = (bf16[512,768]{1,0:T(8,128)(2,1)}, f32[512,768]{1,0:T(8,128)}, bf16[512,192]{1,0:T(8,128)(2,1)}) custom-call(bf16[512,384]{1,0:T(8,128)(2,1)} %get-tuple-element.47.nm_ref, bf16[2,384,1536]{2,1,0:T(8,128)(2,1)S(1)} %copy-done.1, bf16[512,768]{1,0:T(8,128)(2,1)} %get-tuple-element.48.xc_ref, bf16[16,512]{1,0:T(8,128)(2,1)} %get-tuple-element.49.bt_ref, ...), custom_call_target="tpu_custom_call" | custom-call | flops 1000000000 | bytes 6193280 | tf_op jit(solution)/shard_map/pallas_call | solution.py:337
  80.5 9.6 %all-to-all-done.3.recv_ref = bf16[32,104,128]{2,1,0:T(8,128)(2,1)} async-done(((bf16[32,104,128]{2,1,0:T(8,128)(2,1)}), bf16[32,104,128]{2,1,0:T(8,128)(2,1)}, u32[]{:S(2)}, u32[]{:S(2)}) %all-to-all-start.3) | async-done | bytes 852000 | tf_op jit(solution)/shard_map/all_to_all | solution.py:350
  90.1 4.4 %shard_map.115 = bf16[512,384]{1,0:T(8,128)(2,1)} custom-call(s32[1]{0:T(128)} %bitcast.place_ref, bf16[32,104,128]{2,1,0:T(8,128)(2,1)} %all-to-all-done.3.recv_ref, f32[16,768]{1,0:T(8,128)} %get-tuple-element.45.loc_ref, f32[8,768]{1,0:T(8,128)} %get-tuple-element.46.dec_ref, bf16[512,768]{1,0:T(8,128)(2,1)} %get-tuple-element.53.z_ref, ...), custom_call_target="tpu_custom_call" | custom-call | flops 1000000000 | bytes 5453828 | tf_op jit(solution)/shard_map/pallas_call | solution.py:337
  (39 shorter events, 0.1 us)
Async XLA Ops:
  0.0 1.0 %copy-start.3 = (bf16[2,256,384]{2,1,0:T(8,128)(2,1)S(1)}, bf16[2,256,384]{2,1,0:T(8,128)(2,1)}, u32[]{:S(2)}) copy-start(bf16[2,256,384]{2,1,0:T(8,128)(2,1)} %tiles_ref.1) | copy-start | bytes 1179652
  1.0 9.6 %copy-start.15 = (bf16[2,384,44]{1,0,2:T(2,128)(2,1)S(1)}, bf16[2,384,44]{1,0,2:T(2,128)(2,1)}, u32[]{:S(2)}) copy-start(bf16[2,384,44]{1,0,2:T(2,128)(2,1)} %param.14) | copy-start | bytes 202756
  1.0 9.6 %copy-start.16 = (f32[2,12]{1,0:T(2,128)S(1)}, f32[2,12]{1,0:T(2,128)}, u32[]{:S(2)}) copy-start(f32[2,12]{1,0:T(2,128)} %param.18) | copy-start | bytes 292
  1.0 9.6 %copy-start.17 = (f32[2,12]{1,0:T(2,128)S(1)}, f32[2,12]{1,0:T(2,128)}, u32[]{:S(2)}) copy-start(f32[2,12]{1,0:T(2,128)} %param.17) | copy-start | bytes 292
  1.0 9.6 %copy-start.9 = (f32[2,4,800]{2,1,0:T(4,128)S(1)}, f32[2,4,800]{2,1,0:T(4,128)}, u32[]{:S(2)}) copy-start(f32[2,4,800]{2,1,0:T(4,128)} %cw_ref.3) | copy-start | bytes 76804
  1.0 9.7 %slice-start = ((f32[2,800]{1,0:T(2,128)}), f32[2,32]{1,0:T(2,128)S(1)}, s32[]{:S(2)}) async-start(f32[2,800]{1,0:T(2,128)} %cb_ref.3), calls=%async_computation.4 | async-start | bytes 2048 | tf_op jit(solution)/shard_map/slice | solution.py:414
  1.0 20.5 %copy-start.11 = (f32[2,800]{1,0:T(2,128)S(1)}, f32[2,800]{1,0:T(2,128)}, u32[]{:S(2)}) copy-start(f32[2,800]{1,0:T(2,128)} %cb_ref.3) | copy-start | bytes 19204
  1.0 20.5 %copy-start.13 = (f32[2,384]{1,0:T(2,128)S(1)}, f32[2,384]{1,0:T(2,128)}, u32[]{:S(2)}) copy-start(f32[2,384]{1,0:T(2,128)} %gain_ref.6) | copy-start | bytes 9220
  2.0 19.6 %all-to-all-start = ((bf16[32,56,128]{2,1,0:T(8,128)(2,1)}), bf16[32,56,128]{2,1,0:T(8,128)(2,1)S(1)}, u32[]{:S(2)}, u32[]{:S(2)}) async-start(bf16[32,56,128]{2,1,0:T(8,128)(2,1)} %shard_map.109), calls=%async_computation | async-start | bytes 917504 | tf_op jit(solution)/shard_map/all_to_all | solution.py:350
  10.8 16.6 %copy-start.6 = (f32[2,48,8]{2,1,0:T(8,128)}, f32[2,48,8]{2,1,0:T(8,128)S(1)}, u32[]{:S(2)}) copy-start(f32[2,48,8]{2,1,0:T(8,128)S(1)} %copy.21.col_ref) | copy-start | bytes 9220
  10.9 16.6 %copy-start.4 = (bf16[2,48,384]{2,1,0:T(8,128)(2,1)}, bf16[2,48,384]{2,1,0:T(8,128)(2,1)S(1)}, u32[]{:S(2)}) copy-start(bf16[2,48,384]{2,1,0:T(8,128)(2,1)S(1)} %pad.12.ws_ref) | copy-start | bytes 221188
  21.5 1.7 %copy-start = (bf16[2,384,1536]{2,1,0:T(8,128)(2,1)S(1)}, bf16[2,384,1536]{2,1,0:T(8,128)(2,1)}, u32[]{:S(2)}) copy-start(bf16[2,384,1536]{2,1,0:T(8,128)(2,1)} %wz_ref.3) | copy-start | bytes 7077892
  23.2 8.7 %copy-start.1 = (bf16[2,384,1536]{2,1,0:T(8,128)(2,1)S(1)}, bf16[2,384,1536]{2,1,0:T(8,128)(2,1)}, u32[]{:S(2)}) copy-start(bf16[2,384,1536]{2,1,0:T(8,128)(2,1)} %wz_ref.3) | copy-start | bytes 7077892
  27.5 4.5 %copy-start.18 = (f32[2,12]{1,0:T(2,128)S(1)}, f32[2,12]{1,0:T(2,128)}, u32[]{:S(2)}) copy-start(f32[2,12]{1,0:T(2,128)} %param.19) | copy-start | bytes 292
  27.5 19.1 %all-to-all-start.1 = ((bf16[32,104,128]{2,1,0:T(8,128)(2,1)}), bf16[32,104,128]{2,1,0:T(8,128)(2,1)}, u32[]{:S(2)}, u32[]{:S(2)}) async-start(bf16[32,104,128]{2,1,0:T(8,128)(2,1)} %get-tuple-element.31), calls=%async_computation.1 | async-start | bytes 1703936 | tf_op jit(solution)/shard_map/all_to_all | solution.py:350
  31.9 14.6 %copy-start.2 = (bf16[2,768,384]{2,1,0:T(8,128)(2,1)S(1)}, bf16[2,768,384]{2,1,0:T(8,128)(2,1)}, u32[]{:S(2)}) copy-start(bf16[2,768,384]{2,1,0:T(8,128)(2,1)} %wo_ref.3) | copy-start | bytes 3538948
  32.0 14.6 %copy-start.8 = (f32[2,768]{1,0:T(2,128)S(1)}, f32[2,768]{1,0:T(2,128)}, u32[]{:S(2)}) copy-start(f32[2,768]{1,0:T(2,128)} %gain_ref.7) | copy-start | bytes 18436
  46.5 20.3 %copy-start.5 = (bf16[2,48,384]{2,1,0:T(8,128)(2,1)S(1)}, bf16[2,48,384]{2,1,0:T(8,128)(2,1)}, u32[]{:S(2)}) copy-start(bf16[2,48,384]{2,1,0:T(8,128)(2,1)} %copy-done.4) | copy-start | bytes 221188
  46.6 20.3 %copy-start.7 = (f32[2,48,8]{2,1,0:T(8,128)S(1)}, f32[2,48,8]{2,1,0:T(8,128)}, u32[]{:S(2)}) copy-start(f32[2,48,8]{2,1,0:T(8,128)} %copy-done.6) | copy-start | bytes 9220
  46.6 20.3 %copy-start.10 = (f32[2,4,800]{2,1,0:T(4,128)S(1)}, f32[2,4,800]{2,1,0:T(4,128)}, u32[]{:S(2)}) copy-start(f32[2,4,800]{2,1,0:T(4,128)} %cw_ref.3) | copy-start | bytes 76804
  46.6 20.3 %copy-start.12 = (f32[2,800]{1,0:T(2,128)S(1)}, f32[2,800]{1,0:T(2,128)}, u32[]{:S(2)}) copy-start(f32[2,800]{1,0:T(2,128)} %cb_ref.3) | copy-start | bytes 19204
  46.6 20.3 %copy-start.14 = (f32[2,384]{1,0:T(2,128)S(1)}, f32[2,384]{1,0:T(2,128)}, u32[]{:S(2)}) copy-start(f32[2,384]{1,0:T(2,128)} %gain_ref.6) | copy-start | bytes 9220
  71.1 19.0 %all-to-all-start.3 = ((bf16[32,104,128]{2,1,0:T(8,128)(2,1)}), bf16[32,104,128]{2,1,0:T(8,128)(2,1)}, u32[]{:S(2)}, u32[]{:S(2)}) async-start(bf16[32,104,128]{2,1,0:T(8,128)(2,1)} %get-tuple-element.44), calls=%async_computation.3 | async-start | bytes 1703936 | tf_op jit(solution)/shard_map/all_to_all | solution.py:350

commit v3 on v2

--- a/solution.py
+++ b/solution.py
@@ -63,40 +63,68 @@
     return dot(values, jnp.where(mask, 1.0, 0.0), EXACT)
 
 
-def pack_body(tiles_ref, send_ref):
-    halo = jnp.zeros((PEERS, 8, 128), F32)
-    slot = iota((PEERS, 8, 128), 1)
-    for b in range(3):
-        lanes = slice(128 * b, 128 * b + 128)
-        rows = [tiles_ref[r, :, lanes].astype(F32).reshape(PEERS, 8, 128) for r in range(2)]
-        send_ref[:, 16 * b : 16 * b + 16, :] = jnp.concatenate(rows, axis=1).astype(BF)
-        for r in range(2):
-            after = jnp.concatenate([rows[r][1:, 0:1], jnp.zeros((1, 1, 128), F32)], axis=0)
-            halo = jnp.where(slot == 2 * b + r, after, halo)
-    send_ref[:, 48:56, :] = halo.astype(BF)
+def pack_body(tiles_hbm, send_hbm, tiles_ref, send_ref, sems):
+    load = pltpu.make_async_copy(tiles_hbm, tiles_ref, sems.at[0])
+    load.start()
+    load.wait()
+    stores = []
+    part = PEERS // 4
+    slot = iota((part, 8, 128), 1)
+    for q in range(4):
+        halo = jnp.zeros((part, 8, 128), F32)
+        for b in range(3):
+            lanes = slice(128 * b, 128 * b + 128)
+            first = 8 * part * q
+            rows = [
+                tiles_ref[r, first : first + 8 * part, lanes].astype(F32).reshape(part, 8, 128)
+                for r in range(2)
+            ]
+            send_ref[part * q : part * q + part, 16 * b : 16 * b + 16, :] = jnp.concatenate(
+                rows, axis=1
+            ).astype(BF)
+            for r in range(2):
+                if q < 3:
+                    beyond = tiles_ref[r, first + 8 * part : first + 8 * part + 16, lanes]
+                    beyond = beyond.astype(F32)[0:1].reshape(1, 1, 128)
+                else:
+                    beyond = jnp.zeros((1, 1, 128), F32)
+                after = jnp.concatenate([rows[r][1:, 0:1], beyond], axis=0)
+                halo = jnp.where(slot == 2 * b + r, after, halo)
+        send_ref[part * q : part * q + part, 48:56, :] = halo.astype(BF)
+        own = pl.ds(part * q, part)
+        store = pltpu.make_async_copy(send_ref.at[own], send_hbm.at[own], sems.at[1 + q])
+        store.start()
+        stores.append(store)
+    for store in stores:
+        store.wait()
 
 
 def front_body(
     layer,
     recv_ref,
     gain_ref,
-    wx_ref,
+    wx_hbm,
     ws_ref,
     cw_ref,
     cb_ref,
     col_ref,
+    xs_hbm,
+    xc_hbm,
+    rows_hbm,
+    loc_hbm,
+    send_hbm,
+    wx_ref,
+    conv_ref,
     xs_ref,
-    nm_ref,
     xc_ref,
-    bt_ref,
-    cc_ref,
-    cum_ref,
-    rt_ref,
+    rows_ref,
     loc_ref,
-    dec_ref,
-    send_ref,
-    conv_ref,
+    chunk_ref,
+    sems,
+    send_sems,
 ):
+    load = pltpu.make_async_copy(wx_hbm.at[layer, :, pl.ds(INNER, INNER)], wx_ref, sems.at[0])
+    load.start()
     t = iota((TOKENS, 1), 0)
     place = iota((16, 1), 0)
     if layer == 0:
@@ -125,11 +153,13 @@
         halo = dot(one_hot((16, 16), jnp.where(place >= 13, place - 13, -1)), halo_in)
     xs = dot(one_hot((TOKENS, TOKENS), column), main)
     xs_ref[...] = xs.astype(BF)
+    stores = [pltpu.make_async_copy(xs_ref, xs_hbm, sems.at[1])]
+    stores[0].start()
     gain = gain_ref[layer : layer + 1, :]
     normed = rms(xs, gain).astype(BF)
     halo_normed = rms(halo, gain).astype(BF)
-    nm_ref[...] = normed
-    wx = wx_ref[0]
+    load.wait()
+    wx = wx_ref[...]
     conv_ref[8 : 8 + TOKENS, :] = dot(normed, wx).astype(BF).astype(F32)
     conv_ref[0:8, :] = dot(halo_normed, wx).astype(BF).astype(F32)[8:16]
     for block in range(INNER // 128):
@@ -142,6 +172,8 @@
                 5 + tap : 5 + tap + TOKENS, lanes
             ]
         xc_ref[:, lanes] = silu(total).astype(BF)
+    stores.append(pltpu.make_async_copy(xc_ref, xc_hbm, sems.at[2]))
+    stores[1].start()
 
     tall = jnp.concatenate([normed, jnp.zeros((112, D), BF), halo_normed], axis=0)
     proj = dot_rows(ws_ref[layer], tall).astype(BF).astype(F32)
@@ -151,9 +183,7 @@
     for back in range(1, 4):
         bc = bc + col[0:32, 3 - back : 4 - back] * pltpu.roll(bc_in, back, 1)
     bc = silu(bc[:, 0:TOKENS])
-    bt = bc[0:16]
-    bt_ref[...] = bt.astype(BF)
-    cc_ref[...] = bc.T[:, 16:32].astype(BF)
+    rows_ref[0:32, :] = bc.astype(BF).astype(F32)
 
     raw = proj[32:48, 0:TOKENS] + col[32:48, 5:6]
     step = jnp.maximum(raw, 0.0) + jnp.log1p(jnp.exp(-jnp.abs(raw)))
@@ -162,13 +192,16 @@
     cums = [dot(rate[:, g * GROUP : (g + 1) * GROUP], upper, EXACT) for g in range(2)]
     cum_rows = jnp.concatenate(cums, axis=1)
     rt = cum_rows - jnp.log(step)
-    rt_ref[...] = rt
-    cum = cum_rows.T
-    cum_ref[...] = cum
-    totals = jnp.concatenate([cum[255:256], cum[511:512], jnp.zeros((6, 16), F32)], axis=0)
+    rows_ref[32:48, :] = rt
+    rows_ref[48:64, :] = cum_rows
+    stores.append(pltpu.make_async_copy(rows_ref, rows_hbm, sems.at[3]))
+    stores[2].start()
+    ends = [jnp.broadcast_to(c[:, GROUP - 1 : GROUP], (16, 128)) for c in cums]
+    ends = [e.T[0:1] for e in ends]
+    totals = jnp.concatenate([ends[0], ends[1], jnp.zeros((6, 16), F32)], axis=0)
     decays = spread(jnp.exp(totals), HEADDIM)
-    dec_ref[...] = decays
-    bt_held = bt.astype(BF).astype(F32)
+    loc_ref[16:24, :] = decays
+    bt_held = rows_ref[0:16, :]
     head = lax.shift_right_logical(iota((16, INNER), 1), 6)
     locals_ = []
     for g in range(2):
@@ -182,7 +215,9 @@
         for h in range(1, HEADS):
             local = jnp.where(head == h, every[16 * h : 16 * h + 16], local)
         locals_.append(local)
-    loc_ref[...] = locals_[0]
+    loc_ref[0:16, :] = locals_[0]
+    stores.append(pltpu.make_async_copy(loc_ref, loc_hbm, sems.at[4]))
+    stores[3].start()
     final = (decays[1:2] * locals_[0] + locals_[1]).astype(BF)
     total = totals[0:1] + totals[1:2]
     high, low = in_two(total)
@@ -195,18 +230,24 @@
         ],
         axis=0,
     )
-    packed = jnp.concatenate(
+    chunk_ref[...] = jnp.concatenate(
         [final[:, 128 * b : 128 * b + 128].astype(F32) for b in range(6)] + [decay_rows], axis=0
     ).astype(BF)
     for peer in range(PEERS):
-        send_ref[peer] = packed
+        stores.append(pltpu.make_async_copy(chunk_ref, send_hbm.at[peer], send_sems.at[peer]))
+        stores[-1].start()
+    for store in stores:
+        store.wait()
 
 
 def middle_body(
-    layer, nm_ref, wz_ref, xc_ref, bt_ref, cc_ref, cum_ref, rt_ref, skip_ref, z_ref, y_ref, ct_ref
+    layer, xs_ref, gain_ref, wz_ref, xc_ref, rows_ref, skip_ref, z_ref, y_ref, ct_ref, cum_ref
 ):
-    z_ref[...] = dot(nm_ref[...], wz_ref[0]).astype(BF)
-    held = cc_ref[...]
+    normed = rms(xs_ref[...].astype(F32), gain_ref[layer : layer + 1, :]).astype(BF)
+    z_ref[...] = dot(normed, wz_ref[0]).astype(BF)
+    bt_ref = rows_ref[0:16, :].astype(BF)
+    held = rows_ref[0:32, :].T[:, 16:32].astype(BF)
+    cum_ref[...] = rows_ref[48:64, :].T
     mask = jnp.bitwise_and(iota((16, 192), 1), 15) == iota((16, 192), 0)
     repeated = dot(held, jnp.where(mask, 1.0, 0.0).astype(BF))
     ct_ref[...] = (repeated * spread(jnp.exp(cum_ref[...]), STATE)).astype(BF)
@@ -228,8 +269,8 @@
                 h = 2 * pair + which
                 c0 = cum_ref[base : base + half, h : h + 1]
                 c1 = cum_ref[base + half : base + GROUP, h : h + 1]
-                r0 = rt_ref[h : h + 1, base : base + half]
-                r1 = rt_ref[h : h + 1, base + half : base + GROUP]
+                r0 = rows_ref[32 + h : 33 + h, base : base + half]
+                r1 = rows_ref[32 + h : 33 + h, base + half : base + GROUP]
                 top.append((s00 * jnp.exp(jnp.minimum(c0 - r0, 80.0))).astype(BF))
                 low.append((s10 * jnp.exp(c1 - r0)).astype(BF))
                 low.append((s11 * jnp.exp(jnp.minimum(c1 - r1, 80.0))).astype(BF))
@@ -247,16 +288,36 @@
     layer,
     place_ref,
     recv_ref,
+    loc_hbm,
+    ct_hbm,
+    y_hbm,
+    z_hbm,
+    xs_hbm,
+    gain_ref,
+    wo_hbm,
+    out_ref,
     loc_ref,
-    dec_ref,
+    ct_ref,
+    y_ref,
     z_ref,
-    y_ref,
-    ct_ref,
     xs_ref,
-    gain_ref,
     wo_ref,
-    out_ref,
+    sems,
 ):
+    moves = [
+        (loc_hbm, loc_ref),
+        (ct_hbm, ct_ref),
+        (y_hbm, y_ref),
+        (z_hbm, z_ref),
+        (wo_hbm.at[layer], wo_ref),
+        (xs_hbm, xs_ref),
+    ]
+    loads = [
+        pltpu.make_async_copy(source, target, sems.at[k])
+        for k, (source, target) in enumerate(moves)
+    ]
+    for load in loads:
+        load.start()
     place = place_ref[0]
     decays = jnp.sum(recv_ref[:, 96:104, :].astype(F32), axis=1)
     source, between = iota((PEERS, PEERS), 0), iota((PEERS, PEERS), 1)
@@ -280,19 +341,24 @@
             ].astype(F32)
         blocks.append(total)
     start = jnp.concatenate(blocks, axis=1)
-    starts = [start, dec_ref[0:1, :] * start + loc_ref[...]]
+    loads[0].wait()
+    starts = [start, loc_ref[16:17, :] * start + loc_ref[0:16, :]]
     own = lax.shift_right_logical(iota((192, INNER), 1), 6) == lax.shift_right_logical(
         iota((192, INNER), 0), 4
     )
     mixed = []
+    for load in loads[1:4]:
+        load.wait()
     for g in range(2):
         span = slice(g * GROUP, (g + 1) * GROUP)
         wide = jnp.where(own, jnp.concatenate([starts[g]] * HEADS, axis=0), 0.0).astype(BF)
         y = y_ref[span, :] + dot(ct_ref[span, :], wide)
         gated = y * silu(z_ref[span, :].astype(F32))
         mixed.append(rms(gated, gain_ref[layer : layer + 1, :]).astype(BF))
+    for load in loads[4:]:
+        load.wait()
     result = (
-        xs_ref[...].astype(F32) + dot(jnp.concatenate(mixed, axis=0), wo_ref[0])
+        xs_ref[...].astype(F32) + dot(jnp.concatenate(mixed, axis=0), wo_ref[...])
     ).astype(BF)
     if layer == 1:
         out_ref[...] = result
@@ -310,8 +376,8 @@
     )
 
 
-def layer_half(which, axis_size):
-    return pl.BlockSpec((1, D, INNER), lambda *_: (which[0], 0, which[1]))
+ANYWHERE = pl.BlockSpec(memory_space=pl.ANY)
+VMEM = pl.BlockSpec(memory_space=pltpu.VMEM)
 
 
 def shaped(shape, dtype):
@@ -326,71 +392,112 @@
     return tuple(pltpu.with_memory_space_constraint(a, pltpu.HBM) for a in arrays)
 
 
-def whole(a):
-    return pl.BlockSpec(a.shape, lambda *_: (0,) * len(a.shape))
-
-
-def call(body, args, specs, outs, flops, scratch=(), many=True):
+def call(body, args, in_specs, outs, out_specs, scratch, flops, grid=()):
     moved = sum(a.size * a.dtype.itemsize for a in args) + sum(
         math.prod(o.shape) * jnp.dtype(o.dtype).itemsize for o in outs
     )
     return pl.pallas_call(
         body,
-        grid=(1,),
-        out_shape=tuple(outs) if many else outs[0],
-        in_specs=[whole(a) if s is None else s for a, s in zip(args, specs)],
-        out_specs=tuple(whole(o) for o in outs) if many else whole(outs[0]),
-        scratch_shapes=list(scratch),
+        grid=grid,
+        out_shape=tuple(outs),
+        in_specs=in_specs,
+        out_specs=tuple(out_specs),
+        scratch_shapes=scratch,
         compiler_params=pltpu.CompilerParams(vmem_limit_bytes=40 * 1024 * 1024),
         cost_estimate=pl.CostEstimate(flops=flops, bytes_accessed=moved, transcendentals=0),
     )(*args)
 
 
+def whole(shape):
+    return pl.BlockSpec(shape, lambda *_: (0,) * len(shape))
+
+
 def exchange(chunks):
     return lax.all_to_all(chunks, "seq", 0, 0, tiled=True)
 
 
-def run_layer(layer, received, place, params):
-    gain, in_weight, ws, conv_weight, conv_bias, cols, skip, out_gain, out_weight = params
-    fronts = call(
+def front(layer, received, params):
+    gain, in_weight, ws, conv_weight, conv_bias, cols, _, _, _ = params
+    return call(
         functools.partial(front_body, layer),
         (received, gain, in_weight, ws, conv_weight, conv_bias, cols),
-        (None, None, layer_half((layer, 1), 0), None, None, None, None),
+        [VMEM, VMEM, ANYWHERE, VMEM, VMEM, VMEM, VMEM],
         (
             kept((TOKENS, D), BF),
-            kept((TOKENS, D), BF),
             kept((TOKENS, INNER), BF),
-            kept((16, TOKENS), BF),
-            kept((TOKENS, 16), BF),
-            kept((TOKENS, 16), F32),
-            kept((16, TOKENS), F32),
-            kept((16, INNER), F32),
-            kept((8, INNER), F32),
+            kept((64, TOKENS), F32),
+            kept((24, INNER), F32),
             kept((PEERS, STATE_ROWS, 128), BF),
         ),
+        [ANYWHERE] * 5,
+        [
+            pltpu.VMEM((D, INNER), BF),
+            pltpu.VMEM((TOKENS + 8, INNER), F32),
+            pltpu.VMEM((TOKENS, D), BF),
+            pltpu.VMEM((TOKENS, INNER), BF),
+            pltpu.VMEM((64, TOKENS), F32),
+            pltpu.VMEM((24, INNER), F32),
+            pltpu.VMEM((STATE_ROWS, 128), BF),
+            pltpu.SemaphoreType.DMA((5,)),
+            pltpu.SemaphoreType.DMA((PEERS,)),
+        ],
         1_000_000_000,
-        [pltpu.VMEM((TOKENS + 8, INNER), F32)],
-    )
-    xs, normed, xc, bt, cc, cum, rt, local, decays, send = pinned(*fronts)
-    arrived = exchange(send)
-    z, y, ct = pinned(*call(
+    )
+
+
+def middle(layer, xs, xc, rows, params):
+    gain, in_weight, _, _, _, _, skip, _, _ = params
+    outs = (
+        kept((TOKENS, INNER), BF),
+        kept((TOKENS, INNER), F32),
+        kept((TOKENS, 192), BF),
+    )
+    return call(
         functools.partial(middle_body, layer),
-        (normed, in_weight, xc, bt, cc, cum, rt, skip),
-        (None, layer_half((layer, 0), 0)) + (None,) * 6,
-        (
-            kept((TOKENS, INNER), BF),
-            kept((TOKENS, INNER), F32),
-            kept((TOKENS, 192), BF),
-        ),
+        (xs, gain, in_weight, xc, rows, skip),
+        [
+            whole(xs.shape),
+            whole(gain.shape),
+            pl.BlockSpec((1, D, INNER), lambda *_: (layer, 0, 0)),
+            whole(xc.shape),
+            whole(rows.shape),
+            whole(skip.shape),
+        ],
+        outs,
+        [whole(o.shape) for o in outs],
+        [pltpu.VMEM((TOKENS, 16), F32)],
         1_000_000_000,
-    ))
+        (1,),
+    )
+
+
+def finish(layer, place, arrived, local, ct, y, z, xs, params):
+    out_gain, out_weight = params[-2:]
     out = shaped((TOKENS, D), BF) if layer else shaped((PEERS, CHUNK, D), BF)
-    args = (place, arrived, local, decays, z, y, ct, xs, out_gain, out_weight)
-    specs = [pl.BlockSpec(memory_space=pltpu.SMEM)] + [None] * 8
-    specs.append(pl.BlockSpec((1, INNER, D), lambda *_: (layer, 0, 0)))
     return call(
-        functools.partial(finish_body, layer), args, specs, (out,), 1_000_000_000, many=False
-    )
+        functools.partial(finish_body, layer),
+        (place, arrived, local, ct, y, z, xs, out_gain, out_weight),
+        [pl.BlockSpec(memory_space=pltpu.SMEM), VMEM] + [ANYWHERE] * 5 + [VMEM, ANYWHERE],
+        (out,),
+        [VMEM],
+        [
+            pltpu.VMEM((24, INNER), F32),
+            pltpu.VMEM((TOKENS, 192), BF),
+            pltpu.VMEM((TOKENS, INNER), F32),
+            pltpu.VMEM((TOKENS, INNER), BF),
+            pltpu.VMEM((TOKENS, D), BF),
+            pltpu.VMEM((INNER, D), BF),
+            pltpu.SemaphoreType.DMA((6,)),
+        ],
+        1_000_000_000,
+    )[0]
+
+
+def run_layer(layer, received, place, params):
+    xs, xc, rows, local, send = pinned(*front(layer, received, params))
+    arrived = pltpu.with_memory_space_constraint(exchange(send), pltpu.VMEM)
+    z, y, ct = pinned(*middle(layer, xs, xc, rows, params))
+    return finish(layer, place, arrived, local, ct, y, z, xs, params)
 
 
 def on_device(
@@ -420,6 +527,7 @@
     head_cols = jnp.pad(head_cols, ((0, 0), (0, 4), (5, 1)))
     cols = jnp.concatenate([conv_cols, head_cols], axis=1)
     skip = jnp.pad(skip_gain, ((0, 0), (0, 4)))
+    slide_tiles, in_weight, out_weight = pinned(slide_tiles, in_weight, out_weight)
     params = (
         norm_gain,
         in_weight,
@@ -431,16 +539,21 @@
         out_gain,
         out_weight,
     )
-    send = call(
+    (send,) = call(
         pack_body,
         (slide_tiles,),
-        (None,),
+        [ANYWHERE],
         (kept((PEERS, 56, 128), BF),),
+        [ANYWHERE],
+        [
+            pltpu.VMEM(slide_tiles.shape, BF),
+            pltpu.VMEM((PEERS, 56, 128), BF),
+            pltpu.SemaphoreType.DMA((5,)),
+        ],
         1_000_000,
-        many=False,
-    )
-    middle = run_layer(0, exchange(send), place, params)
-    result = run_layer(1, exchange(middle), place, params)
+    )
+    between = run_layer(0, exchange(send), place, params)
+    result = run_layer(1, exchange(between), place, params)
     return result.reshape(slide_tiles.shape)
 
 

time: 95.1 us -> 93 us (0.978)
  local copies, waits for them, and re-layouts: 2.88 us -> 0.17 us
  starting transfers between devices: 17.6 us -> 16.2 us
  Pallas kernels: 27.8 us -> 29.2 us
    unnamed x39 -> x17, local copies, waits for them, and re-layouts: 2.75 us -> 0.05 us
    pallas_call x7, Pallas kernels: 27.8 us -> 29.2 us  [call(): pl.pallas_call(body, grid=grid, out_shape=tuple(outs), in_specs=in_specs,...]
    all_to_all x3, starting transfers between devices: 17.6 us -> 16.2 us  [exchange(): return lax.all_to_all(chunks, 'seq', 0, 0, tiled=True)]
  transfers between devices with their start and end apart: 3 -> 3, of which waited for: 3 -> 3; matrix products, arithmetic and copies ran while one was open for 0% -> 0% of each run, Pallas kernels for 10% -> 11%
where the time goes in v3:
time: 93 us; the launch traced here: 92.4 us
  waiting for transfers between devices  30.4 us (33%)
  Pallas kernels  29.2 us (31%)
  starting transfers between devices  16.2 us (17%)
  blocking collectives  16 us (17%)
    all_to_all x3, waiting for transfers between devices, exchange(): return lax.all_to_all(chunks, 'seq', 0, 0, tiled=True)  30.4 us
    pallas_call x7, Pallas kernels, call(): pl.pallas_call(body, grid=grid, out_shape=tuple(outs), in_specs=in_specs,...  29.2 us
    all_to_all x3, starting transfers between devices, exchange(): return lax.all_to_all(chunks, 'seq', 0, 0, tiled=True)  16.2 us
    all_to_all x1, blocking collectives, exchange(): return lax.all_to_all(chunks, 'seq', 0, 0, tiled=True)  16 us
  transfers between devices with their start and end apart: 3, of which 3 were waited for; matrix products, arithmetic and copies ran while one was open for 0% of the time, Pallas kernels for 11%

profile of v3, /device:TPU:1, one launch (start us, length us, event | category | flops | bytes accessed | tf_op | source)
XLA Modules:
  0.0 92.4 jit_solution(6140532117180605160)
XLA Ops:
  0.0 0.0 copy-start.6
  0.0 0.0 copy-start.5
  0.0 0.0 copy-start.1
  0.0 0.0 copy-start.3
  0.0 1.9 %shard_map.109 = bf16[32,56,128]{2,1,0:T(8,128)(2,1)} custom-call(bf16[2,256,384]{2,1,0:T(8,128)(2,1)} %tiles_hbm.1), custom_call_target="tpu_custom_call" | custom-call | flops 1000000 | bytes 851968 | tf_op jit(solution)/shard_map/pallas_call | solution.py:399
  2.0 8.6 %all-to-all-start = ((bf16[32,56,128]{2,1,0:T(8,128)(2,1)}), bf16[32,56,128]{2,1,0:T(8,128)(2,1)S(1)}, u32[]{:S(2)}, u32[]{:S(2)}) async-start(bf16[32,56,128]{2,1,0:T(8,128)(2,1)} %shard_map.109), calls=%async_computation | async-start | bytes 917504 | tf_op jit(solution)/shard_map/all_to_all | solution.py:416
  10.6 0.0 copy-done.4
  10.7 0.1 pad_maximum_fusion
  10.8 0.1 copy.21.col_ref
  10.9 10.7 %all-to-all-done.recv_ref = bf16[32,56,128]{2,1,0:T(8,128)(2,1)S(1)} async-done(((bf16[32,56,128]{2,1,0:T(8,128)(2,1)}), bf16[32,56,128]{2,1,0:T(8,128)(2,1)S(1)}, u32[]{:S(2)}, u32[]{:S(2)}) %all-to-all-start) | async-done | bytes 458784 | tf_op jit(solution)/shard_map/all_to_all | solution.py:416
  21.5 0.0 copy-done.3
  21.6 4.9 %shard_map.110 = (bf16[512,384]{1,0:T(8,128)(2,1)}, bf16[512,768]{1,0:T(8,128)(2,1)}, f32[64,512]{1,0:T(8,128)}, f32[24,768]{1,0:T(8,128)}, bf16[32,104,128]{2,1,0:T(8,128)(2,1)}) custom-call(bf16[32,56,128]{2,1,0:T(8,128)(2,1)S(1)} %all-to-all-done.recv_ref, f32[2,384]{1,0:T(2,128)S(1)} %copy-done.3, bf16[2,384,1536]{2,1,0:T(8,128)(2,1)} %wz_ref.3, ...), custom_call_target="tpu_custom_call" | custom-call | flops 1000000000 | bytes 5166336 | tf_op jit(solution)/shard_map/pallas_call | solution.py:399
  26.5 0.0 copy-start.7
  26.5 3.7 %all-to-all-start.1 = ((bf16[32,104,128]{2,1,0:T(8,128)(2,1)}), bf16[32,104,128]{2,1,0:T(8,128)(2,1)S(1)}, u32[]{:S(2)}, u32[]{:S(2)}) async-start(bf16[32,104,128]{2,1,0:T(8,128)(2,1)} %get-tuple-element.21), calls=%async_computation.1 | async-start | bytes 1703936 | tf_op jit(solution)/shard_map/all_to_all | solution.py:416
  30.2 0.0 copy-start
  30.3 4.9 %shard_map.111 = (bf16[512,768]{1,0:T(8,128)(2,1)}, f32[512,768]{1,0:T(8,128)}, bf16[512,192]{1,0:T(8,128)(2,1)}) custom-call(bf16[512,384]{1,0:T(8,128)(2,1)} %get-tuple-element.23.xs_ref.xs_hbm, f32[2,384]{1,0:T(2,128)S(1)} %copy-done.3, bf16[2,384,1536]{2,1,0:T(8,128)(2,1)} %wz_ref.3, bf16[512,768]{1,0:T(8,128)(2,1)} %get-tuple-element.24.xc_ref, ...), custom_call_target="tpu_custom_call" | custom-call | flops 1000000000 | bytes 6229120 | tf_op jit(solution)/shard_map/pallas_call | solution.py:399
  35.2 9.8 %all-to-all-done.1.recv_ref = bf16[32,104,128]{2,1,0:T(8,128)(2,1)S(1)} async-done(((bf16[32,104,128]{2,1,0:T(8,128)(2,1)}), bf16[32,104,128]{2,1,0:T(8,128)(2,1)S(1)}, u32[]{:S(2)}, u32[]{:S(2)}) %all-to-all-start.1) | async-done | bytes 852000 | tf_op jit(solution)/shard_map/all_to_all | solution.py:416
  45.0 3.8 %shard_map.112 = bf16[32,24,384]{2,1,0:T(8,128)(2,1)S(1)} custom-call(s32[1]{0:T(128)} %bitcast.place_ref, bf16[32,104,128]{2,1,0:T(8,128)(2,1)S(1)} %all-to-all-done.1.recv_ref, f32[24,768]{1,0:T(8,128)} %get-tuple-element.22.loc_hbm, bf16[512,192]{1,0:T(8,128)(2,1)} %get-tuple-element.26.ct_hbm, f32[512,768]{1,0:T(8,128)} %get-tuple-element.27.y_hbm, ...), custom_call_target="tpu_custom_call" | custom-call | flops 1000000000 | bytes 5650436 | tf_op jit(solution)/shard_map/pallas_call | solution.py:399
  48.7 16.0 %all_to_all.20.recv_ref = bf16[32,24,384]{2,1,0:T(8,128)(2,1)S(1)} all-to-all(bf16[32,24,384]{2,1,0:T(8,128)(2,1)S(1)} %shard_map.112), channel_id=1, replica_groups=mesh['dp'=8,'seq'=32] {'seq'}, dimensions={0} | all-to-all | bytes 1179648 | tf_op jit(solution)/shard_map/all_to_all | solution.py:416
  64.7 4.9 %shard_map.113 = (bf16[512,384]{1,0:T(8,128)(2,1)}, bf16[512,768]{1,0:T(8,128)(2,1)}, f32[64,512]{1,0:T(8,128)}, f32[24,768]{1,0:T(8,128)}, bf16[32,104,128]{2,1,0:T(8,128)(2,1)}) custom-call(bf16[32,24,384]{2,1,0:T(8,128)(2,1)S(1)} %all_to_all.20.recv_ref, f32[2,384]{1,0:T(2,128)S(1)} %copy-done.3, bf16[2,384,1536]{2,1,0:T(8,128)(2,1)} %wz_ref.3, ...), custom_call_target="tpu_custom_call" | custom-call | flops 1000000000 | bytes 5297408 | tf_op jit(solution)/shard_map/pallas_call | solution.py:399
  69.6 3.9 %all-to-all-start.3 = ((bf16[32,104,128]{2,1,0:T(8,128)(2,1)}), bf16[32,104,128]{2,1,0:T(8,128)(2,1)S(1)}, u32[]{:S(2)}, u32[]{:S(2)}) async-start(bf16[32,104,128]{2,1,0:T(8,128)(2,1)} %get-tuple-element.29), calls=%async_computation.3 | async-start | bytes 1703936 | tf_op jit(solution)/shard_map/all_to_all | solution.py:416
  73.5 4.9 %shard_map.114 = (bf16[512,768]{1,0:T(8,128)(2,1)}, f32[512,768]{1,0:T(8,128)}, bf16[512,192]{1,0:T(8,128)(2,1)}) custom-call(bf16[512,384]{1,0:T(8,128)(2,1)} %get-tuple-element.31.xs_ref.xs_hbm, f32[2,384]{1,0:T(2,128)S(1)} %copy-done.3, bf16[2,384,1536]{2,1,0:T(8,128)(2,1)} %wz_ref.3, bf16[512,768]{1,0:T(8,128)(2,1)} %get-tuple-element.32.xc_ref, ...), custom_call_target="tpu_custom_call" | custom-call | flops 1000000000 | bytes 6229120 | tf_op jit(solution)/shard_map/pallas_call | solution.py:399
  78.4 9.9 %all-to-all-done.3.recv_ref = bf16[32,104,128]{2,1,0:T(8,128)(2,1)S(1)} async-done(((bf16[32,104,128]{2,1,0:T(8,128)(2,1)}), bf16[32,104,128]{2,1,0:T(8,128)(2,1)S(1)}, u32[]{:S(2)}, u32[]{:S(2)}) %all-to-all-start.3) | async-done | bytes 852000 | tf_op jit(solution)/shard_map/all_to_all | solution.py:416
  88.3 3.9 %shard_map.115 = bf16[512,384]{1,0:T(8,128)(2,1)} custom-call(s32[1]{0:T(128)} %bitcast.place_ref, bf16[32,104,128]{2,1,0:T(8,128)(2,1)S(1)} %all-to-all-done.3.recv_ref, f32[24,768]{1,0:T(8,128)} %get-tuple-element.30.loc_hbm, bf16[512,192]{1,0:T(8,128)(2,1)} %get-tuple-element.34.ct_hbm, f32[512,768]{1,0:T(8,128)} %get-tuple-element.35.y_hbm, ...), custom_call_target="tpu_custom_call" | custom-call | flops 1000000000 | bytes 5453828 | tf_op jit(solution)/shard_map/pallas_call | solution.py:399
  (17 shorter events, 0.1 us)
Async XLA Ops:
  0.0 10.6 %copy-start.4 = (bf16[2,384,44]{1,0,2:T(2,128)(2,1)S(1)}, bf16[2,384,44]{1,0,2:T(2,128)(2,1)}, u32[]{:S(2)}) copy-start(bf16[2,384,44]{1,0,2:T(2,128)(2,1)} %param.14) | copy-start | bytes 202756
  0.0 10.7 %slice-start = ((f32[2,800]{1,0:T(2,128)}), f32[2,32]{1,0:T(2,128)S(1)}, s32[]{:S(2)}) async-start(f32[2,800]{1,0:T(2,128)} %cb_ref.3), calls=%async_computation.4 | async-start | bytes 2048 | tf_op jit(solution)/shard_map/slice | solution.py:521
  0.0 21.5 %copy-start.2 = (f32[2,800]{1,0:T(2,128)S(1)}, f32[2,800]{1,0:T(2,128)}, u32[]{:S(2)}) copy-start(f32[2,800]{1,0:T(2,128)} %cb_ref.3) | copy-start | bytes 19204
  0.0 10.6 %copy-start.6 = (f32[2,12]{1,0:T(2,128)S(1)}, f32[2,12]{1,0:T(2,128)}, u32[]{:S(2)}) copy-start(f32[2,12]{1,0:T(2,128)} %param.17) | copy-start | bytes 292
  0.0 10.6 %copy-start.5 = (f32[2,12]{1,0:T(2,128)S(1)}, f32[2,12]{1,0:T(2,128)}, u32[]{:S(2)}) copy-start(f32[2,12]{1,0:T(2,128)} %param.18) | copy-start | bytes 292
  0.0 10.6 %copy-start.1 = (f32[2,4,800]{2,1,0:T(4,128)S(1)}, f32[2,4,800]{2,1,0:T(4,128)}, u32[]{:S(2)}) copy-start(f32[2,4,800]{2,1,0:T(4,128)} %cw_ref.3) | copy-start | bytes 76804
  0.0 21.5 %copy-start.3 = (f32[2,384]{1,0:T(2,128)S(1)}, f32[2,384]{1,0:T(2,128)}, u32[]{:S(2)}) copy-start(f32[2,384]{1,0:T(2,128)} %gain_ref.10) | copy-start | bytes 9220
  2.0 19.6 %all-to-all-start = ((bf16[32,56,128]{2,1,0:T(8,128)(2,1)}), bf16[32,56,128]{2,1,0:T(8,128)(2,1)S(1)}, u32[]{:S(2)}, u32[]{:S(2)}) async-start(bf16[32,56,128]{2,1,0:T(8,128)(2,1)} %shard_map.109), calls=%async_computation | async-start | bytes 917504 | tf_op jit(solution)/shard_map/all_to_all | solution.py:416
  26.5 3.7 %copy-start.7 = (f32[2,12]{1,0:T(2,128)S(1)}, f32[2,12]{1,0:T(2,128)}, u32[]{:S(2)}) copy-start(f32[2,12]{1,0:T(2,128)} %param.19) | copy-start | bytes 292
  26.5 18.5 %all-to-all-start.1 = ((bf16[32,104,128]{2,1,0:T(8,128)(2,1)}), bf16[32,104,128]{2,1,0:T(8,128)(2,1)S(1)}, u32[]{:S(2)}, u32[]{:S(2)}) async-start(bf16[32,104,128]{2,1,0:T(8,128)(2,1)} %get-tuple-element.21), calls=%async_computation.1 | async-start | bytes 1703936 | tf_op jit(solution)/shard_map/all_to_all | solution.py:416
  30.2 14.7 %copy-start = (f32[2,768]{1,0:T(2,128)S(1)}, f32[2,768]{1,0:T(2,128)}, u32[]{:S(2)}) copy-start(f32[2,768]{1,0:T(2,128)} %gain_ref.11) | copy-start | bytes 18436
  69.6 18.7 %all-to-all-start.3 = ((bf16[32,104,128]{2,1,0:T(8,128)(2,1)}), bf16[32,104,128]{2,1,0:T(8,128)(2,1)S(1)}, u32[]{:S(2)}, u32[]{:S(2)}) async-start(bf16[32,104,128]{2,1,0:T(8,128)(2,1)} %get-tuple-element.29), calls=%async_computation.3 | async-start | bytes 1703936 | tf_op jit(solution)/shard_map/all_to_all | solution.py:416

commit v4 on v3

--- a/solution.py
+++ b/solution.py
@@ -18,6 +18,7 @@
 PEERS = 32
 CHUNK = 24
 STATE_ROWS = 104
+WIDE = 256
 EPS = 1e-05
 BF = jnp.bfloat16
 F32 = jnp.float32
@@ -99,6 +100,23 @@
         store.wait()
 
 
+def convolve(layer, normed, halo_normed, wx_ref, cw_ref, cb_ref, conv_ref, xc_ref):
+    for first in range(0, INNER, WIDE):
+        lanes = slice(first, first + WIDE)
+        wx = wx_ref[:, lanes]
+        conv_ref[8 : 8 + TOKENS, lanes] = dot(normed, wx).astype(BF).astype(F32)
+        conv_ref[0:8, lanes] = dot(halo_normed, wx).astype(BF).astype(F32)[8:16]
+    for first in range(0, INNER, 128):
+        lanes = slice(first, first + 128)
+        taps = 0.5 * cw_ref[layer, :, lanes]
+        total = 0.5 * cb_ref[layer : layer + 1, lanes] + taps[0:1] * conv_ref[
+            5 : 5 + TOKENS, lanes
+        ]
+        for tap in range(1, 4):
+            total = total + taps[tap : tap + 1] * conv_ref[5 + tap : 5 + tap + TOKENS, lanes]
+        xc_ref[:, lanes] = (total + total * jnp.tanh(total)).astype(BF)
+
+
 def front_body(
     layer,
     recv_ref,
@@ -109,7 +127,6 @@
     cb_ref,
     col_ref,
     xs_hbm,
-    xc_hbm,
     rows_hbm,
     loc_hbm,
     send_hbm,
@@ -120,6 +137,7 @@
     rows_ref,
     loc_ref,
     chunk_ref,
+    all_ref,
     sems,
     send_sems,
 ):
@@ -152,29 +170,15 @@
         ).astype(BF)
         halo = dot(one_hot((16, 16), jnp.where(place >= 13, place - 13, -1)), halo_in)
     xs = dot(one_hot((TOKENS, TOKENS), column), main)
-    xs_ref[...] = xs.astype(BF)
-    stores = [pltpu.make_async_copy(xs_ref, xs_hbm, sems.at[1])]
-    stores[0].start()
+    xs_ref[0:TOKENS, :] = xs.astype(BF)
+    xs_ref[TOKENS : TOKENS + 16, :] = halo.astype(BF)
     gain = gain_ref[layer : layer + 1, :]
     normed = rms(xs, gain).astype(BF)
     halo_normed = rms(halo, gain).astype(BF)
     load.wait()
-    wx = wx_ref[...]
-    conv_ref[8 : 8 + TOKENS, :] = dot(normed, wx).astype(BF).astype(F32)
-    conv_ref[0:8, :] = dot(halo_normed, wx).astype(BF).astype(F32)[8:16]
-    for block in range(INNER // 128):
-        lanes = slice(128 * block, 128 * block + 128)
-        total = cb_ref[layer : layer + 1, lanes] + cw_ref[layer, 0:1, lanes] * conv_ref[
-            5 : 5 + TOKENS, lanes
-        ]
-        for tap in range(1, 4):
-            total = total + cw_ref[layer, tap : tap + 1, lanes] * conv_ref[
-                5 + tap : 5 + tap + TOKENS, lanes
-            ]
-        xc_ref[:, lanes] = silu(total).astype(BF)
-    stores.append(pltpu.make_async_copy(xc_ref, xc_hbm, sems.at[2]))
-    stores[1].start()
-
+    stores = [pltpu.make_async_copy(xs_ref, xs_hbm, sems.at[1])]
+    stores[0].start()
+    convolve(layer, normed, halo_normed, wx_ref, cw_ref, cb_ref, conv_ref, xc_ref)
     tall = jnp.concatenate([normed, jnp.zeros((112, D), BF), halo_normed], axis=0)
     proj = dot_rows(ws_ref[layer], tall).astype(BF).astype(F32)
     col = col_ref[layer]
@@ -182,9 +186,7 @@
     bc = col[0:32, 4:5] + col[0:32, 3:4] * bc_in
     for back in range(1, 4):
         bc = bc + col[0:32, 3 - back : 4 - back] * pltpu.roll(bc_in, back, 1)
-    bc = silu(bc[:, 0:TOKENS])
-    rows_ref[0:32, :] = bc.astype(BF).astype(F32)
-
+    rows_ref[0:32, :] = silu(bc[:, 0:TOKENS]).astype(BF).astype(F32)
     raw = proj[32:48, 0:TOKENS] + col[32:48, 5:6]
     step = jnp.maximum(raw, 0.0) + jnp.log1p(jnp.exp(-jnp.abs(raw)))
     rate = -step * jnp.exp(col[32:48, 6:7])
@@ -194,35 +196,21 @@
     rt = cum_rows - jnp.log(step)
     rows_ref[32:48, :] = rt
     rows_ref[48:64, :] = cum_rows
-    stores.append(pltpu.make_async_copy(rows_ref, rows_hbm, sems.at[3]))
-    stores[2].start()
     ends = [jnp.broadcast_to(c[:, GROUP - 1 : GROUP], (16, 128)) for c in cums]
     ends = [e.T[0:1] for e in ends]
     totals = jnp.concatenate([ends[0], ends[1], jnp.zeros((6, 16), F32)], axis=0)
     decays = spread(jnp.exp(totals), HEADDIM)
     loc_ref[16:24, :] = decays
-    bt_held = rows_ref[0:16, :]
-    head = lax.shift_right_logical(iota((16, INNER), 1), 6)
-    locals_ = []
+    tilted = []
     for g in range(2):
         span = slice(g * GROUP, (g + 1) * GROUP)
         tail = jnp.exp(cums[g][:, GROUP - 1 : GROUP] - rt[:, span])
-        tilted = jnp.concatenate(
-            [bt_held[:, span] * tail[h : h + 1, :] for h in range(HEADS)], axis=0
-        ).astype(BF)
-        every = dot(tilted, xc_ref[span, :])
-        local = every[0:16]
-        for h in range(1, HEADS):
-            local = jnp.where(head == h, every[16 * h : 16 * h + 16], local)
-        locals_.append(local)
-    loc_ref[0:16, :] = locals_[0]
-    stores.append(pltpu.make_async_copy(loc_ref, loc_hbm, sems.at[4]))
-    stores[3].start()
-    final = (decays[1:2] * locals_[0] + locals_[1]).astype(BF)
+        bt = rows_ref[0:16, span]
+        tilted.append([(bt * tail[h : h + 1, :]).astype(BF) for h in range(HEADS)])
     total = totals[0:1] + totals[1:2]
     high, low = in_two(total)
     pad = jnp.zeros((1, 112), F32)
-    decay_rows = jnp.concatenate(
+    chunk_ref[96:104, :] = jnp.concatenate(
         [
             jnp.concatenate([high.astype(F32), pad], axis=1),
             jnp.concatenate([low.astype(F32), pad], axis=1),
@@ -230,21 +218,62 @@
         ],
         axis=0,
     )
-    chunk_ref[...] = jnp.concatenate(
-        [final[:, 128 * b : 128 * b + 128].astype(F32) for b in range(6)] + [decay_rows], axis=0
-    ).astype(BF)
-    for peer in range(PEERS):
-        stores.append(pltpu.make_async_copy(chunk_ref, send_hbm.at[peer], send_sems.at[peer]))
+
+    head = lax.shift_right_logical(iota((16, WIDE), 1), 6)
+    for q in range(INNER // WIDE):
+        lanes = slice(WIDE * q, WIDE * q + WIDE)
+        heads = WIDE // HEADDIM
+        found = []
+        for g in range(2):
+            every = dot(
+                jnp.concatenate(tilted[g][heads * q : heads * q + heads], axis=0),
+                xc_ref[g * GROUP : (g + 1) * GROUP, lanes],
+            )
+            local = every[0:16]
+            for h in range(1, heads):
+                local = jnp.where(head == h, every[16 * h : 16 * h + 16], local)
+            found.append(local)
+        loc_ref[0:16, lanes] = found[0]
+        final = decays[1:2, lanes] * found[0] + found[1]
+        for b in range(WIDE // 128):
+            slot = 16 * (WIDE // 128 * q + b)
+            chunk_ref[slot : slot + 16, :] = final[:, 128 * b : 128 * b + 128]
+    packed = chunk_ref[...].astype(BF)
+    for peer in range(8):
+        all_ref[peer] = packed
+    for part in range(4):
+        target = send_hbm.at[pl.ds(8 * part, 8)]
+        stores.append(pltpu.make_async_copy(all_ref, target, send_sems.at[part]))
+        stores[-1].start()
+    late = ((rows_ref, rows_hbm), (loc_ref, loc_hbm))
+    for k, (source, target) in enumerate(late):
+        stores.append(pltpu.make_async_copy(source, target, sems.at[2 + k]))
         stores[-1].start()
     for store in stores:
         store.wait()
 
 
 def middle_body(
-    layer, xs_ref, gain_ref, wz_ref, xc_ref, rows_ref, skip_ref, z_ref, y_ref, ct_ref, cum_ref
+    layer,
+    xs_ref,
+    gain_ref,
+    w_ref,
+    cw_ref,
+    cb_ref,
+    rows_ref,
+    skip_ref,
+    z_ref,
+    y_ref,
+    ct_ref,
+    cum_ref,
+    conv_ref,
+    xc_ref,
 ):
-    normed = rms(xs_ref[...].astype(F32), gain_ref[layer : layer + 1, :]).astype(BF)
-    z_ref[...] = dot(normed, wz_ref[0]).astype(BF)
+    every = rms(xs_ref[...].astype(F32), gain_ref[layer : layer + 1, :]).astype(BF)
+    normed, halo_normed = every[0:TOKENS], every[TOKENS : TOKENS + 16]
+    wx_ref = w_ref.at[0, :, pl.ds(INNER, INNER)]
+    convolve(layer, normed, halo_normed, wx_ref, cw_ref, cb_ref, conv_ref, xc_ref)
+    z_ref[...] = dot(normed, w_ref[0, :, 0:INNER]).astype(BF)
     bt_ref = rows_ref[0:16, :].astype(BF)
     held = rows_ref[0:32, :].T[:, 16:32].astype(BF)
     cum_ref[...] = rows_ref[48:64, :].T
@@ -310,7 +339,7 @@
         (y_hbm, y_ref),
         (z_hbm, z_ref),
         (wo_hbm.at[layer], wo_ref),
-        (xs_hbm, xs_ref),
+        (xs_hbm.at[pl.ds(0, TOKENS)], xs_ref),
     ]
     loads = [
         pltpu.make_async_copy(source, target, sems.at[k])
@@ -423,49 +452,49 @@
         (received, gain, in_weight, ws, conv_weight, conv_bias, cols),
         [VMEM, VMEM, ANYWHERE, VMEM, VMEM, VMEM, VMEM],
         (
-            kept((TOKENS, D), BF),
-            kept((TOKENS, INNER), BF),
+            kept((TOKENS + 16, D), BF),
             kept((64, TOKENS), F32),
             kept((24, INNER), F32),
             kept((PEERS, STATE_ROWS, 128), BF),
         ),
-        [ANYWHERE] * 5,
+        [ANYWHERE] * 4,
         [
             pltpu.VMEM((D, INNER), BF),
             pltpu.VMEM((TOKENS + 8, INNER), F32),
-            pltpu.VMEM((TOKENS, D), BF),
+            pltpu.VMEM((TOKENS + 16, D), BF),
             pltpu.VMEM((TOKENS, INNER), BF),
             pltpu.VMEM((64, TOKENS), F32),
             pltpu.VMEM((24, INNER), F32),
-            pltpu.VMEM((STATE_ROWS, 128), BF),
-            pltpu.SemaphoreType.DMA((5,)),
-            pltpu.SemaphoreType.DMA((PEERS,)),
+            pltpu.VMEM((STATE_ROWS, 128), F32),
+            pltpu.VMEM((8, STATE_ROWS, 128), BF),
+            pltpu.SemaphoreType.DMA((4,)),
+            pltpu.SemaphoreType.DMA((4,)),
         ],
         1_000_000_000,
     )
 
 
-def middle(layer, xs, xc, rows, params):
-    gain, in_weight, _, _, _, _, skip, _, _ = params
+def middle(layer, xs, rows, params):
+    gain, in_weight, _, conv_weight, conv_bias, _, skip, _, _ = params
     outs = (
         kept((TOKENS, INNER), BF),
         kept((TOKENS, INNER), F32),
         kept((TOKENS, 192), BF),
     )
+    args = (xs, gain, in_weight, conv_weight, conv_bias, rows, skip)
+    specs = [whole(a.shape) for a in args]
+    specs[2] = pl.BlockSpec((1, D, 2 * INNER), lambda *_: (layer, 0, 0))
     return call(
         functools.partial(middle_body, layer),
-        (xs, gain, in_weight, xc, rows, skip),
-        [
-            whole(xs.shape),
-            whole(gain.shape),
-            pl.BlockSpec((1, D, INNER), lambda *_: (layer, 0, 0)),
-            whole(xc.shape),
-            whole(rows.shape),
-            whole(skip.shape),
-        ],
+        args,
+        specs,
         outs,
         [whole(o.shape) for o in outs],
-        [pltpu.VMEM((TOKENS, 16), F32)],
+        [
+            pltpu.VMEM((TOKENS, 16), F32),
+            pltpu.VMEM((TOKENS + 8, INNER), F32),
+            pltpu.VMEM((TOKENS, INNER), BF),
+        ],
         1_000_000_000,
         (1,),
     )
@@ -494,9 +523,9 @@
 
 
 def run_layer(layer, received, place, params):
-    xs, xc, rows, local, send = pinned(*front(layer, received, params))
+    xs, rows, local, send = pinned(*front(layer, received, params))
     arrived = pltpu.with_memory_space_constraint(exchange(send), pltpu.VMEM)
-    z, y, ct = pinned(*middle(layer, xs, xc, rows, params))
+    z, y, ct = pinned(*middle(layer, xs, rows, params))
     return finish(layer, place, arrived, local, ct, y, z, xs, params)
 
 

time: 93 us -> 91.7 us (0.986)
  waiting for transfers between devices: 30.4 us -> 27.8 us
  Pallas kernels: 29.2 us -> 30.7 us
    all_to_all x3, waiting for transfers between devices: 30.4 us -> 27.8 us  [exchange(): return lax.all_to_all(chunks, 'seq', 0, 0, tiled=True)]
    pallas_call x7, Pallas kernels: 29.2 us -> 30.7 us  [call(): pl.pallas_call(body, grid=grid, out_shape=tuple(outs), in_specs=in_specs,...]
  transfers between devices with their start and end apart: 3 -> 3, of which waited for: 3 -> 3; matrix products, arithmetic and copies ran while one was open for 0% -> 0% of each run, Pallas kernels for 11% -> 14%
where the time goes in v4:
time: 91.7 us; the launch traced here: 91.1 us
  Pallas kernels  30.7 us (33%)
  waiting for transfers between devices  27.8 us (30%)
  starting transfers between devices  16 us (17%)
  blocking collectives  16 us (17%)
    pallas_call x7, Pallas kernels, call(): pl.pallas_call(body, grid=grid, out_shape=tuple(outs), in_specs=in_specs,...  30.7 us
    all_to_all x3, waiting for transfers between devices, exchange(): return lax.all_to_all(chunks, 'seq', 0, 0, tiled=True)  27.8 us
    all_to_all x3, starting transfers between devices, exchange(): return lax.all_to_all(chunks, 'seq', 0, 0, tiled=True)  16 us
    all_to_all x1, blocking collectives, exchange(): return lax.all_to_all(chunks, 'seq', 0, 0, tiled=True)  16 us
  transfers between devices with their start and end apart: 3, of which 3 were waited for; matrix products, arithmetic and copies ran while one was open for 0% of the time, Pallas kernels for 14%

profile of v4, /device:TPU:1, one launch (start us, length us, event | category | flops | bytes accessed | tf_op | source)
XLA Modules:
  0.0 91.1 jit_solution(17325941537114098322)
XLA Ops:
  0.0 0.0 copy-start.6
  0.0 0.0 copy-start.1
  0.0 0.0 copy-start.4
  0.0 0.0 copy-start.3
  0.0 1.9 %shard_map.109 = bf16[32,56,128]{2,1,0:T(8,128)(2,1)} custom-call(bf16[2,256,384]{2,1,0:T(8,128)(2,1)} %tiles_hbm.1), custom_call_target="tpu_custom_call" | custom-call | flops 1000000 | bytes 851968 | tf_op jit(solution)/shard_map/pallas_call | solution.py:428
  2.0 8.6 %all-to-all-start = ((bf16[32,56,128]{2,1,0:T(8,128)(2,1)}), bf16[32,56,128]{2,1,0:T(8,128)(2,1)S(1)}, u32[]{:S(2)}, u32[]{:S(2)}) async-start(bf16[32,56,128]{2,1,0:T(8,128)(2,1)} %shard_map.109), calls=%async_computation | async-start | bytes 917504 | tf_op jit(solution)/shard_map/all_to_all | solution.py:445
  10.7 0.1 pad_maximum_fusion
  10.7 0.1 copy.21.col_ref
  10.9 10.7 %all-to-all-done.recv_ref = bf16[32,56,128]{2,1,0:T(8,128)(2,1)S(1)} async-done(((bf16[32,56,128]{2,1,0:T(8,128)(2,1)}), bf16[32,56,128]{2,1,0:T(8,128)(2,1)S(1)}, u32[]{:S(2)}, u32[]{:S(2)}) %all-to-all-start) | async-done | bytes 458784 | tf_op jit(solution)/shard_map/all_to_all | solution.py:445
  21.5 0.0 copy-done.2
  21.5 4.4 %shard_map.110 = (bf16[528,384]{1,0:T(8,128)(2,1)}, f32[64,512]{1,0:T(8,128)}, f32[24,768]{1,0:T(8,128)}, bf16[32,104,128]{2,1,0:T(8,128)(2,1)}) custom-call(bf16[32,56,128]{2,1,0:T(8,128)(2,1)S(1)} %all-to-all-done.recv_ref, f32[2,384]{1,0:T(2,128)S(1)} %copy-done.3, bf16[2,384,1536]{2,1,0:T(8,128)(2,1)} %w_ref.3, bf16[2,48,384]{2,1,0:T(8,128)(2,1)S(1)} %pad.12.ws_ref, ...), custom_call_target="tpu_custom_call" | custom-call | flops 1000000000 | bytes 4392192 | tf_op jit(solution)/shard_map/pallas_call | solution.py:428
  25.9 0.0 copy-start.7
  25.9 3.7 %all-to-all-start.1 = ((bf16[32,104,128]{2,1,0:T(8,128)(2,1)}), bf16[32,104,128]{2,1,0:T(8,128)(2,1)S(1)}, u32[]{:S(2)}, u32[]{:S(2)}) async-start(bf16[32,104,128]{2,1,0:T(8,128)(2,1)} %get-tuple-element.19), calls=%async_computation.1 | async-start | bytes 1703936 | tf_op jit(solution)/shard_map/all_to_all | solution.py:445
  29.7 0.0 copy-done.7
  29.7 0.0 copy-start
  29.7 6.2 %shard_map.111 = (bf16[512,768]{1,0:T(8,128)(2,1)}, f32[512,768]{1,0:T(8,128)}, bf16[512,192]{1,0:T(8,128)(2,1)}) custom-call(bf16[528,384]{1,0:T(8,128)(2,1)} %get-tuple-element.21.xs_ref.xs_hbm, f32[2,384]{1,0:T(2,128)S(1)} %copy-done.3, bf16[2,384,1536]{2,1,0:T(8,128)(2,1)} %w_ref.3, f32[2,4,800]{2,1,0:T(4,128)S(1)} %copy-done.1, f32[2,800]{1,0:T(2,128)S(1)} %copy-done.2, ...), custom_call_target="tpu_custom_call" | custom-call | flops 1000000000 | bytes 5486976 | tf_op jit(solution)/shard_map/pallas_call | solution.py:428
  35.9 8.5 %all-to-all-done.1.recv_ref = bf16[32,104,128]{2,1,0:T(8,128)(2,1)S(1)} async-done(((bf16[32,104,128]{2,1,0:T(8,128)(2,1)}), bf16[32,104,128]{2,1,0:T(8,128)(2,1)S(1)}, u32[]{:S(2)}, u32[]{:S(2)}) %all-to-all-start.1) | async-done | bytes 852000 | tf_op jit(solution)/shard_map/all_to_all | solution.py:445
  44.4 3.8 %shard_map.112 = bf16[32,24,384]{2,1,0:T(8,128)(2,1)S(1)} custom-call(s32[1]{0:T(128)} %bitcast.place_ref, bf16[32,104,128]{2,1,0:T(8,128)(2,1)S(1)} %all-to-all-done.1.recv_ref, f32[24,768]{1,0:T(8,128)} %get-tuple-element.20.loc_hbm, bf16[512,192]{1,0:T(8,128)(2,1)} %get-tuple-element.23.ct_hbm, f32[512,768]{1,0:T(8,128)} %get-tuple-element.24.y_hbm, ...), custom_call_target="tpu_custom_call" | custom-call | flops 1000000000 | bytes 5662724 | tf_op jit(solution)/shard_map/pallas_call | solution.py:428
  48.2 16.0 %all_to_all.20.recv_ref = bf16[32,24,384]{2,1,0:T(8,128)(2,1)S(1)} all-to-all(bf16[32,24,384]{2,1,0:T(8,128)(2,1)S(1)} %shard_map.112), channel_id=1, replica_groups=mesh['dp'=8,'seq'=32] {'seq'}, dimensions={0} | all-to-all | bytes 1179648 | tf_op jit(solution)/shard_map/all_to_all | solution.py:445
  64.2 4.3 %shard_map.113 = (bf16[528,384]{1,0:T(8,128)(2,1)}, f32[64,512]{1,0:T(8,128)}, f32[24,768]{1,0:T(8,128)}, bf16[32,104,128]{2,1,0:T(8,128)(2,1)}) custom-call(bf16[32,24,384]{2,1,0:T(8,128)(2,1)S(1)} %all_to_all.20.recv_ref, f32[2,384]{1,0:T(2,128)S(1)} %copy-done.3, bf16[2,384,1536]{2,1,0:T(8,128)(2,1)} %w_ref.3, bf16[2,48,384]{2,1,0:T(8,128)(2,1)S(1)} %pad.12.ws_ref, ...), custom_call_target="tpu_custom_call" | custom-call | flops 1000000000 | bytes 4523264 | tf_op jit(solution)/shard_map/pallas_call | solution.py:428
  68.5 3.7 %all-to-all-start.3 = ((bf16[32,104,128]{2,1,0:T(8,128)(2,1)}), bf16[32,104,128]{2,1,0:T(8,128)(2,1)S(1)}, u32[]{:S(2)}, u32[]{:S(2)}) async-start(bf16[32,104,128]{2,1,0:T(8,128)(2,1)} %get-tuple-element.26), calls=%async_computation.3 | async-start | bytes 1703936 | tf_op jit(solution)/shard_map/all_to_all | solution.py:445
  72.2 6.2 %shard_map.114 = (bf16[512,768]{1,0:T(8,128)(2,1)}, f32[512,768]{1,0:T(8,128)}, bf16[512,192]{1,0:T(8,128)(2,1)}) custom-call(bf16[528,384]{1,0:T(8,128)(2,1)} %get-tuple-element.28.xs_ref.xs_hbm, f32[2,384]{1,0:T(2,128)S(1)} %copy-done.3, bf16[2,384,1536]{2,1,0:T(8,128)(2,1)} %w_ref.3, f32[2,4,800]{2,1,0:T(4,128)S(1)} %copy-done.1, f32[2,800]{1,0:T(2,128)S(1)} %copy-done.2, ...), custom_call_target="tpu_custom_call" | custom-call | flops 1000000000 | bytes 5486976 | tf_op jit(solution)/shard_map/pallas_call | solution.py:428
  78.4 8.6 %all-to-all-done.3.recv_ref = bf16[32,104,128]{2,1,0:T(8,128)(2,1)S(1)} async-done(((bf16[32,104,128]{2,1,0:T(8,128)(2,1)}), bf16[32,104,128]{2,1,0:T(8,128)(2,1)S(1)}, u32[]{:S(2)}, u32[]{:S(2)}) %all-to-all-start.3) | async-done | bytes 852000 | tf_op jit(solution)/shard_map/all_to_all | solution.py:445
  87.0 3.9 %shard_map.115 = bf16[512,384]{1,0:T(8,128)(2,1)} custom-call(s32[1]{0:T(128)} %bitcast.place_ref, bf16[32,104,128]{2,1,0:T(8,128)(2,1)S(1)} %all-to-all-done.3.recv_ref, f32[24,768]{1,0:T(8,128)} %get-tuple-element.27.loc_hbm, bf16[512,192]{1,0:T(8,128)(2,1)} %get-tuple-element.30.ct_hbm, f32[512,768]{1,0:T(8,128)} %get-tuple-element.31.y_hbm, ...), custom_call_target="tpu_custom_call" | custom-call | flops 1000000000 | bytes 5466116 | tf_op jit(solution)/shard_map/pallas_call | solution.py:428
  (17 shorter events, 0.1 us)
Async XLA Ops:
  0.0 10.7 %slice-start = ((f32[2,800]{1,0:T(2,128)}), f32[2,32]{1,0:T(2,128)S(1)}, s32[]{:S(2)}) async-start(f32[2,800]{1,0:T(2,128)} %cb_ref.7), calls=%async_computation.4 | async-start | bytes 2048 | tf_op jit(solution)/shard_map/slice | solution.py:550
  0.0 21.5 %copy-start.2 = (f32[2,800]{1,0:T(2,128)S(1)}, f32[2,800]{1,0:T(2,128)}, u32[]{:S(2)}) copy-start(f32[2,800]{1,0:T(2,128)} %cb_ref.7) | copy-start | bytes 19204
  0.0 10.6 %copy-start.5 = (f32[2,12]{1,0:T(2,128)S(1)}, f32[2,12]{1,0:T(2,128)}, u32[]{:S(2)}) copy-start(f32[2,12]{1,0:T(2,128)} %param.18) | copy-start | bytes 292
  0.0 10.6 %copy-start.6 = (f32[2,12]{1,0:T(2,128)S(1)}, f32[2,12]{1,0:T(2,128)}, u32[]{:S(2)}) copy-start(f32[2,12]{1,0:T(2,128)} %param.17) | copy-start | bytes 292
  0.0 10.6 %copy-start.1 = (f32[2,4,800]{2,1,0:T(4,128)S(1)}, f32[2,4,800]{2,1,0:T(4,128)}, u32[]{:S(2)}) copy-start(f32[2,4,800]{2,1,0:T(4,128)} %cw_ref.7) | copy-start | bytes 76804
  0.0 10.8 %copy-start.4 = (bf16[2,384,44]{1,0,2:T(2,128)(2,1)S(1)}, bf16[2,384,44]{1,0,2:T(2,128)(2,1)}, u32[]{:S(2)}) copy-start(bf16[2,384,44]{1,0,2:T(2,128)(2,1)} %param.14) | copy-start | bytes 202756
  0.0 21.5 %copy-start.3 = (f32[2,384]{1,0:T(2,128)S(1)}, f32[2,384]{1,0:T(2,128)}, u32[]{:S(2)}) copy-start(f32[2,384]{1,0:T(2,128)} %gain_ref.10) | copy-start | bytes 9220
  2.0 19.6 %all-to-all-start = ((bf16[32,56,128]{2,1,0:T(8,128)(2,1)}), bf16[32,56,128]{2,1,0:T(8,128)(2,1)S(1)}, u32[]{:S(2)}, u32[]{:S(2)}) async-start(bf16[32,56,128]{2,1,0:T(8,128)(2,1)} %shard_map.109), calls=%async_computation | async-start | bytes 917504 | tf_op jit(solution)/shard_map/all_to_all | solution.py:445
  25.9 3.7 %copy-start.7 = (f32[2,12]{1,0:T(2,128)S(1)}, f32[2,12]{1,0:T(2,128)}, u32[]{:S(2)}) copy-start(f32[2,12]{1,0:T(2,128)} %param.19) | copy-start | bytes 292
  25.9 18.5 %all-to-all-start.1 = ((bf16[32,104,128]{2,1,0:T(8,128)(2,1)}), bf16[32,104,128]{2,1,0:T(8,128)(2,1)S(1)}, u32[]{:S(2)}, u32[]{:S(2)}) async-start(bf16[32,104,128]{2,1,0:T(8,128)(2,1)} %get-tuple-element.19), calls=%async_computation.1 | async-start | bytes 1703936 | tf_op jit(solution)/shard_map/all_to_all | solution.py:445
  29.7 14.7 %copy-start = (f32[2,768]{1,0:T(2,128)S(1)}, f32[2,768]{1,0:T(2,128)}, u32[]{:S(2)}) copy-start(f32[2,768]{1,0:T(2,128)} %gain_ref.11) | copy-start | bytes 18436
  68.5 18.5 %all-to-all-start.3 = ((bf16[32,104,128]{2,1,0:T(8,128)(2,1)}), bf16[32,104,128]{2,1,0:T(8,128)(2,1)S(1)}, u32[]{:S(2)}, u32[]{:S(2)}) async-start(bf16[32,104,128]{2,1,0:T(8,128)(2,1)} %get-tuple-element.26), calls=%async_computation.3 | async-start | bytes 1703936 | tf_op jit(solution)/shard_map/all_to_all | solution.py:445

commit v5 on v4

--- a/solution.py
+++ b/solution.py
@@ -65,13 +65,19 @@
 
 
 def pack_body(tiles_hbm, send_hbm, tiles_ref, send_ref, sems):
-    load = pltpu.make_async_copy(tiles_hbm, tiles_ref, sems.at[0])
-    load.start()
-    load.wait()
+    part = PEERS // 4
+    loads = []
+    for q in range(4):
+        own = pl.ds(8 * part * q, 8 * part)
+        loads.append(
+            pltpu.make_async_copy(tiles_hbm.at[:, own], tiles_ref.at[:, own], sems.at[4 + q])
+        )
+    for load in loads[::-1]:
+        load.start()
     stores = []
-    part = PEERS // 4
     slot = iota((part, 8, 128), 1)
-    for q in range(4):
+    for q in (3, 2, 1, 0):
+        loads[q].wait()
         halo = jnp.zeros((part, 8, 128), F32)
         for b in range(3):
             lanes = slice(128 * b, 128 * b + 128)
@@ -93,7 +99,7 @@
                 halo = jnp.where(slot == 2 * b + r, after, halo)
         send_ref[part * q : part * q + part, 48:56, :] = halo.astype(BF)
         own = pl.ds(part * q, part)
-        store = pltpu.make_async_copy(send_ref.at[own], send_hbm.at[own], sems.at[1 + q])
+        store = pltpu.make_async_copy(send_ref.at[own], send_hbm.at[own], sems.at[q])
         store.start()
         stores.append(store)
     for store in stores:
@@ -333,14 +339,11 @@
     wo_ref,
     sems,
 ):
-    moves = [
-        (loc_hbm, loc_ref),
-        (ct_hbm, ct_ref),
-        (y_hbm, y_ref),
-        (z_hbm, z_ref),
-        (wo_hbm.at[layer], wo_ref),
-        (xs_hbm.at[pl.ds(0, TOKENS)], xs_ref),
-    ]
+    spans = [pl.ds(0, GROUP), pl.ds(GROUP, GROUP)]
+    moves = [(loc_hbm, loc_ref), (ct_hbm, ct_ref)]
+    moves += [(y_hbm.at[spans[0]], y_ref.at[spans[0]]), (z_hbm.at[spans[0]], z_ref.at[spans[0]])]
+    moves += [(wo_hbm.at[layer], wo_ref), (xs_hbm.at[pl.ds(0, TOKENS)], xs_ref)]
+    moves += [(y_hbm.at[spans[1]], y_ref.at[spans[1]]), (z_hbm.at[spans[1]], z_ref.at[spans[1]])]
     loads = [
         pltpu.make_async_copy(source, target, sems.at[k])
         for k, (source, target) in enumerate(moves)
@@ -375,34 +378,31 @@
     own = lax.shift_right_logical(iota((192, INNER), 1), 6) == lax.shift_right_logical(
         iota((192, INNER), 0), 4
     )
-    mixed = []
-    for load in loads[1:4]:
-        load.wait()
-    for g in range(2):
-        span = slice(g * GROUP, (g + 1) * GROUP)
-        wide = jnp.where(own, jnp.concatenate([starts[g]] * HEADS, axis=0), 0.0).astype(BF)
-        y = y_ref[span, :] + dot(ct_ref[span, :], wide)
-        gated = y * silu(z_ref[span, :].astype(F32))
-        mixed.append(rms(gated, gain_ref[layer : layer + 1, :]).astype(BF))
-    for load in loads[4:]:
-        load.wait()
-    result = (
-        xs_ref[...].astype(F32) + dot(jnp.concatenate(mixed, axis=0), wo_ref[...])
-    ).astype(BF)
-    if layer == 1:
-        out_ref[...] = result
-        return
     row = iota((PEERS * CHUNK, 1), 0)
     peer = lax.shift_right_logical(row * 2731, 16)
     slot = row - CHUNK * peer
     token = (7 - jnp.bitwise_and(slot, 7)) * 64 + 63 - 2 * peer - lax.shift_right_logical(slot, 3)
     edge = (18 - slot) * 64 + 64 - 2 * peer
     token = jnp.where(slot < 16, token, jnp.where((slot < 19) & (peer > 0), edge, -1))
-    out_ref[...] = (
-        dot(one_hot((PEERS * CHUNK, TOKENS), token), result)
-        .reshape(PEERS, CHUNK, D)
-        .astype(BF)
-    )
+    gain = gain_ref[layer : layer + 1, :]
+    results = []
+    for g in range(2):
+        span = slice(g * GROUP, (g + 1) * GROUP)
+        for load in loads[6:] if g else loads[1:6]:
+            load.wait()
+        wide = jnp.where(own, jnp.concatenate([starts[g]] * HEADS, axis=0), 0.0).astype(BF)
+        y = y_ref[span, :] + dot(ct_ref[span, :], wide)
+        gated = y * silu(z_ref[span, :].astype(F32))
+        mixed = rms(gated, gain).astype(BF)
+        result = (xs_ref[span, :].astype(F32) + dot(mixed, wo_ref[...])).astype(BF)
+        if layer == 1:
+            out_ref[span, :] = result
+        results.append(result)
+    if layer == 0:
+        out_ref[...] = (
+            dot(one_hot((PEERS * CHUNK, GROUP), token), results[0])
+            + dot(one_hot((PEERS * CHUNK, GROUP), token - GROUP), results[1])
+        ).reshape(PEERS, CHUNK, D).astype(BF)
 
 
 ANYWHERE = pl.BlockSpec(memory_space=pl.ANY)
@@ -516,7 +516,7 @@
             pltpu.VMEM((TOKENS, INNER), BF),
             pltpu.VMEM((TOKENS, D), BF),
             pltpu.VMEM((INNER, D), BF),
-            pltpu.SemaphoreType.DMA((6,)),
+            pltpu.SemaphoreType.DMA((8,)),
         ],
         1_000_000_000,
     )[0]
@@ -577,7 +577,7 @@
         [
             pltpu.VMEM(slide_tiles.shape, BF),
             pltpu.VMEM((PEERS, 56, 128), BF),
-            pltpu.SemaphoreType.DMA((5,)),
+            pltpu.SemaphoreType.DMA((8,)),
         ],
         1_000_000,
     )

time: 91.7 us -> 91.6 us (level)
  no operation moved by 1% of the time
where the time goes in v5:
time: 91.6 us; the launch traced here: 91 us
  Pallas kernels  30.6 us (33%)
  waiting for transfers between devices  27.8 us (30%)
  starting transfers between devices  16 us (17%)
  blocking collectives  16 us (17%)
    pallas_call x7, Pallas kernels, call(): pl.pallas_call(body, grid=grid, out_shape=tuple(outs), in_specs=in_specs,...  30.6 us
    all_to_all x3, waiting for transfers between devices, exchange(): return lax.all_to_all(chunks, 'seq', 0, 0, tiled=True)  27.8 us
    all_to_all x3, starting transfers between devices, exchange(): return lax.all_to_all(chunks, 'seq', 0, 0, tiled=True)  16 us
    all_to_all x1, blocking collectives, exchange(): return lax.all_to_all(chunks, 'seq', 0, 0, tiled=True)  16 us
  transfers between devices with their start and end apart: 3, of which 3 were waited for; matrix products, arithmetic and copies ran while one was open for 0% of the time, Pallas kernels for 14%

profile of v5, /device:TPU:1, one launch (start us, length us, event | category | flops | bytes accessed | tf_op | source)
XLA Modules:
  0.0 91.0 jit_solution(15780598032062232279)
XLA Ops:
  0.0 0.0 copy-start.6
  0.0 0.0 copy-start.1
  0.0 0.0 copy-start.4
  0.0 1.9 %shard_map.109 = bf16[32,56,128]{2,1,0:T(8,128)(2,1)} custom-call(bf16[2,256,384]{2,1,0:T(8,128)(2,1)} %tiles_hbm.1), custom_call_target="tpu_custom_call" | custom-call | flops 1000000 | bytes 851968 | tf_op jit(solution)/shard_map/pallas_call | solution.py:428
  1.9 8.6 %all-to-all-start = ((bf16[32,56,128]{2,1,0:T(8,128)(2,1)}), bf16[32,56,128]{2,1,0:T(8,128)(2,1)S(1)}, u32[]{:S(2)}, u32[]{:S(2)}) async-start(bf16[32,56,128]{2,1,0:T(8,128)(2,1)} %shard_map.109), calls=%async_computation | async-start | bytes 917504 | tf_op jit(solution)/shard_map/all_to_all | solution.py:445
  10.5 0.0 copy-done.5
  10.6 0.0 copy-done.6
  10.6 0.1 pad_maximum_fusion
  10.7 0.1 copy.21.col_ref
  10.8 10.7 %all-to-all-done.recv_ref = bf16[32,56,128]{2,1,0:T(8,128)(2,1)S(1)} async-done(((bf16[32,56,128]{2,1,0:T(8,128)(2,1)}), bf16[32,56,128]{2,1,0:T(8,128)(2,1)S(1)}, u32[]{:S(2)}, u32[]{:S(2)}) %all-to-all-start) | async-done | bytes 458784 | tf_op jit(solution)/shard_map/all_to_all | solution.py:445
  21.5 4.4 %shard_map.110 = (bf16[528,384]{1,0:T(8,128)(2,1)}, f32[64,512]{1,0:T(8,128)}, f32[24,768]{1,0:T(8,128)}, bf16[32,104,128]{2,1,0:T(8,128)(2,1)}) custom-call(bf16[32,56,128]{2,1,0:T(8,128)(2,1)S(1)} %all-to-all-done.recv_ref, f32[2,384]{1,0:T(2,128)S(1)} %copy-done.3, bf16[2,384,1536]{2,1,0:T(8,128)(2,1)} %w_ref.3, bf16[2,48,384]{2,1,0:T(8,128)(2,1)S(1)} %pad.12.ws_ref, ...), custom_call_target="tpu_custom_call" | custom-call | flops 1000000000 | bytes 4392192 | tf_op jit(solution)/shard_map/pallas_call | solution.py:428
  25.9 0.0 copy-start.7
  25.9 3.7 %all-to-all-start.1 = ((bf16[32,104,128]{2,1,0:T(8,128)(2,1)}), bf16[32,104,128]{2,1,0:T(8,128)(2,1)S(1)}, u32[]{:S(2)}, u32[]{:S(2)}) async-start(bf16[32,104,128]{2,1,0:T(8,128)(2,1)} %get-tuple-element.19), calls=%async_computation.1 | async-start | bytes 1703936 | tf_op jit(solution)/shard_map/all_to_all | solution.py:445
  29.6 0.0 copy-done.7
  29.6 0.0 copy-start
  29.6 6.2 %shard_map.111 = (bf16[512,768]{1,0:T(8,128)(2,1)}, f32[512,768]{1,0:T(8,128)}, bf16[512,192]{1,0:T(8,128)(2,1)}) custom-call(bf16[528,384]{1,0:T(8,128)(2,1)} %get-tuple-element.21.xs_ref.xs_hbm, f32[2,384]{1,0:T(2,128)S(1)} %copy-done.3, bf16[2,384,1536]{2,1,0:T(8,128)(2,1)} %w_ref.3, f32[2,4,800]{2,1,0:T(4,128)S(1)} %copy-done.1, f32[2,800]{1,0:T(2,128)S(1)} %copy-done.2, ...), custom_call_target="tpu_custom_call" | custom-call | flops 1000000000 | bytes 5486976 | tf_op jit(solution)/shard_map/pallas_call | solution.py:428
  35.8 8.5 %all-to-all-done.1.recv_ref = bf16[32,104,128]{2,1,0:T(8,128)(2,1)S(1)} async-done(((bf16[32,104,128]{2,1,0:T(8,128)(2,1)}), bf16[32,104,128]{2,1,0:T(8,128)(2,1)S(1)}, u32[]{:S(2)}, u32[]{:S(2)}) %all-to-all-start.1) | async-done | bytes 852000 | tf_op jit(solution)/shard_map/all_to_all | solution.py:445
  44.3 3.7 %shard_map.112 = bf16[32,24,384]{2,1,0:T(8,128)(2,1)S(1)} custom-call(s32[1]{0:T(128)} %bitcast.place_ref, bf16[32,104,128]{2,1,0:T(8,128)(2,1)S(1)} %all-to-all-done.1.recv_ref, f32[24,768]{1,0:T(8,128)} %get-tuple-element.20.loc_hbm, bf16[512,192]{1,0:T(8,128)(2,1)} %get-tuple-element.23.ct_hbm, f32[512,768]{1,0:T(8,128)} %get-tuple-element.24.y_hbm, ...), custom_call_target="tpu_custom_call" | custom-call | flops 1000000000 | bytes 5662724 | tf_op jit(solution)/shard_map/pallas_call | solution.py:428
  48.1 16.0 %all_to_all.20.recv_ref = bf16[32,24,384]{2,1,0:T(8,128)(2,1)S(1)} all-to-all(bf16[32,24,384]{2,1,0:T(8,128)(2,1)S(1)} %shard_map.112), channel_id=1, replica_groups=mesh['dp'=8,'seq'=32] {'seq'}, dimensions={0} | all-to-all | bytes 1179648 | tf_op jit(solution)/shard_map/all_to_all | solution.py:445
  64.0 4.3 %shard_map.113 = (bf16[528,384]{1,0:T(8,128)(2,1)}, f32[64,512]{1,0:T(8,128)}, f32[24,768]{1,0:T(8,128)}, bf16[32,104,128]{2,1,0:T(8,128)(2,1)}) custom-call(bf16[32,24,384]{2,1,0:T(8,128)(2,1)S(1)} %all_to_all.20.recv_ref, f32[2,384]{1,0:T(2,128)S(1)} %copy-done.3, bf16[2,384,1536]{2,1,0:T(8,128)(2,1)} %w_ref.3, bf16[2,48,384]{2,1,0:T(8,128)(2,1)S(1)} %pad.12.ws_ref, ...), custom_call_target="tpu_custom_call" | custom-call | flops 1000000000 | bytes 4523264 | tf_op jit(solution)/shard_map/pallas_call | solution.py:428
  68.4 3.7 %all-to-all-start.3 = ((bf16[32,104,128]{2,1,0:T(8,128)(2,1)}), bf16[32,104,128]{2,1,0:T(8,128)(2,1)S(1)}, u32[]{:S(2)}, u32[]{:S(2)}) async-start(bf16[32,104,128]{2,1,0:T(8,128)(2,1)} %get-tuple-element.26), calls=%async_computation.3 | async-start | bytes 1703936 | tf_op jit(solution)/shard_map/all_to_all | solution.py:445
  72.1 6.2 %shard_map.114 = (bf16[512,768]{1,0:T(8,128)(2,1)}, f32[512,768]{1,0:T(8,128)}, bf16[512,192]{1,0:T(8,128)(2,1)}) custom-call(bf16[528,384]{1,0:T(8,128)(2,1)} %get-tuple-element.28.xs_ref.xs_hbm, f32[2,384]{1,0:T(2,128)S(1)} %copy-done.3, bf16[2,384,1536]{2,1,0:T(8,128)(2,1)} %w_ref.3, f32[2,4,800]{2,1,0:T(4,128)S(1)} %copy-done.1, f32[2,800]{1,0:T(2,128)S(1)} %copy-done.2, ...), custom_call_target="tpu_custom_call" | custom-call | flops 1000000000 | bytes 5486976 | tf_op jit(solution)/shard_map/pallas_call | solution.py:428
  78.3 8.6 %all-to-all-done.3.recv_ref = bf16[32,104,128]{2,1,0:T(8,128)(2,1)S(1)} async-done(((bf16[32,104,128]{2,1,0:T(8,128)(2,1)}), bf16[32,104,128]{2,1,0:T(8,128)(2,1)S(1)}, u32[]{:S(2)}, u32[]{:S(2)}) %all-to-all-start.3) | async-done | bytes 852000 | tf_op jit(solution)/shard_map/all_to_all | solution.py:445
  86.9 3.9 %shard_map.115 = bf16[512,384]{1,0:T(8,128)(2,1)} custom-call(s32[1]{0:T(128)} %bitcast.place_ref, bf16[32,104,128]{2,1,0:T(8,128)(2,1)S(1)} %all-to-all-done.3.recv_ref, f32[24,768]{1,0:T(8,128)} %get-tuple-element.27.loc_hbm, bf16[512,192]{1,0:T(8,128)(2,1)} %get-tuple-element.30.ct_hbm, f32[512,768]{1,0:T(8,128)} %get-tuple-element.31.y_hbm, ...), custom_call_target="tpu_custom_call" | custom-call | flops 1000000000 | bytes 5466116 | tf_op jit(solution)/shard_map/pallas_call | solution.py:428
  (17 shorter events, 0.1 us)
Async XLA Ops:
  0.0 10.6 %slice-start = ((f32[2,800]{1,0:T(2,128)}), f32[2,32]{1,0:T(2,128)S(1)}, s32[]{:S(2)}) async-start(f32[2,800]{1,0:T(2,128)} %cb_ref.7), calls=%async_computation.4 | async-start | bytes 2048 | tf_op jit(solution)/shard_map/slice | solution.py:550
  0.0 21.5 %copy-start.2 = (f32[2,800]{1,0:T(2,128)S(1)}, f32[2,800]{1,0:T(2,128)}, u32[]{:S(2)}) copy-start(f32[2,800]{1,0:T(2,128)} %cb_ref.7) | copy-start | bytes 19204
  0.0 10.5 %copy-start.5 = (f32[2,12]{1,0:T(2,128)S(1)}, f32[2,12]{1,0:T(2,128)}, u32[]{:S(2)}) copy-start(f32[2,12]{1,0:T(2,128)} %param.18) | copy-start | bytes 292
  0.0 10.5 %copy-start.6 = (f32[2,12]{1,0:T(2,128)S(1)}, f32[2,12]{1,0:T(2,128)}, u32[]{:S(2)}) copy-start(f32[2,12]{1,0:T(2,128)} %param.17) | copy-start | bytes 292
  0.0 10.6 %copy-start.1 = (f32[2,4,800]{2,1,0:T(4,128)S(1)}, f32[2,4,800]{2,1,0:T(4,128)}, u32[]{:S(2)}) copy-start(f32[2,4,800]{2,1,0:T(4,128)} %cw_ref.7) | copy-start | bytes 76804
  0.0 10.8 %copy-start.4 = (bf16[2,384,44]{1,0,2:T(2,128)(2,1)S(1)}, bf16[2,384,44]{1,0,2:T(2,128)(2,1)}, u32[]{:S(2)}) copy-start(bf16[2,384,44]{1,0,2:T(2,128)(2,1)} %param.14) | copy-start | bytes 202756
  0.0 21.4 %copy-start.3 = (f32[2,384]{1,0:T(2,128)S(1)}, f32[2,384]{1,0:T(2,128)}, u32[]{:S(2)}) copy-start(f32[2,384]{1,0:T(2,128)} %gain_ref.10) | copy-start | bytes 9220
  1.9 19.6 %all-to-all-start = ((bf16[32,56,128]{2,1,0:T(8,128)(2,1)}), bf16[32,56,128]{2,1,0:T(8,128)(2,1)S(1)}, u32[]{:S(2)}, u32[]{:S(2)}) async-start(bf16[32,56,128]{2,1,0:T(8,128)(2,1)} %shard_map.109), calls=%async_computation | async-start | bytes 917504 | tf_op jit(solution)/shard_map/all_to_all | solution.py:445
  25.9 3.7 %copy-start.7 = (f32[2,12]{1,0:T(2,128)S(1)}, f32[2,12]{1,0:T(2,128)}, u32[]{:S(2)}) copy-start(f32[2,12]{1,0:T(2,128)} %param.19) | copy-start | bytes 292
  25.9 18.5 %all-to-all-start.1 = ((bf16[32,104,128]{2,1,0:T(8,128)(2,1)}), bf16[32,104,128]{2,1,0:T(8,128)(2,1)S(1)}, u32[]{:S(2)}, u32[]{:S(2)}) async-start(bf16[32,104,128]{2,1,0:T(8,128)(2,1)} %get-tuple-element.19), calls=%async_computation.1 | async-start | bytes 1703936 | tf_op jit(solution)/shard_map/all_to_all | solution.py:445
  29.6 14.7 %copy-start = (f32[2,768]{1,0:T(2,128)S(1)}, f32[2,768]{1,0:T(2,128)}, u32[]{:S(2)}) copy-start(f32[2,768]{1,0:T(2,128)} %gain_ref.11) | copy-start | bytes 18436
  68.4 18.5 %all-to-all-start.3 = ((bf16[32,104,128]{2,1,0:T(8,128)(2,1)}), bf16[32,104,128]{2,1,0:T(8,128)(2,1)S(1)}, u32[]{:S(2)}, u32[]{:S(2)}) async-start(bf16[32,104,128]{2,1,0:T(8,128)(2,1)} %get-tuple-element.26), calls=%async_computation.3 | async-start | bytes 1703936 | tf_op jit(solution)/shard_map/all_to_all | solution.py:445

commit v6 on v5

--- a/solution.py
+++ b/solution.py
@@ -16,7 +16,7 @@
 GROUP = 256
 TOKENS = 512
 PEERS = 32
-CHUNK = 24
+CHUNK = 64
 STATE_ROWS = 104
 WIDE = 256
 EPS = 1e-05
@@ -165,17 +165,19 @@
         halo = jnp.concatenate(
             [dot(one_hot((16, 16), picked + 2 * b), halo_in) for b in range(3)], axis=1
         )
+        xs = dot(one_hot((TOKENS, TOKENS), column), main)
     else:
-        main = recv_ref[:, 0:16, :].reshape(TOKENS, D)
-        low = jnp.bitwise_and(t, 7)
-        column = (
-            2 * (jnp.bitwise_and(t, 255) - low) + 8 * lax.shift_right_logical(t, 8) + low
-        )
-        halo_in = jnp.concatenate(
-            [recv_ref[PEERS - 1, 16:24, :].astype(F32), jnp.zeros((8, D), F32)], axis=0
-        ).astype(BF)
-        halo = dot(one_hot((16, 16), jnp.where(place >= 13, place - 13, -1)), halo_in)
-    xs = dot(one_hot((TOKENS, TOKENS), column), main)
+        parts = [recv_ref[:, 16 * b : 16 * b + 16, :].astype(F32) for b in range(3)]
+        parts = [p.reshape(PEERS, 2, 8, 128) for p in parts]
+        xs = jnp.concatenate(
+            [jnp.concatenate([p[:, r].reshape(256, 128) for p in parts], axis=1) for r in range(2)],
+            axis=0,
+        )
+        halo_in = recv_ref[PEERS - 1, 48:64, :]
+        picked = jnp.where(place >= 13, place - 13, -16)
+        halo = jnp.concatenate(
+            [dot(one_hot((16, 16), picked + 3 * b), halo_in) for b in range(3)], axis=1
+        )
     xs_ref[0:TOKENS, :] = xs.astype(BF)
     xs_ref[TOKENS : TOKENS + 16, :] = halo.astype(BF)
     gain = gain_ref[layer : layer + 1, :]
@@ -378,12 +380,6 @@
     own = lax.shift_right_logical(iota((192, INNER), 1), 6) == lax.shift_right_logical(
         iota((192, INNER), 0), 4
     )
-    row = iota((PEERS * CHUNK, 1), 0)
-    peer = lax.shift_right_logical(row * 2731, 16)
-    slot = row - CHUNK * peer
-    token = (7 - jnp.bitwise_and(slot, 7)) * 64 + 63 - 2 * peer - lax.shift_right_logical(slot, 3)
-    edge = (18 - slot) * 64 + 64 - 2 * peer
-    token = jnp.where(slot < 16, token, jnp.where((slot < 19) & (peer > 0), edge, -1))
     gain = gain_ref[layer : layer + 1, :]
     results = []
     for g in range(2):
@@ -399,10 +395,22 @@
             out_ref[span, :] = result
         results.append(result)
     if layer == 0:
-        out_ref[...] = (
-            dot(one_hot((PEERS * CHUNK, GROUP), token), results[0])
-            + dot(one_hot((PEERS * CHUNK, GROUP), token - GROUP), results[1])
-        ).reshape(PEERS, CHUNK, D).astype(BF)
+        row = iota((TOKENS, 1), 0)
+        peer, slot = lax.shift_right_logical(row, 4), jnp.bitwise_and(row, 15)
+        token = (
+            (7 - jnp.bitwise_and(slot, 7)) * 64 + 63 - 2 * peer - lax.shift_right_logical(slot, 3)
+        )
+        moved = dot(one_hot((TOKENS, GROUP), token), results[0]) + dot(
+            one_hot((TOKENS, GROUP), token - GROUP), results[1]
+        )
+        block = lax.shift_right_logical(slot * 11, 5)
+        edge = GROUP * block + (2 - slot + 3 * block) * 64 + 64 - 2 * peer
+        edge = jnp.where((slot < 9) & (peer > 0), edge, -1)
+        lanes = [slice(128 * b, 128 * b + 128) for b in range(3)]
+        stacked = jnp.concatenate([results[0][:, own] for own in lanes], axis=0)
+        edges = dot(one_hot((TOKENS, 3 * GROUP), edge), stacked)
+        for b, part in enumerate([moved[:, own] for own in lanes] + [edges]):
+            out_ref[:, 16 * b : 16 * b + 16, :] = part.reshape(PEERS, 16, 128).astype(BF)
 
 
 ANYWHERE = pl.BlockSpec(memory_space=pl.ANY)
@@ -502,7 +510,7 @@
 
 def finish(layer, place, arrived, local, ct, y, z, xs, params):
     out_gain, out_weight = params[-2:]
-    out = shaped((TOKENS, D), BF) if layer else shaped((PEERS, CHUNK, D), BF)
+    out = shaped((TOKENS, D), BF) if layer else shaped((PEERS, CHUNK, 128), BF)
     return call(
         functools.partial(finish_body, layer),
         (place, arrived, local, ct, y, z, xs, out_gain, out_weight),

time: 91.6 us -> 91 us (level)
  no operation moved by 1% of the time
where the time goes in v6:
time: 91 us; the launch traced here: 90.4 us
  Pallas kernels  30.7 us (34%)
  waiting for transfers between devices  27.7 us (30%)
  starting transfers between devices  16 us (18%)
  blocking collectives  15.3 us (17%)
    pallas_call x7, Pallas kernels, call(): pl.pallas_call(body, grid=grid, out_shape=tuple(outs), in_specs=in_specs,...  30.7 us
    all_to_all x3, waiting for transfers between devices, exchange(): return lax.all_to_all(chunks, 'seq', 0, 0, tiled=True)  27.7 us
    all_to_all x3, starting transfers between devices, exchange(): return lax.all_to_all(chunks, 'seq', 0, 0, tiled=True)  16 us
    all_to_all x1, blocking collectives, exchange(): return lax.all_to_all(chunks, 'seq', 0, 0, tiled=True)  15.3 us
  transfers between devices with their start and end apart: 3, of which 3 were waited for; matrix products, arithmetic and copies ran while one was open for 0% of the time, Pallas kernels for 14%

profile of v6, /device:TPU:1, one launch (start us, length us, event | category | flops | bytes accessed | tf_op | source)
XLA Modules:
  0.0 90.4 jit_solution(15846411415634754879)
XLA Ops:
  0.0 0.0 copy-start.6
  0.0 0.0 copy-start.1
  0.0 0.0 copy-start.4
  0.0 0.0 copy-start.3
  0.0 1.9 %shard_map.109 = bf16[32,56,128]{2,1,0:T(8,128)(2,1)} custom-call(bf16[2,256,384]{2,1,0:T(8,128)(2,1)} %tiles_hbm.1), custom_call_target="tpu_custom_call" | custom-call | flops 1000000 | bytes 851968 | tf_op jit(solution)/shard_map/pallas_call | solution.py:436
  1.9 8.6 %all-to-all-start = ((bf16[32,56,128]{2,1,0:T(8,128)(2,1)}), bf16[32,56,128]{2,1,0:T(8,128)(2,1)S(1)}, u32[]{:S(2)}, u32[]{:S(2)}) async-start(bf16[32,56,128]{2,1,0:T(8,128)(2,1)} %shard_map.109), calls=%async_computation | async-start | bytes 917504 | tf_op jit(solution)/shard_map/all_to_all | solution.py:453
  10.6 0.1 pad_maximum_fusion
  10.7 0.1 copy.21.col_ref
  10.8 10.7 %all-to-all-done.recv_ref = bf16[32,56,128]{2,1,0:T(8,128)(2,1)S(1)} async-done(((bf16[32,56,128]{2,1,0:T(8,128)(2,1)}), bf16[32,56,128]{2,1,0:T(8,128)(2,1)S(1)}, u32[]{:S(2)}, u32[]{:S(2)}) %all-to-all-start) | async-done | bytes 458784 | tf_op jit(solution)/shard_map/all_to_all | solution.py:453
  21.5 0.0 copy-done.2
  21.5 4.4 %shard_map.110 = (bf16[528,384]{1,0:T(8,128)(2,1)}, f32[64,512]{1,0:T(8,128)}, f32[24,768]{1,0:T(8,128)}, bf16[32,104,128]{2,1,0:T(8,128)(2,1)}) custom-call(bf16[32,56,128]{2,1,0:T(8,128)(2,1)S(1)} %all-to-all-done.recv_ref, f32[2,384]{1,0:T(2,128)S(1)} %copy-done.3, bf16[2,384,1536]{2,1,0:T(8,128)(2,1)} %w_ref.3, bf16[2,48,384]{2,1,0:T(8,128)(2,1)S(1)} %pad.12.ws_ref, ...), custom_call_target="tpu_custom_call" | custom-call | flops 1000000000 | bytes 4392192 | tf_op jit(solution)/shard_map/pallas_call | solution.py:436
  25.9 0.0 copy-start.7
  25.9 3.7 %all-to-all-start.1 = ((bf16[32,104,128]{2,1,0:T(8,128)(2,1)}), bf16[32,104,128]{2,1,0:T(8,128)(2,1)S(1)}, u32[]{:S(2)}, u32[]{:S(2)}) async-start(bf16[32,104,128]{2,1,0:T(8,128)(2,1)} %get-tuple-element.19), calls=%async_computation.1 | async-start | bytes 1703936 | tf_op jit(solution)/shard_map/all_to_all | solution.py:453
  29.6 0.0 copy-start
  29.6 6.2 %shard_map.111 = (bf16[512,768]{1,0:T(8,128)(2,1)}, f32[512,768]{1,0:T(8,128)}, bf16[512,192]{1,0:T(8,128)(2,1)}) custom-call(bf16[528,384]{1,0:T(8,128)(2,1)} %get-tuple-element.21.xs_ref.xs_hbm, f32[2,384]{1,0:T(2,128)S(1)} %copy-done.3, bf16[2,384,1536]{2,1,0:T(8,128)(2,1)} %w_ref.3, f32[2,4,800]{2,1,0:T(4,128)S(1)} %copy-done.1, f32[2,800]{1,0:T(2,128)S(1)} %copy-done.2, ...), custom_call_target="tpu_custom_call" | custom-call | flops 1000000000 | bytes 5486976 | tf_op jit(solution)/shard_map/pallas_call | solution.py:436
  35.8 8.5 %all-to-all-done.1.recv_ref = bf16[32,104,128]{2,1,0:T(8,128)(2,1)S(1)} async-done(((bf16[32,104,128]{2,1,0:T(8,128)(2,1)}), bf16[32,104,128]{2,1,0:T(8,128)(2,1)S(1)}, u32[]{:S(2)}, u32[]{:S(2)}) %all-to-all-start.1) | async-done | bytes 852000 | tf_op jit(solution)/shard_map/all_to_all | solution.py:453
  44.3 0.0 copy-done
  44.3 3.8 %shard_map.112 = bf16[32,64,128]{2,1,0:T(8,128)(2,1)S(1)} custom-call(s32[1]{0:T(128)} %bitcast.place_ref, bf16[32,104,128]{2,1,0:T(8,128)(2,1)S(1)} %all-to-all-done.1.recv_ref, f32[24,768]{1,0:T(8,128)} %get-tuple-element.20.loc_hbm, bf16[512,192]{1,0:T(8,128)(2,1)} %get-tuple-element.23.ct_hbm, f32[512,768]{1,0:T(8,128)} %get-tuple-element.24.y_hbm, ...), custom_call_target="tpu_custom_call" | custom-call | flops 1000000000 | bytes 5597188 | tf_op jit(solution)/shard_map/pallas_call | solution.py:436
  48.2 15.3 %all_to_all.20.recv_ref = bf16[32,64,128]{2,1,0:T(8,128)(2,1)S(1)} all-to-all(bf16[32,64,128]{2,1,0:T(8,128)(2,1)S(1)} %shard_map.112), channel_id=1, replica_groups=mesh['dp'=8,'seq'=32] {'seq'}, dimensions={0} | all-to-all | bytes 1048576 | tf_op jit(solution)/shard_map/all_to_all | solution.py:453
  63.5 4.3 %shard_map.113 = (bf16[528,384]{1,0:T(8,128)(2,1)}, f32[64,512]{1,0:T(8,128)}, f32[24,768]{1,0:T(8,128)}, bf16[32,104,128]{2,1,0:T(8,128)(2,1)}) custom-call(bf16[32,64,128]{2,1,0:T(8,128)(2,1)S(1)} %all_to_all.20.recv_ref, f32[2,384]{1,0:T(2,128)S(1)} %copy-done.3, bf16[2,384,1536]{2,1,0:T(8,128)(2,1)} %w_ref.3, bf16[2,48,384]{2,1,0:T(8,128)(2,1)S(1)} %pad.12.ws_ref, ...), custom_call_target="tpu_custom_call" | custom-call | flops 1000000000 | bytes 4457728 | tf_op jit(solution)/shard_map/pallas_call | solution.py:436
  67.8 3.7 %all-to-all-start.3 = ((bf16[32,104,128]{2,1,0:T(8,128)(2,1)}), bf16[32,104,128]{2,1,0:T(8,128)(2,1)S(1)}, u32[]{:S(2)}, u32[]{:S(2)}) async-start(bf16[32,104,128]{2,1,0:T(8,128)(2,1)} %get-tuple-element.26), calls=%async_computation.3 | async-start | bytes 1703936 | tf_op jit(solution)/shard_map/all_to_all | solution.py:453
  71.5 6.2 %shard_map.114 = (bf16[512,768]{1,0:T(8,128)(2,1)}, f32[512,768]{1,0:T(8,128)}, bf16[512,192]{1,0:T(8,128)(2,1)}) custom-call(bf16[528,384]{1,0:T(8,128)(2,1)} %get-tuple-element.28.xs_ref.xs_hbm, f32[2,384]{1,0:T(2,128)S(1)} %copy-done.3, bf16[2,384,1536]{2,1,0:T(8,128)(2,1)} %w_ref.3, f32[2,4,800]{2,1,0:T(4,128)S(1)} %copy-done.1, f32[2,800]{1,0:T(2,128)S(1)} %copy-done.2, ...), custom_call_target="tpu_custom_call" | custom-call | flops 1000000000 | bytes 5486976 | tf_op jit(solution)/shard_map/pallas_call | solution.py:436
  77.8 8.6 %all-to-all-done.3.recv_ref = bf16[32,104,128]{2,1,0:T(8,128)(2,1)S(1)} async-done(((bf16[32,104,128]{2,1,0:T(8,128)(2,1)}), bf16[32,104,128]{2,1,0:T(8,128)(2,1)S(1)}, u32[]{:S(2)}, u32[]{:S(2)}) %all-to-all-start.3) | async-done | bytes 852000 | tf_op jit(solution)/shard_map/all_to_all | solution.py:453
  86.3 3.9 %shard_map.115 = bf16[512,384]{1,0:T(8,128)(2,1)} custom-call(s32[1]{0:T(128)} %bitcast.place_ref, bf16[32,104,128]{2,1,0:T(8,128)(2,1)S(1)} %all-to-all-done.3.recv_ref, f32[24,768]{1,0:T(8,128)} %get-tuple-element.27.loc_hbm, bf16[512,192]{1,0:T(8,128)(2,1)} %get-tuple-element.30.ct_hbm, f32[512,768]{1,0:T(8,128)} %get-tuple-element.31.y_hbm, ...), custom_call_target="tpu_custom_call" | custom-call | flops 1000000000 | bytes 5466116 | tf_op jit(solution)/shard_map/pallas_call | solution.py:436
  (17 shorter events, 0.1 us)
Async XLA Ops:
  0.0 10.6 %slice-start = ((f32[2,800]{1,0:T(2,128)}), f32[2,32]{1,0:T(2,128)S(1)}, s32[]{:S(2)}) async-start(f32[2,800]{1,0:T(2,128)} %cb_ref.7), calls=%async_computation.4 | async-start | bytes 2048 | tf_op jit(solution)/shard_map/slice | solution.py:558
  0.0 21.5 %copy-start.2 = (f32[2,800]{1,0:T(2,128)S(1)}, f32[2,800]{1,0:T(2,128)}, u32[]{:S(2)}) copy-start(f32[2,800]{1,0:T(2,128)} %cb_ref.7) | copy-start | bytes 19204
  0.0 10.5 %copy-start.5 = (f32[2,12]{1,0:T(2,128)S(1)}, f32[2,12]{1,0:T(2,128)}, u32[]{:S(2)}) copy-start(f32[2,12]{1,0:T(2,128)} %param.18) | copy-start | bytes 292
  0.0 10.5 %copy-start.6 = (f32[2,12]{1,0:T(2,128)S(1)}, f32[2,12]{1,0:T(2,128)}, u32[]{:S(2)}) copy-start(f32[2,12]{1,0:T(2,128)} %param.17) | copy-start | bytes 292
  0.0 10.6 %copy-start.1 = (f32[2,4,800]{2,1,0:T(4,128)S(1)}, f32[2,4,800]{2,1,0:T(4,128)}, u32[]{:S(2)}) copy-start(f32[2,4,800]{2,1,0:T(4,128)} %cw_ref.7) | copy-start | bytes 76804
  0.0 10.8 %copy-start.4 = (bf16[2,384,44]{1,0,2:T(2,128)(2,1)S(1)}, bf16[2,384,44]{1,0,2:T(2,128)(2,1)}, u32[]{:S(2)}) copy-start(bf16[2,384,44]{1,0,2:T(2,128)(2,1)} %param.14) | copy-start | bytes 202756
  0.0 21.4 %copy-start.3 = (f32[2,384]{1,0:T(2,128)S(1)}, f32[2,384]{1,0:T(2,128)}, u32[]{:S(2)}) copy-start(f32[2,384]{1,0:T(2,128)} %gain_ref.10) | copy-start | bytes 9220
  1.9 19.6 %all-to-all-start = ((bf16[32,56,128]{2,1,0:T(8,128)(2,1)}), bf16[32,56,128]{2,1,0:T(8,128)(2,1)S(1)}, u32[]{:S(2)}, u32[]{:S(2)}) async-start(bf16[32,56,128]{2,1,0:T(8,128)(2,1)} %shard_map.109), calls=%async_computation | async-start | bytes 917504 | tf_op jit(solution)/shard_map/all_to_all | solution.py:453
  25.9 3.7 %copy-start.7 = (f32[2,12]{1,0:T(2,128)S(1)}, f32[2,12]{1,0:T(2,128)}, u32[]{:S(2)}) copy-start(f32[2,12]{1,0:T(2,128)} %param.19) | copy-start | bytes 292
  25.9 18.5 %all-to-all-start.1 = ((bf16[32,104,128]{2,1,0:T(8,128)(2,1)}), bf16[32,104,128]{2,1,0:T(8,128)(2,1)S(1)}, u32[]{:S(2)}, u32[]{:S(2)}) async-start(bf16[32,104,128]{2,1,0:T(8,128)(2,1)} %get-tuple-element.19), calls=%async_computation.1 | async-start | bytes 1703936 | tf_op jit(solution)/shard_map/all_to_all | solution.py:453
  29.6 14.7 %copy-start = (f32[2,768]{1,0:T(2,128)S(1)}, f32[2,768]{1,0:T(2,128)}, u32[]{:S(2)}) copy-start(f32[2,768]{1,0:T(2,128)} %gain_ref.11) | copy-start | bytes 18436
  67.8 18.5 %all-to-all-start.3 = ((bf16[32,104,128]{2,1,0:T(8,128)(2,1)}), bf16[32,104,128]{2,1,0:T(8,128)(2,1)S(1)}, u32[]{:S(2)}, u32[]{:S(2)}) async-start(bf16[32,104,128]{2,1,0:T(8,128)(2,1)} %get-tuple-element.26), calls=%async_computation.3 | async-start | bytes 1703936 | tf_op jit(solution)/shard_map/all_to_all | solution.py:453

commit v7 on v6

--- a/solution.py
+++ b/solution.py
@@ -115,11 +115,11 @@
     for first in range(0, INNER, 128):
         lanes = slice(first, first + 128)
         taps = 0.5 * cw_ref[layer, :, lanes]
-        total = 0.5 * cb_ref[layer : layer + 1, lanes] + taps[0:1] * conv_ref[
-            5 : 5 + TOKENS, lanes
-        ]
-        for tap in range(1, 4):
-            total = total + taps[tap : tap + 1] * conv_ref[5 + tap : 5 + tap + TOKENS, lanes]
+        bias = 0.5 * cb_ref[layer : layer + 1, lanes]
+        rows = conv_ref[:, lanes]
+        total = bias + taps[3:4] * rows[8:]
+        for back in range(1, 4):
+            total = total + taps[3 - back : 4 - back] * pltpu.roll(rows, back, 0)[8:]
         xc_ref[:, lanes] = (total + total * jnp.tanh(total)).astype(BF)
 
 

time: 91 us -> 90.9 us (level)
  transfers between devices with their start and end apart: 3 -> 3, of which waited for: 3 -> 3; matrix products, arithmetic and copies ran while one was open for 0% -> 0% of each run, Pallas kernels for 14% -> 13%
where the time goes in v7:
time: 90.9 us; the launch traced here: 90.3 us
  Pallas kernels  30.3 us (33%)
  waiting for transfers between devices  28 us (31%)
  starting transfers between devices  16 us (18%)
  blocking collectives  15.3 us (17%)
    pallas_call x7, Pallas kernels, call(): pl.pallas_call(body, grid=grid, out_shape=tuple(outs), in_specs=in_specs,...  30.3 us
    all_to_all x3, waiting for transfers between devices, exchange(): return lax.all_to_all(chunks, 'seq', 0, 0, tiled=True)  28 us
    all_to_all x3, starting transfers between devices, exchange(): return lax.all_to_all(chunks, 'seq', 0, 0, tiled=True)  16 us
    all_to_all x1, blocking collectives, exchange(): return lax.all_to_all(chunks, 'seq', 0, 0, tiled=True)  15.3 us
  transfers between devices with their start and end apart: 3, of which 3 were waited for; matrix products, arithmetic and copies ran while one was open for 0% of the time, Pallas kernels for 13%

profile of v7, /device:TPU:1, one launch (start us, length us, event | category | flops | bytes accessed | tf_op | source)
XLA Modules:
  0.0 90.3 jit_solution(11814355064364185051)
XLA Ops:
  0.0 0.0 copy-start.6
  0.0 0.0 copy-start.1
  0.0 0.0 copy-start.4
  0.0 1.9 %shard_map.109 = bf16[32,56,128]{2,1,0:T(8,128)(2,1)} custom-call(bf16[2,256,384]{2,1,0:T(8,128)(2,1)} %tiles_hbm.1), custom_call_target="tpu_custom_call" | custom-call | flops 1000000 | bytes 851968 | tf_op jit(solution)/shard_map/pallas_call | solution.py:436
  1.9 8.6 %all-to-all-start = ((bf16[32,56,128]{2,1,0:T(8,128)(2,1)}), bf16[32,56,128]{2,1,0:T(8,128)(2,1)S(1)}, u32[]{:S(2)}, u32[]{:S(2)}) async-start(bf16[32,56,128]{2,1,0:T(8,128)(2,1)} %shard_map.109), calls=%async_computation | async-start | bytes 917504 | tf_op jit(solution)/shard_map/all_to_all | solution.py:453
  10.6 0.0 copy-done.1
  10.6 0.1 pad_maximum_fusion
  10.7 0.1 copy.21.col_ref
  10.8 10.7 %all-to-all-done.recv_ref = bf16[32,56,128]{2,1,0:T(8,128)(2,1)S(1)} async-done(((bf16[32,56,128]{2,1,0:T(8,128)(2,1)}), bf16[32,56,128]{2,1,0:T(8,128)(2,1)S(1)}, u32[]{:S(2)}, u32[]{:S(2)}) %all-to-all-start) | async-done | bytes 458784 | tf_op jit(solution)/shard_map/all_to_all | solution.py:453
  21.5 0.0 copy-done.3
  21.5 4.3 %shard_map.110 = (bf16[528,384]{1,0:T(8,128)(2,1)}, f32[64,512]{1,0:T(8,128)}, f32[24,768]{1,0:T(8,128)}, bf16[32,104,128]{2,1,0:T(8,128)(2,1)}) custom-call(bf16[32,56,128]{2,1,0:T(8,128)(2,1)S(1)} %all-to-all-done.recv_ref, f32[2,384]{1,0:T(2,128)S(1)} %copy-done.3, bf16[2,384,1536]{2,1,0:T(8,128)(2,1)} %w_ref.3, bf16[2,48,384]{2,1,0:T(8,128)(2,1)S(1)} %pad.12.ws_ref, ...), custom_call_target="tpu_custom_call" | custom-call | flops 1000000000 | bytes 4392192 | tf_op jit(solution)/shard_map/pallas_call | solution.py:436
  25.8 0.0 copy-start.7
  25.8 3.7 %all-to-all-start.1 = ((bf16[32,104,128]{2,1,0:T(8,128)(2,1)}), bf16[32,104,128]{2,1,0:T(8,128)(2,1)S(1)}, u32[]{:S(2)}, u32[]{:S(2)}) async-start(bf16[32,104,128]{2,1,0:T(8,128)(2,1)} %get-tuple-element.19), calls=%async_computation.1 | async-start | bytes 1703936 | tf_op jit(solution)/shard_map/all_to_all | solution.py:453
  29.5 0.0 copy-done.7
  29.6 0.0 copy-start
  29.6 6.0 %shard_map.111 = (bf16[512,768]{1,0:T(8,128)(2,1)}, f32[512,768]{1,0:T(8,128)}, bf16[512,192]{1,0:T(8,128)(2,1)}) custom-call(bf16[528,384]{1,0:T(8,128)(2,1)} %get-tuple-element.21.xs_ref.xs_hbm, f32[2,384]{1,0:T(2,128)S(1)} %copy-done.3, bf16[2,384,1536]{2,1,0:T(8,128)(2,1)} %w_ref.3, f32[2,4,800]{2,1,0:T(4,128)S(1)} %copy-done.1, f32[2,800]{1,0:T(2,128)S(1)} %copy-done.2, ...), custom_call_target="tpu_custom_call" | custom-call | flops 1000000000 | bytes 5486976 | tf_op jit(solution)/shard_map/pallas_call | solution.py:436
  35.6 8.7 %all-to-all-done.1.recv_ref = bf16[32,104,128]{2,1,0:T(8,128)(2,1)S(1)} async-done(((bf16[32,104,128]{2,1,0:T(8,128)(2,1)}), bf16[32,104,128]{2,1,0:T(8,128)(2,1)S(1)}, u32[]{:S(2)}, u32[]{:S(2)}) %all-to-all-start.1) | async-done | bytes 852000 | tf_op jit(solution)/shard_map/all_to_all | solution.py:453
  44.3 3.8 %shard_map.112 = bf16[32,64,128]{2,1,0:T(8,128)(2,1)S(1)} custom-call(s32[1]{0:T(128)} %bitcast.place_ref, bf16[32,104,128]{2,1,0:T(8,128)(2,1)S(1)} %all-to-all-done.1.recv_ref, f32[24,768]{1,0:T(8,128)} %get-tuple-element.20.loc_hbm, bf16[512,192]{1,0:T(8,128)(2,1)} %get-tuple-element.23.ct_hbm, f32[512,768]{1,0:T(8,128)} %get-tuple-element.24.y_hbm, ...), custom_call_target="tpu_custom_call" | custom-call | flops 1000000000 | bytes 5597188 | tf_op jit(solution)/shard_map/pallas_call | solution.py:436
  48.1 15.3 %all_to_all.20.recv_ref = bf16[32,64,128]{2,1,0:T(8,128)(2,1)S(1)} all-to-all(bf16[32,64,128]{2,1,0:T(8,128)(2,1)S(1)} %shard_map.112), channel_id=1, replica_groups=mesh['dp'=8,'seq'=32] {'seq'}, dimensions={0} | all-to-all | bytes 1048576 | tf_op jit(solution)/shard_map/all_to_all | solution.py:453
  63.4 4.3 %shard_map.113 = (bf16[528,384]{1,0:T(8,128)(2,1)}, f32[64,512]{1,0:T(8,128)}, f32[24,768]{1,0:T(8,128)}, bf16[32,104,128]{2,1,0:T(8,128)(2,1)}) custom-call(bf16[32,64,128]{2,1,0:T(8,128)(2,1)S(1)} %all_to_all.20.recv_ref, f32[2,384]{1,0:T(2,128)S(1)} %copy-done.3, bf16[2,384,1536]{2,1,0:T(8,128)(2,1)} %w_ref.3, bf16[2,48,384]{2,1,0:T(8,128)(2,1)S(1)} %pad.12.ws_ref, ...), custom_call_target="tpu_custom_call" | custom-call | flops 1000000000 | bytes 4457728 | tf_op jit(solution)/shard_map/pallas_call | solution.py:436
  67.7 3.7 %all-to-all-start.3 = ((bf16[32,104,128]{2,1,0:T(8,128)(2,1)}), bf16[32,104,128]{2,1,0:T(8,128)(2,1)S(1)}, u32[]{:S(2)}, u32[]{:S(2)}) async-start(bf16[32,104,128]{2,1,0:T(8,128)(2,1)} %get-tuple-element.26), calls=%async_computation.3 | async-start | bytes 1703936 | tf_op jit(solution)/shard_map/all_to_all | solution.py:453
  71.4 6.1 %shard_map.114 = (bf16[512,768]{1,0:T(8,128)(2,1)}, f32[512,768]{1,0:T(8,128)}, bf16[512,192]{1,0:T(8,128)(2,1)}) custom-call(bf16[528,384]{1,0:T(8,128)(2,1)} %get-tuple-element.28.xs_ref.xs_hbm, f32[2,384]{1,0:T(2,128)S(1)} %copy-done.3, bf16[2,384,1536]{2,1,0:T(8,128)(2,1)} %w_ref.3, f32[2,4,800]{2,1,0:T(4,128)S(1)} %copy-done.1, f32[2,800]{1,0:T(2,128)S(1)} %copy-done.2, ...), custom_call_target="tpu_custom_call" | custom-call | flops 1000000000 | bytes 5486976 | tf_op jit(solution)/shard_map/pallas_call | solution.py:436
  77.5 8.7 %all-to-all-done.3.recv_ref = bf16[32,104,128]{2,1,0:T(8,128)(2,1)S(1)} async-done(((bf16[32,104,128]{2,1,0:T(8,128)(2,1)}), bf16[32,104,128]{2,1,0:T(8,128)(2,1)S(1)}, u32[]{:S(2)}, u32[]{:S(2)}) %all-to-all-start.3) | async-done | bytes 852000 | tf_op jit(solution)/shard_map/all_to_all | solution.py:453
  86.2 3.9 %shard_map.115 = bf16[512,384]{1,0:T(8,128)(2,1)} custom-call(s32[1]{0:T(128)} %bitcast.place_ref, bf16[32,104,128]{2,1,0:T(8,128)(2,1)S(1)} %all-to-all-done.3.recv_ref, f32[24,768]{1,0:T(8,128)} %get-tuple-element.27.loc_hbm, bf16[512,192]{1,0:T(8,128)(2,1)} %get-tuple-element.30.ct_hbm, f32[512,768]{1,0:T(8,128)} %get-tuple-element.31.y_hbm, ...), custom_call_target="tpu_custom_call" | custom-call | flops 1000000000 | bytes 5466116 | tf_op jit(solution)/shard_map/pallas_call | solution.py:436
  (17 shorter events, 0.1 us)
Async XLA Ops:
  0.0 10.6 %slice-start = ((f32[2,800]{1,0:T(2,128)}), f32[2,32]{1,0:T(2,128)S(1)}, s32[]{:S(2)}) async-start(f32[2,800]{1,0:T(2,128)} %cb_ref.7), calls=%async_computation.4 | async-start | bytes 2048 | tf_op jit(solution)/shard_map/slice | solution.py:558
  0.0 21.5 %copy-start.2 = (f32[2,800]{1,0:T(2,128)S(1)}, f32[2,800]{1,0:T(2,128)}, u32[]{:S(2)}) copy-start(f32[2,800]{1,0:T(2,128)} %cb_ref.7) | copy-start | bytes 19204
  0.0 10.5 %copy-start.5 = (f32[2,12]{1,0:T(2,128)S(1)}, f32[2,12]{1,0:T(2,128)}, u32[]{:S(2)}) copy-start(f32[2,12]{1,0:T(2,128)} %param.18) | copy-start | bytes 292
  0.0 10.5 %copy-start.6 = (f32[2,12]{1,0:T(2,128)S(1)}, f32[2,12]{1,0:T(2,128)}, u32[]{:S(2)}) copy-start(f32[2,12]{1,0:T(2,128)} %param.17) | copy-start | bytes 292
  0.0 10.6 %copy-start.1 = (f32[2,4,800]{2,1,0:T(4,128)S(1)}, f32[2,4,800]{2,1,0:T(4,128)}, u32[]{:S(2)}) copy-start(f32[2,4,800]{2,1,0:T(4,128)} %cw_ref.7) | copy-start | bytes 76804
  0.0 10.8 %copy-start.4 = (bf16[2,384,44]{1,0,2:T(2,128)(2,1)S(1)}, bf16[2,384,44]{1,0,2:T(2,128)(2,1)}, u32[]{:S(2)}) copy-start(bf16[2,384,44]{1,0,2:T(2,128)(2,1)} %param.14) | copy-start | bytes 202756
  0.0 21.4 %copy-start.3 = (f32[2,384]{1,0:T(2,128)S(1)}, f32[2,384]{1,0:T(2,128)}, u32[]{:S(2)}) copy-start(f32[2,384]{1,0:T(2,128)} %gain_ref.10) | copy-start | bytes 9220
  1.9 19.6 %all-to-all-start = ((bf16[32,56,128]{2,1,0:T(8,128)(2,1)}), bf16[32,56,128]{2,1,0:T(8,128)(2,1)S(1)}, u32[]{:S(2)}, u32[]{:S(2)}) async-start(bf16[32,56,128]{2,1,0:T(8,128)(2,1)} %shard_map.109), calls=%async_computation | async-start | bytes 917504 | tf_op jit(solution)/shard_map/all_to_all | solution.py:453
  25.8 3.7 %copy-start.7 = (f32[2,12]{1,0:T(2,128)S(1)}, f32[2,12]{1,0:T(2,128)}, u32[]{:S(2)}) copy-start(f32[2,12]{1,0:T(2,128)} %param.19) | copy-start | bytes 292
  25.8 18.5 %all-to-all-start.1 = ((bf16[32,104,128]{2,1,0:T(8,128)(2,1)}), bf16[32,104,128]{2,1,0:T(8,128)(2,1)S(1)}, u32[]{:S(2)}, u32[]{:S(2)}) async-start(bf16[32,104,128]{2,1,0:T(8,128)(2,1)} %get-tuple-element.19), calls=%async_computation.1 | async-start | bytes 1703936 | tf_op jit(solution)/shard_map/all_to_all | solution.py:453
  29.6 14.7 %copy-start = (f32[2,768]{1,0:T(2,128)S(1)}, f32[2,768]{1,0:T(2,128)}, u32[]{:S(2)}) copy-start(f32[2,768]{1,0:T(2,128)} %gain_ref.11) | copy-start | bytes 18436
  67.7 18.5 %all-to-all-start.3 = ((bf16[32,104,128]{2,1,0:T(8,128)(2,1)}), bf16[32,104,128]{2,1,0:T(8,128)(2,1)S(1)}, u32[]{:S(2)}, u32[]{:S(2)}) async-start(bf16[32,104,128]{2,1,0:T(8,128)(2,1)} %get-tuple-element.26), calls=%async_computation.3 | async-start | bytes 1703936 | tf_op jit(solution)/shard_map/all_to_all | solution.py:453
